TPU v7x, 128 devices: a whole 4x4x4 slice. The times are simulated.
128 devices in a mesh: section: 2 (over z_hi), ctx: 8 (over y, core), fsdp: 8 (over z_lo, x).
Axes of the slice: x: 4, y: 4, z: 4 (z_hi: 2, z_lo: 2; z = z_hi * 2 + z_lo), core: 2. Of those that a mesh axis runs over, the one named last changes fastest.
Arguments:
- block_input: bfloat16 [2, 8, 1024, 576], P(None, 'fsdp', 'ctx'), may hold values from -6 to 6
- cotangent: bfloat16 [2, 8, 1024, 576], P(None, 'fsdp', 'ctx'), may hold values from -6 to 6
- segment_ids: int32 [2, 8, 1024], P(None, 'fsdp'), may hold values from 0 to 2, as said below
- attn_gain: bfloat16 [2, 576], P('section', ('ctx', 'fsdp')), may hold values from 0.25 to 1.75
- w_query: bfloat16 [2, 576, 576], P('section', ('ctx', 'fsdp')), may hold values from -0.25 to 0.25
- w_key: bfloat16 [2, 576, 192], P('section', ('ctx', 'fsdp')), may hold values from -0.25 to 0.25
- w_value: bfloat16 [2, 576, 192], P('section', ('ctx', 'fsdp')), may hold values from -0.25 to 0.25
- w_out: bfloat16 [2, 576, 576], P('section', ('ctx', 'fsdp')), may hold values from -1 to 1
- w_gate: bfloat16 [2, 576, 1536], P('section', ('ctx', 'fsdp')), may hold values from -0.25 to 0.25
- w_up: bfloat16 [2, 576, 1536], P('section', ('ctx', 'fsdp')), may hold values from -0.25 to 0.25
- w_down: bfloat16 [2, 1536, 576], P('section', ('ctx', 'fsdp')), may hold values from -0.15625 to 0.15625
- mlp_gain: bfloat16 [2, 576], P('section', ('ctx', 'fsdp')), may hold values from 0.25 to 1.75
Outputs:
- edges: float32 [2, 2, 8, 1024, 576], P('section', None, 'fsdp', 'ctx')
- grad_attn_gain: float32 [2, 576], P('section', ('ctx', 'fsdp'))
- grad_w_query: float32 [2, 576, 576], P('section', ('ctx', 'fsdp'))
- grad_w_key: float32 [2, 576, 192], P('section', ('ctx', 'fsdp'))
- grad_w_value: float32 [2, 576, 192], P('section', ('ctx', 'fsdp'))
- grad_w_out: float32 [2, 576, 576], P('section', ('ctx', 'fsdp'))
- grad_w_gate: float32 [2, 576, 1536], P('section', ('ctx', 'fsdp'))
- grad_w_up: float32 [2, 576, 1536], P('section', ('ctx', 'fsdp'))
- grad_w_down: float32 [2, 1536, 576], P('section', ('ctx', 'fsdp'))
- grad_mlp_gain: float32 [2, 576], P('section', ('ctx', 'fsdp'))
Inputs may be any that keep to these rules, and one draw needn't show every extreme that they name: `segment_ids`: each sequence holds three documents numbered 0, 1, 2 in order; document 0 ends within the first 128 positions and document 2 begins within the last 128.
All inputs are finite; a program needn't handle non-finite values.
Results may differ from a plain program's by a relative error of at most 0.025.
Values may be sent and summed in bfloat16 or wider, within the bound.
A program may use at most 128 MiB of HBM per device.

v0:
```python
import jax
import jax.numpy as jnp
from jax import lax
from jax.sharding import PartitionSpec as P

HEADS = 9
KV_HEADS = 3
HEAD_DIM = 64
GROUP = 3


norm_eps = 1e-05
rope_base = 100000.0
masked_score = -1e30


def passed_along(block, axis, distance):
    devices = range(lax.axis_size(axis))
    route = [(i - distance, i) for i in devices if i - distance in devices]
    return lax.ppermute(block, axis, route)


def product(left, right):
    return jnp.dot(left, right, preferred_element_type=jnp.float32)


def product_back(left, right):
    return lax.dot_general(
        left, right, (((1,), (1,)), ((), ())), preferred_element_type=jnp.float32
    )


def row_contract(left, right):
    return lax.dot_general(
        left, right, (((0,), (0,)), ((), ())), preferred_element_type=jnp.float32
    )


def rope_tables(places):
    pair_index = jnp.arange(HEAD_DIM // 2).astype(jnp.float32)
    frequency = rope_base ** (-2.0 * pair_index / HEAD_DIM)
    angles = places.astype(jnp.float32)[:, None] * frequency[None, :]
    return (jnp.cos(angles), jnp.sin(angles))


def rotate(vectors, cos_table, sin_table):
    half_dim = vectors.shape[-1] // 2
    lower_half = vectors[..., :half_dim]
    upper_half = vectors[..., half_dim:]
    cos_part = cos_table[:, None, :]
    sin_part = sin_table[:, None, :]
    return jnp.concatenate(
        [
            lower_half * cos_part - upper_half * sin_part,
            upper_half * cos_part + lower_half * sin_part,
        ],
        axis=-1,
    )


def rotate_back(grads, cos_table, sin_table):
    half_dim = grads.shape[-1] // 2
    lower_half = grads[..., :half_dim]
    upper_half = grads[..., half_dim:]
    cos_part = cos_table[:, None, :]
    sin_part = sin_table[:, None, :]
    return jnp.concatenate(
        [
            lower_half * cos_part + upper_half * sin_part,
            upper_half * cos_part - lower_half * sin_part,
        ],
        axis=-1,
    )


def norm_backward(scaled_grad, values_in, scale_rows):
    return scale_rows * scaled_grad - values_in * scale_rows**3 * jnp.mean(
        scaled_grad * values_in, axis=-1, keepdims=True
    )


def local_places(ctx_index, row_count):
    return ctx_index * row_count + jnp.arange(row_count, dtype=jnp.int32)


def masked_scores(grouped, all_keys, seg_row, places):
    seq_len = all_keys.shape[0]
    key_heads = all_keys.reshape(seq_len, KV_HEADS, HEAD_DIM)
    raw_scores = jnp.einsum(
        "qgrd,kgd->grqk", grouped, key_heads, preferred_element_type=jnp.float32
    ) * HEAD_DIM ** (-0.5)
    own_seg = lax.dynamic_slice_in_dim(seg_row, places[0], places.shape[0], 0)
    key_places = jnp.arange(seq_len, dtype=jnp.int32)
    allowed = (key_places[None, :] <= places[:, None]) & (seg_row[None, :] == own_seg[:, None])
    return jnp.where(allowed, raw_scores, masked_score)


def forward_layer(current, seg_row, ctx_index, params):
    attn_gain, w_query, w_key, w_value, w_out, w_gate, w_up, w_down, mlp_gain = params
    row_count = current.shape[0]
    places = local_places(ctx_index, row_count)
    cos_table, sin_table = rope_tables(places)
    scale_one = lax.rsqrt(jnp.mean(current * current, axis=-1, keepdims=True) + norm_eps)
    normed = (current * scale_one * attn_gain).astype(jnp.bfloat16)
    queries = rotate(
        product(normed, w_query).reshape(row_count, HEADS, HEAD_DIM), cos_table, sin_table
    )
    grouped = queries.astype(jnp.bfloat16).reshape(row_count, KV_HEADS, GROUP, HEAD_DIM)
    key_rows = rotate(
        product(normed, w_key).reshape(row_count, KV_HEADS, HEAD_DIM), cos_table, sin_table
    )
    key_rows = key_rows.astype(jnp.bfloat16).reshape(row_count, KV_HEADS * HEAD_DIM)
    values = product(normed, w_value).astype(jnp.bfloat16)
    all_keys, all_values = (
        lax.all_gather(key_rows, "ctx", axis=0, tiled=True),
        lax.all_gather(values, "ctx", axis=0, tiled=True),
    )
    scores = masked_scores(grouped, all_keys, seg_row, places)
    row_max = jnp.max(scores, axis=-1, keepdims=True)
    log_total = row_max + jnp.log(jnp.sum(jnp.exp(scores - row_max), axis=-1, keepdims=True))
    prob_rows = jnp.exp(scores - log_total).astype(jnp.bfloat16)
    value_heads = all_values.reshape(all_values.shape[0], KV_HEADS, HEAD_DIM)
    mixture = jnp.einsum(
        "grqk,kgd->qgrd", prob_rows, value_heads, preferred_element_type=jnp.float32
    )
    attended = mixture.reshape(row_count, HEADS * HEAD_DIM).astype(jnp.bfloat16)
    midway = current + product(attended, w_out)
    scale_two = lax.rsqrt(jnp.mean(midway * midway, axis=-1, keepdims=True) + norm_eps)
    normed_two = (midway * scale_two * mlp_gain).astype(jnp.bfloat16)
    gate_act = product(normed_two, w_gate)
    up_act = product(normed_two, w_up)
    hidden = (jax.nn.silu(gate_act) * up_act).astype(jnp.bfloat16)
    result = midway + product(hidden, w_down)
    kept = (
        current,
        scale_one,
        normed,
        grouped,
        all_keys,
        all_values,
        log_total,
        attended,
        midway,
        scale_two,
        normed_two,
        gate_act,
        up_act,
        hidden,
    )
    return (result, kept)


def backward_layer(incoming, kept_state, ctx_index, params):
    attn_gain, w_query, w_key, w_value, w_out, w_gate, w_up, w_down, mlp_gain = params
    (
        seg_row,
        current,
        scale_one,
        normed,
        grouped,
        all_keys,
        all_values,
        log_total,
        attended,
        midway,
        scale_two,
        normed_two,
        gate_act,
        up_act,
        hidden,
    ) = kept_state
    row_count = current.shape[0]
    seq_len = all_keys.shape[0]
    places = local_places(ctx_index, row_count)
    cos_table, sin_table = rope_tables(places)
    down_grad = incoming.astype(jnp.bfloat16)
    hidden_grad = product_back(down_grad, w_down)
    sigmoid_gate = jax.nn.sigmoid(gate_act)
    gate_grad = (
        hidden_grad * up_act * sigmoid_gate * (1.0 + gate_act * (1.0 - sigmoid_gate))
    ).astype(jnp.bfloat16)
    up_grad = (hidden_grad * gate_act * sigmoid_gate).astype(jnp.bfloat16)
    normed_two_grad = product_back(gate_grad, w_gate) + product_back(up_grad, w_up)
    mlp_gain_grad = jnp.sum(normed_two_grad * midway * scale_two, axis=0)
    midway_grad = incoming + norm_backward(normed_two_grad * mlp_gain, midway, scale_two)
    out_grad = midway_grad.astype(jnp.bfloat16)
    mixed_grad = (
        product_back(out_grad, w_out)
        .astype(jnp.bfloat16)
        .reshape(row_count, KV_HEADS, GROUP, HEAD_DIM)
    )
    scores = masked_scores(grouped, all_keys, seg_row, places)
    prob_rows = jnp.exp(scores - log_total)
    key_heads = all_keys.reshape(seq_len, KV_HEADS, HEAD_DIM)
    value_heads = all_values.reshape(seq_len, KV_HEADS, HEAD_DIM)
    prob_grad = jnp.einsum(
        "qgrd,kgd->grqk", mixed_grad, value_heads, preferred_element_type=jnp.float32
    )
    row_delta = jnp.sum(prob_rows * prob_grad, axis=-1, keepdims=True)
    score_grad = (prob_rows * (prob_grad - row_delta)).astype(jnp.bfloat16)
    query_grad = jnp.einsum(
        "grqk,kgd->qgrd", score_grad, key_heads, preferred_element_type=jnp.float32
    ) * HEAD_DIM ** (-0.5)
    key_part = jnp.einsum(
        "grqk,qgrd->kgd", score_grad, grouped, preferred_element_type=jnp.float32
    ) * HEAD_DIM ** (-0.5)
    value_part = jnp.einsum(
        "grqk,qgrd->kgd",
        prob_rows.astype(jnp.bfloat16),
        mixed_grad,
        preferred_element_type=jnp.float32,
    )
    key_grad, value_grad = (
        lax.psum_scatter(
            key_part.reshape(seq_len, KV_HEADS * HEAD_DIM), "ctx", scatter_dimension=0, tiled=True
        ),
        lax.psum_scatter(
            value_part.reshape(seq_len, KV_HEADS * HEAD_DIM), "ctx", scatter_dimension=0, tiled=True
        ),
    )
    qpre_grad = rotate_back(query_grad.reshape(row_count, HEADS, HEAD_DIM), cos_table, sin_table)
    qpre_grad = qpre_grad.reshape(row_count, HEADS * HEAD_DIM).astype(jnp.bfloat16)
    kpre_grad = rotate_back(key_grad.reshape(row_count, KV_HEADS, HEAD_DIM), cos_table, sin_table)
    kpre_grad = kpre_grad.reshape(row_count, KV_HEADS * HEAD_DIM).astype(jnp.bfloat16)
    vpre_grad = value_grad.astype(jnp.bfloat16)
    normed_grad = (
        product_back(qpre_grad, w_query)
        + product_back(kpre_grad, w_key)
        + product_back(vpre_grad, w_value)
    )
    attn_gain_grad = jnp.sum(normed_grad * current * scale_one, axis=0)
    grad_in = midway_grad + norm_backward(normed_grad * attn_gain, current, scale_one)
    record = (
        normed,
        qpre_grad,
        kpre_grad,
        vpre_grad,
        attended,
        out_grad,
        normed_two,
        gate_grad,
        up_grad,
        hidden,
        down_grad,
    )
    return (grad_in, record, (attn_gain_grad, mlp_gain_grad))


def grad_terms(first_gain, record, second_gain):
    (
        normed,
        qpre_grad,
        kpre_grad,
        vpre_grad,
        attended,
        out_grad,
        normed_two,
        gate_grad,
        up_grad,
        hidden,
        down_grad,
    ) = record
    return (
        first_gain[None],
        row_contract(normed, qpre_grad)[None],
        row_contract(normed, kpre_grad)[None],
        row_contract(normed, vpre_grad)[None],
        row_contract(attended, out_grad)[None],
        row_contract(normed_two, gate_grad)[None],
        row_contract(normed_two, up_grad)[None],
        row_contract(hidden, down_grad)[None],
        second_gain[None],
    )


def local(
    block_input,
    cotangent,
    segment_ids,
    attn_gain,
    w_query,
    w_key,
    w_value,
    w_out,
    w_gate,
    w_up,
    w_down,
    mlp_gain,
):
    gathered = (
        lax.all_gather(attn_gain, ("ctx", "fsdp"), axis=1, tiled=True),
        lax.all_gather(w_query, ("ctx", "fsdp"), axis=1, tiled=True),
        lax.all_gather(w_key, ("ctx", "fsdp"), axis=1, tiled=True),
        lax.all_gather(w_value, ("ctx", "fsdp"), axis=1, tiled=True),
        lax.all_gather(w_out, ("ctx", "fsdp"), axis=1, tiled=True),
        lax.all_gather(w_gate, ("ctx", "fsdp"), axis=1, tiled=True),
        lax.all_gather(w_up, ("ctx", "fsdp"), axis=1, tiled=True),
        lax.all_gather(w_down, ("ctx", "fsdp"), axis=1, tiled=True),
        lax.all_gather(mlp_gain, ("ctx", "fsdp"), axis=1, tiled=True),
    )
    params = tuple((gathered_piece[0] for gathered_piece in gathered))
    section_index = lax.axis_index("section")
    ctx_index = lax.axis_index("ctx")
    micro_count = block_input.shape[0]
    row_count = block_input.shape[2]
    feature_count = block_input.shape[3]
    saved = []
    outputs = []
    arrived = jnp.zeros((row_count, feature_count), jnp.bfloat16)
    for step_index in range(micro_count + 1):
        own_input = block_input[min(step_index, micro_count - 1), 0]
        current = jnp.where(section_index == 0, own_input, arrived).astype(jnp.float32)
        seg_row = jnp.where(
            section_index == 0,
            segment_ids[min(step_index, micro_count - 1), 0],
            segment_ids[max(step_index - 1, 0), 0],
        )
        result, kept = forward_layer(current, seg_row, ctx_index, params)
        saved.append((seg_row,) + kept)
        outputs.append(result)
        if step_index < micro_count:
            arrived = passed_along(result.astype(jnp.bfloat16), "section", 1)
    regathered = (
        lax.all_gather(attn_gain, ("ctx", "fsdp"), axis=1, tiled=True),
        lax.all_gather(w_query, ("ctx", "fsdp"), axis=1, tiled=True),
        lax.all_gather(w_key, ("ctx", "fsdp"), axis=1, tiled=True),
        lax.all_gather(w_value, ("ctx", "fsdp"), axis=1, tiled=True),
        lax.all_gather(w_out, ("ctx", "fsdp"), axis=1, tiled=True),
        lax.all_gather(w_gate, ("ctx", "fsdp"), axis=1, tiled=True),
        lax.all_gather(w_up, ("ctx", "fsdp"), axis=1, tiled=True),
        lax.all_gather(w_down, ("ctx", "fsdp"), axis=1, tiled=True),
        lax.all_gather(mlp_gain, ("ctx", "fsdp"), axis=1, tiled=True),
    )
    params = tuple((gathered_piece[0] for gathered_piece in regathered))
    returned = jnp.zeros((row_count, feature_count), jnp.bfloat16)
    gain_totals = (
        jnp.zeros((feature_count,), jnp.float32),
        jnp.zeros((feature_count,), jnp.float32),
    )
    records = []
    input_grads = []
    for step_index in range(micro_count + 1):
        if step_index < micro_count:
            late_grad = cotangent[step_index, 0]
        else:
            late_grad = jnp.zeros((row_count, feature_count), jnp.bfloat16)
        incoming = jnp.where(section_index == 1, late_grad, returned).astype(jnp.float32)
        kept_state = jax.tree.map(
            lambda later, earlier: jnp.where(section_index == 1, later, earlier),
            saved[min(step_index + 1, micro_count)],
            saved[max(step_index - 1, 0)],
        )
        grad_in, record, gain_grads = backward_layer(incoming, kept_state, ctx_index, params)
        gain_totals = (gain_totals[0] + gain_grads[0], gain_totals[1] + gain_grads[1])
        records.append(record)
        if step_index >= 1:
            input_grads.append(grad_in)
        if step_index < micro_count:
            returned = passed_along(grad_in.astype(jnp.bfloat16), "section", -1)
    chosen = [
        jax.tree.map(
            lambda later, earlier: jnp.where(section_index == 1, later, earlier),
            records[batch_index],
            records[batch_index + 1],
        )
        for batch_index in range(micro_count)
    ]
    joined = jax.tree.map(lambda *row_parts: jnp.concatenate(row_parts, axis=0), *chosen)
    grad_shards = lax.psum_scatter(
        grad_terms(gain_totals[0], joined, gain_totals[1]),
        ("ctx", "fsdp"),
        scatter_dimension=1,
        tiled=True,
    )
    layer_outputs = jnp.stack([outputs[batch_index + 1] for batch_index in range(micro_count)])
    first_grads = jnp.stack(input_grads)
    edges = jnp.where(section_index == 0, first_grads, layer_outputs)[None, :, None]
    return (
        edges,
        grad_shards[0],
        grad_shards[1],
        grad_shards[2],
        grad_shards[3],
        grad_shards[4],
        grad_shards[5],
        grad_shards[6],
        grad_shards[7],
        grad_shards[8],
    )


def solution(mesh):
    return jax.shard_map(
        local,
        mesh=mesh,
        in_specs=(
            P(None, "fsdp", "ctx", None),
            P(None, "fsdp", "ctx", None),
            P(None, "fsdp", None),
            P("section", ("ctx", "fsdp")),
            P("section", ("ctx", "fsdp"), None),
            P("section", ("ctx", "fsdp"), None),
            P("section", ("ctx", "fsdp"), None),
            P("section", ("ctx", "fsdp"), None),
            P("section", ("ctx", "fsdp"), None),
            P("section", ("ctx", "fsdp"), None),
            P("section", ("ctx", "fsdp"), None),
            P("section", ("ctx", "fsdp")),
        ),
        out_specs=(
            P("section", None, "fsdp", "ctx", None),
            P("section", ("ctx", "fsdp")),
            P("section", ("ctx", "fsdp"), None),
            P("section", ("ctx", "fsdp"), None),
            P("section", ("ctx", "fsdp"), None),
            P("section", ("ctx", "fsdp"), None),
            P("section", ("ctx", "fsdp"), None),
            P("section", ("ctx", "fsdp"), None),
            P("section", ("ctx", "fsdp"), None),
            P("section", ("ctx", "fsdp")),
        ),
        check_vma=False,
    )
```

profile of v0, /device:TPU:0, one launch (start us, length us, event | category | flops | bytes accessed | tf_op | source)
XLA Modules:
  0.0 1782.4 jit_solution(5166516582812384477)
XLA Ops:
  11.9 145.4 %all_gather.55 = bf16[1,576,192]{2,0,1:T(2,128)(2,1)S(1)} all-gather(bf16[1,9,192]{2,0,1:T(2,128)(2,1)S(1)} %copy.71), channel_id=1, replica_groups=mesh['section'=2,'ctx'=8,'fsdp'=8] {'ctx','fsdp'}, dimensions={1}, use_global_device_ids=true | all-gather | bytes 224640 | tf_op jit(solution)/shard_map/all_gather | solution.py:294
  161.9 138.7 %all-reduce.13 = (bf16[576]{0:T(1024)(128)(2,1)S(1)}, bf16[576]{0:T(1024)(128)(2,1)S(1)}) all-reduce(bf16[576]{0:T(1024)(128)(2,1)S(1)} %dynamic-update-slice, bf16[576]{0:T(1024)(128)(2,1)S(1)} %dynamic-update-slice.1), channel_id=1, replica_groups=mesh['section'=2,'ctx'=8,'fsdp'=8] {'ctx','fsdp'}, use_global_device_ids=true, to_apply=%add | all-reduce | flops 1152 | bytes 4608
  303.3 11.9 all_gather.56
  316.9 141.5 %all_gather.57 = bf16[1,576,192]{2,0,1:T(2,128)(2,1)S(1)} all-gather(bf16[1,9,192]{2,0,1:T(2,128)(2,1)S(1)} %copy.73), channel_id=1, replica_groups=mesh['section'=2,'ctx'=8,'fsdp'=8] {'ctx','fsdp'}, dimensions={1}, use_global_device_ids=true | all-gather | bytes 224640 | tf_op jit(solution)/shard_map/all_gather | solution.py:293
  459.6 145.1 %all_gather.59 = bf16[1,576,576]{2,0,1:T(2,128)(2,1)S(1)} all-gather(bf16[1,9,576]{2,0,1:T(2,128)(2,1)S(1)} %copy.75), channel_id=1, replica_groups=mesh['section'=2,'ctx'=8,'fsdp'=8] {'ctx','fsdp'}, dimensions={1}, use_global_device_ids=true | all-gather | bytes 673920 | tf_op jit(solution)/shard_map/all_gather | solution.py:292
  604.8 155.5 %all_gather.60 = bf16[1,576,576]{2,0,1:T(2,128)(2,1)} all-gather(bf16[1,9,576]{2,0,1:T(2,128)(2,1)S(1)} %copy.78), channel_id=1, replica_groups=mesh['section'=2,'ctx'=8,'fsdp'=8] {'ctx','fsdp'}, dimensions={1}, use_global_device_ids=true | all-gather | bytes 673920 | tf_op jit(solution)/shard_map/all_gather | solution.py:295
  760.9 2.1 copy.138
  765.4 11.8 all_gather.58
  777.8 2.3 fusion.123
  785.0 2.4 copy.136
  787.5 2.5 copy.137
  794.0 2.5 fusion.96
  796.6 6.1 collective-permute-start
  802.6 3.4 collective-permute-done
  811.3 12.3 all_gather.65
  823.6 11.8 all_gather.66
  844.2 5.9 collective-permute-start.2
  850.7 3.0 collective-permute-done.2
  855.6 12.3 all_gather.67
  867.9 12.1 all_gather.68
  897.6 2.4 convolution_multiply_fusion.2
  904.2 2.2 fusion.25
  906.9 2.6 fusion.121
  909.5 2.4 fusion.52
  911.8 2.3 fusion.64
  914.2 3.0 fusion.188
  917.2 11.3 reduce-scatter.9.cloned.1.call-done
  929.9 2.2 convolution_add_fusion.5
  932.0 29.0 %reduce-scatter.11.cloned.1.call-done = f32[128,192]{0,1:T(8,128)} async-done(((f32[1024,192]{0,1:T(8,128)}), f32[128,192]{0,1:T(8,128)}) %reduce-scatter.11.cloned.1.call-update) | async-done | bytes 98320 | tf_op jit(solution)/shard_map/reduce_scatter | solution.py:217
  961.1 2.3 multiply_reduce_fusion.5
  966.7 6.5 collective-permute-done.1
  974.9 5.1 select_select_fusion.1
  989.8 4.5 fusion.23
  994.4 2.4 convolution_multiply_fusion.1
  1000.9 18.0 %reduce-scatter.13.cloned.1.call-done = f32[128,192]{0,1:T(8,128)} async-done(((f32[1024,192]{0,1:T(8,128)}), f32[128,192]{0,1:T(8,128)}) %reduce-scatter.13.cloned.1.call-update) | async-done | bytes 98320 | tf_op jit(solution)/shard_map/reduce_scatter | solution.py:214
  1023.9 27.8 %reduce-scatter.15.cloned.1.call-done = f32[128,192]{0,1:T(8,128)} async-done(((f32[1024,192]{0,1:T(8,128)}), f32[128,192]{0,1:T(8,128)}) %reduce-scatter.15.cloned.1.call-update) | async-done | bytes 98320 | tf_op jit(solution)/shard_map/reduce_scatter | solution.py:217
  1051.7 2.5 multiply_reduce_fusion.4
  1059.6 5.1 collective-permute-done.3
  1078.4 4.6 fusion.21
  1086.4 2.7 copy.92
  1089.5 2.7 copy.95
  1092.8 5.5 copy.96
  1099.0 5.6 copy.97
  1105.3 5.9 copy.98
  1114.5 22.4 %reduce-scatter.19.cloned.1.call-done = f32[128,192]{0,1:T(8,128)} async-done(((f32[1024,192]{0,1:T(8,128)}), f32[128,192]{0,1:T(8,128)}) %reduce-scatter.19.cloned.1.call-update) | async-done | bytes 98320 | tf_op jit(solution)/shard_map/reduce_scatter | solution.py:217
  1142.0 2.5 fusion.93
  1147.3 147.1 %all-reduce.11 = (f32[1,576]{1,0:T(1,128)S(1)}, f32[1,576]{1,0:T(1,128)S(1)}) all-reduce(f32[1,576]{1,0:T(1,128)S(1)} %add.454, f32[1,576]{1,0:T(1,128)S(1)} %add.457), channel_id=8, replica_groups=mesh['section'=2,'ctx'=8,'fsdp'=8] {'ctx','fsdp'}, use_global_device_ids=true, to_apply=%region_30.31.clone | all-reduce | flops 1152 | bytes 9216
  1296.6 468.8 %all-reduce.16.cloned.1.call-done = (f32[1,576,576]{2,0,1:T(1,128)}, f32[1,576,192]{2,0,1:T(1,128)}, f32[1,576,192]{2,0,1:T(1,128)}, f32[1,576,576]{2,0,1:T(1,12...) async-done(((f32[1,576,576]{2,0,1:T(1,128)}, f32[1,576,192]{2,0,1:T(1,128)}, f32[1,576,192]{2,0,1:T(1,128)}, ...) | async-done | bytes 14155792
  (539 shorter events, 135.3 us)
Async XLA Ops:
  7.2 452.1 %copy-start.30 = (bf16[2,1,128,576]{2,3,1,0:T(8,128)(2,1)S(1)}, bf16[2,1,128,576]{2,3,1,0:T(8,128)(2,1)}, u32[]{:S(2)}) copy-start(bf16[2,1,128,576]{2,3,1,0:T(8,128)(2,1)} %param.12) | copy-start | bytes 884740
  7.2 452.4 %copy-start.151 = (bf16[1,9,576]{2,1,0:T(8,128)(2,1)S(1)}, bf16[1,9,576]{2,1,0:T(8,128)(2,1)}, u32[]{:S(2)}) copy-start(bf16[1,9,576]{2,1,0:T(8,128)(2,1)} %param.16) | copy-start | bytes 31108
  7.2 597.6 %copy-start.152 = (bf16[1,9,576]{2,1,0:T(8,128)(2,1)S(1)}, bf16[1,9,576]{2,1,0:T(8,128)(2,1)}, u32[]{:S(2)}) copy-start(bf16[1,9,576]{2,1,0:T(8,128)(2,1)} %param.19) | copy-start | bytes 31108
  7.2 777.8 %all-gather.4.cloned.1.call-start = ((), (), s32[]{:S(2)}) async-start(), calls=%async_computation.6 | async-start | bytes 3594240 | tf_op jit(solution)/shard_map/all_gather | solution.py:296
  8.8 778.7 %all-gather.6.cloned.1.call-start = ((), (), s32[]{:S(2)}) async-start(), calls=%async_computation.7 | async-start | bytes 3594240 | tf_op jit(solution)/shard_map/all_gather | solution.py:297
  10.3 783.7 %all-gather.8.cloned.1.call-start = ((), (), s32[]{:S(2)}) async-start(), calls=%async_computation.8 | async-start | bytes 1996800 | tf_op jit(solution)/shard_map/all_gather | solution.py:298
  11.1 917.4 %reduce-scatter.9.cloned.1.call-start = ((), (), s32[]{:S(2)}) async-start(), calls=%async_computation.9 | async-start | bytes 884736 | tf_op jit(solution)/shard_map/reduce_scatter | solution.py:214
  158.2 158.7 %copy-start.45 = (bf16[1,576,192]{1,2,0:T(8,128)(2,1)}, bf16[1,576,192]{1,2,0:T(8,128)(2,1)S(1)}, u32[]{:S(2)}) copy-start(bf16[1,576,192]{1,2,0:T(8,128)(2,1)S(1)} %copy.72) | copy-start | bytes 663556
  300.5 476.7 %copy-start.104 = (f32[576]{0:T(1024)}, f32[576]{0:T(1024)S(1)}, u32[]{:S(2)}) copy-start(f32[576]{0:T(1024)S(1)} %mul.1116) | copy-start | bytes 6916
  302.1 475.2 %copy-start.165 = (f32[128]{0:T(128)}, f32[128]{0:T(128)S(1)}, u32[]{:S(2)}) copy-start(f32[128]{0:T(128)S(1)} %add_rsqrt_fusion.5) | copy-start | bytes 1540
  315.2 466.8 %copy-start.79 = (bf16[1024,192]{0,1:T(8,128)(2,1)}, bf16[1024,192]{0,1:T(8,128)(2,1)S(1)}, u32[]{:S(2)}) copy-start(bf16[1024,192]{0,1:T(8,128)(2,1)S(1)} %all_gather.56) | copy-start | bytes 1179652
  459.3 301.6 %copy-start.27 = (bf16[1,576,192]{1,2,0:T(8,128)(2,1)}, bf16[1,576,192]{1,2,0:T(8,128)(2,1)S(1)}, u32[]{:S(2)}) copy-start(bf16[1,576,192]{1,2,0:T(8,128)(2,1)S(1)} %copy.74) | copy-start | bytes 663556
  604.8 176.1 %copy-start.36 = (bf16[1,576,576]{2,0,1:T(2,128)(2,1)}, bf16[1,576,576]{2,0,1:T(2,128)(2,1)S(1)}, u32[]{:S(2)}) copy-start(bf16[1,576,576]{2,0,1:T(2,128)(2,1)S(1)} %all_gather.59) | copy-start | bytes 1990660
  760.4 20.5 %copy-start.50 = (f32[128,32]{0,1:T(8,128)}, f32[128,32]{0,1:T(8,128)S(1)}, u32[]{:S(2)}) copy-start(f32[128,32]{0,1:T(8,128)S(1)} %get-tuple-element.168) | copy-start | bytes 49156
  763.0 17.9 %copy-start.25 = (bf16[1,576,576]{1,2,0:T(8,128)(2,1)}, bf16[1,576,576]{1,2,0:T(8,128)(2,1)S(1)}, u32[]{:S(2)}) copy-start(bf16[1,576,576]{1,2,0:T(8,128)(2,1)S(1)} %copy.138) | copy-start | bytes 1990660
  764.8 18.5 %copy-start.3 = (bf16[1,576,576]{2,1,0:T(8,128)(2,1)}, bf16[1,576,576]{2,1,0:T(8,128)(2,1)S(1)}, u32[]{:S(2)}) copy-start(bf16[1,576,576]{2,1,0:T(8,128)(2,1)S(1)} %copy.135) | copy-start | bytes 1990660
  794.0 29.5 %copy-start.51 = (f32[128,32]{0,1:T(8,128)S(1)}, f32[128,32]{0,1:T(8,128)}, u32[]{:S(2)}) copy-start(f32[128,32]{0,1:T(8,128)} %copy-done.50) | copy-start | bytes 49156
  794.0 41.5 %copy-start.94 = (pred[128,1024]{0,1:T(8,128)(4,1)S(1)}, pred[128,1024]{0,1:T(8,128)(4,1)}, u32[]{:S(2)}) copy-start(pred[128,1024]{0,1:T(8,128)(4,1)} %get-tuple-element.180) | copy-start | bytes 393220
  796.6 9.5 collective-permute-start
  807.0 31.8 %copy-start.19 = (bf16[128,576]{0,1:T(8,128)(2,1)}, bf16[128,576]{0,1:T(8,128)(2,1)S(1)}, u32[]{:S(2)}) copy-start(bf16[128,576]{0,1:T(8,128)(2,1)S(1)} %get-tuple-element.115) | copy-start | bytes 442372
  807.1 30.4 %copy-start.161 = (f32[128]{0:T(128)}, f32[128]{0:T(128)S(1)}, u32[]{:S(2)}) copy-start(f32[128]{0:T(128)S(1)} %add_rsqrt_fusion.3) | copy-start | bytes 1540
  835.5 58.7 %copy-start.55 = (bf16[128,9,32]{0,2,1:T(8,128)(2,1)}, bf16[128,9,32]{0,2,1:T(8,128)(2,1)S(1)}, u32[]{:S(2)}) copy-start(bf16[128,9,32]{0,2,1:T(8,128)(2,1)S(1)} %get-tuple-element.145) | copy-start | bytes 221188
  835.5 58.7 %copy-start.57 = (bf16[128,9,32]{0,2,1:T(8,128)(2,1)}, bf16[128,9,32]{0,2,1:T(8,128)(2,1)S(1)}, u32[]{:S(2)}) copy-start(bf16[128,9,32]{0,2,1:T(8,128)(2,1)S(1)} %get-tuple-element.146) | copy-start | bytes 221188
  837.5 55.5 %copy-start.148 = (f32[3,3,128]{2,1,0:T(4,128)}, f32[3,3,128]{2,1,0:T(4,128)S(1)}, u32[]{:S(2)}) copy-start(f32[3,3,128]{2,1,0:T(4,128)S(1)} %get-tuple-element.107) | copy-start | bytes 13828
  839.3 48.9 %copy-start.9 = (f32[128,576]{0,1:T(8,128)}, f32[128,576]{0,1:T(8,128)S(1)}, u32[]{:S(2)}) copy-start(f32[128,576]{0,1:T(8,128)S(1)} %get-tuple-element.196) | copy-start | bytes 884740
  842.5 37.5 %copy-start.129 = (bf16[128,1536]{1,0:T(8,128)(2,1)}, bf16[128,1536]{1,0:T(8,128)(2,1)S(1)}, u32[]{:S(2)}) copy-start(bf16[128,1536]{1,0:T(8,128)(2,1)S(1)} %get-tuple-element.121) | copy-start | bytes 1179652
  842.5 45.7 %copy-start.134 = (bf16[128,1536]{1,0:T(8,128)(2,1)}, bf16[128,1536]{1,0:T(8,128)(2,1)S(1)}, u32[]{:S(2)}) copy-start(bf16[128,1536]{1,0:T(8,128)(2,1)S(1)} %get-tuple-element.120) | copy-start | bytes 1179652
  842.6 38.1 %copy-start.93 = (pred[128,1024]{0,1:T(8,128)(4,1)S(1)}, pred[128,1024]{0,1:T(8,128)(4,1)}, u32[]{:S(2)}) copy-start(pred[128,1024]{0,1:T(8,128)(4,1)} %get-tuple-element.178) | copy-start | bytes 393220
  844.2 9.5 collective-permute-start.2
  853.7 32.7 %copy-start.22 = (bf16[128,576]{0,1:T(8,128)(2,1)}, bf16[128,576]{0,1:T(8,128)(2,1)S(1)}, u32[]{:S(2)}) copy-start(bf16[128,576]{0,1:T(8,128)(2,1)S(1)} %get-tuple-element.113) | copy-start | bytes 442372
  854.4 25.7 %copy-start.159 = (f32[128]{0:T(128)}, f32[128]{0:T(128)S(1)}, u32[]{:S(2)}) copy-start(f32[128]{0:T(128)S(1)} %get-tuple-element.175) | copy-start | bytes 1540
  897.6 63.5 %reduce-scatter.11.cloned.1.call-start = ((), (), s32[]{:S(2)}) async-start(), calls=%async_computation.10 | async-start | bytes 884736 | tf_op jit(solution)/shard_map/reduce_scatter | solution.py:217
  906.4 112.5 %reduce-scatter.13.cloned.1.call-start = ((), (), s32[]{:S(2)}) async-start(), calls=%async_computation.11 | async-start | bytes 884736 | tf_op jit(solution)/shard_map/reduce_scatter | solution.py:214
  964.7 8.5 collective-permute-start.1
  966.7 18.4 %copy-start.146 = (f32[3,3,128]{2,1,0:T(4,128)}, f32[3,3,128]{2,1,0:T(4,128)S(1)}, u32[]{:S(2)}) copy-start(f32[3,3,128]{2,1,0:T(4,128)S(1)} %broadcast_select_fusion.41) | copy-start | bytes 13828
  989.7 61.9 %reduce-scatter.15.cloned.1.call-start = ((), (), s32[]{:S(2)}) async-start(), calls=%async_computation.12 | async-start | bytes 884736 | tf_op jit(solution)/shard_map/reduce_scatter | solution.py:217
  994.3 116.8 %reduce-scatter.17.cloned.1.call-start = ((), (), s32[]{:S(2)}) async-start(), calls=%async_computation.13 | async-start | bytes 884736 | tf_op jit(solution)/shard_map/reduce_scatter | solution.py:214
  1051.7 13.0 copy-start.103
  1051.7 13.0 copy-start.131
  1051.7 13.0 copy-start.136
  1056.1 8.5 collective-permute-start.3
  1074.9 61.9 %reduce-scatter.19.cloned.1.call-start = ((), (), s32[]{:S(2)}) async-start(), calls=%async_computation.14 | async-start | bytes 884736 | tf_op jit(solution)/shard_map/reduce_scatter | solution.py:217
  1083.1 682.4 %all-reduce.16.cloned.1.call-start = ((), (), s32[]{:S(2)}) async-start(), calls=%async_computation.15 | async-start | bytes 30277632
  1140.4 155.1 %copy-start.54 = (f32[128,576]{0,1:T(8,128)S(1)}, f32[128,576]{0,1:T(8,128)}, u32[]{:S(2)}) copy-start(f32[128,576]{0,1:T(8,128)} %copy-done.53) | copy-start | bytes 884740
  1140.4 155.1 %copy-start.166 = (f32[128]{0:T(128)S(1)}, f32[128]{0:T(128)}, u32[]{:S(2)}) copy-start(f32[128]{0:T(128)} %get-tuple-element.89) | copy-start | bytes 1540
  1144.5 151.2 %copy-start.91 = (f32[128,576]{0,1:T(8,128)S(1)}, f32[128,576]{0,1:T(8,128)}, u32[]{:S(2)}) copy-start(f32[128,576]{0,1:T(8,128)} %get-tuple-element.198) | copy-start | bytes 884740
  1144.6 151.2 %copy-start.92 = (f32[1,1,1,128,576]{3,4,2,1,0:T(8,128)S(1)}, f32[1,1,1,128,576]{3,4,2,1,0:T(8,128)}, u32[]{:S(2)}) copy-start(f32[1,1,1,128,576]{3,4,2,1,0:T(8,128)} %fusion.93) | copy-start | bytes 884740
  1144.6 151.2 %copy-start.95 = (f32[128,576]{0,1:T(8,128)S(1)}, f32[128,576]{0,1:T(8,128)}, u32[]{:S(2)}) copy-start(f32[128,576]{0,1:T(8,128)} %get-tuple-element.99) | copy-start | bytes 884740
  (142 other events, 652.4 us)
Sparse Core Ops, SparseCore 0:
  10.3 161.7 all-gather.3
  174.3 159.8 all-gather.5
  335.9 156.4 all-gather.7
  897.7 30.7 reduce-scatter.8
  930.8 30.2 reduce-scatter.10
  989.9 29.0 reduce-scatter.12
  1021.5 30.1 reduce-scatter.14
  1075.0 29.0 reduce-scatter.16
  1106.6 30.1 reduce-scatter.18
  1140.5 624.9 all-reduce.15
where the time goes:
time: 1790 us; the launch traced here: 1780 us
  blocking collectives  945 us (53%)
  waiting for transfers between devices  596 us (33%)
  matrix products  100 us (6%)
  local copies, waits for them, and re-layouts  64.9 us (4%)
  other arithmetic  40.4 us (2%)
  between operations  19.3 us (1%)
    unnamed x11, waiting for transfers between devices  470 us
    unnamed x2, blocking collectives  286 us
    all_gather x1, blocking collectives, local(): lax.all_gather(w_out, ('ctx', 'fsdp'), axis=1, tiled=True)  155 us
    all_gather x1, blocking collectives, local(): lax.all_gather(w_value, ('ctx', 'fsdp'), axis=1, tiled=True)  145 us
    all_gather x1, blocking collectives, local(): lax.all_gather(w_query, ('ctx', 'fsdp'), axis=1, tiled=True)  145 us
    all_gather x1, blocking collectives, local(): lax.all_gather(w_key, ('ctx', 'fsdp'), axis=1, tiled=True)  141 us
    reduce_scatter x3, waiting for transfers between devices, backward_layer(): lax.psum_scatter(value_part.reshape(seq_len, KV_HEADS * HEAD_DIM), 'ctx',...  79.2 us
    all_gather x3, blocking collectives, forward_layer(): lax.all_gather(values, 'ctx', axis=0, tiled=True)  36.5 us
  transfers between devices with their start and end apart: 14, of which 10 were waited for; matrix products, arithmetic and copies ran while one was open for 7% of the time, Pallas kernels for 0%

commit v1 on v0

v1 whole, which is shorter than its diff:
```python
import functools

import jax
import jax.numpy as jnp
from jax import lax
from jax.experimental import pallas as pl
from jax.experimental.pallas import tpu as pltpu
from jax.sharding import PartitionSpec as P

MESH = pl.DeviceIdType.MESH
F32 = jnp.float32
BF16 = jnp.bfloat16
ANY = pl.BlockSpec(memory_space=pl.ANY)
VMEM = pl.BlockSpec(memory_space=pltpu.VMEM)

D = 576
FF = 1536
KVD = 192
HEAD = 64
GROUP = 3
KV_HEADS = 3
ROWS = 128
SEQ = 1024
LANES = 128

norm_eps = 1e-05
rope_base = 100000.0
masked_score = -1e30

WIDE = 4608
GATE_AT = 768
UP_AT = GATE_AT + FF
OUT_AT = UP_AT + FF
VALUE_AT = OUT_AT + D
TAIL_AT = VALUE_AT - HEAD
BLOCKS = WIDE // LANES

DOWN_ROWS = 24
TAIL_ROW = 4 * DOWN_ROWS
WIDE_ROW = TAIL_ROW + DOWN_ROWS // 2
GAIN_ROW = WIDE_ROW + 9 * BLOCKS
PACKED = GAIN_ROW + 16
THIRDS = ((0, 160), (160, 144), (304, 144))
AXIS_ORDERS = (("z", "x", "y"), ("x", "y", "z"), ("y", "z", "x"))
VMEM_BYTES = 60 * 1024 * 1024


def params(collective_id=None):
    if collective_id is None:
        return pltpu.CompilerParams(vmem_limit_bytes=VMEM_BYTES)
    return pltpu.CompilerParams(
        vmem_limit_bytes=VMEM_BYTES, collective_id=collective_id, has_side_effects=True
    )


def dot(left, right):
    return jnp.dot(left, right, preferred_element_type=F32)


def dot_nt(left, right):
    return lax.dot_general(left, right, (((1,), (1,)), ((), ())), preferred_element_type=F32)


def dot_tn(left, right):
    return lax.dot_general(left, right, (((0,), (0,)), ((), ())), preferred_element_type=F32)


class Place:
    def __init__(self):
        self.section = lax.axis_index("section")
        ctx = lax.axis_index("ctx")
        fsdp = lax.axis_index("fsdp")
        self.core = lax.rem(ctx, 2)
        self.at = {
            "x": lax.rem(fsdp, 4),
            "y": ctx // 2,
            "z": self.section * 2 + fsdp // 4,
        }

    def device(self, core=None, **moved):
        at = dict(self.at, **moved)
        core = self.core if core is None else core
        return (at["z"] // 2, at["y"] * 2 + core, lax.rem(at["z"], 2) * 4 + at["x"])

    def shifted(self, axis, step):
        return lax.rem(self.at[axis] + step + 4, 4)

    def neighbour(self, axis, step):
        return self.device(**{axis: self.shifted(axis, step)})

    def partner(self):
        return self.device(core=1 - self.core)


def greet(devices):
    barrier = pltpu.get_barrier_semaphore()
    for device in devices:
        pl.semaphore_signal(barrier, inc=1, device_id=device, device_id_type=MESH)
    pl.semaphore_wait(barrier, len(devices))


def torus_neighbours(place):
    return [place.neighbour(axis, step) for axis in "xyz" for step in (1, -1)]


def region(ref, coords, whole, rows, core):
    first, count = rows
    z_hi = slice(None) if "z" in whole else coords["z"] // 2
    z_lo = slice(None) if "z" in whole else lax.rem(coords["z"], 2)
    y = slice(None) if "y" in whole else coords["y"]
    x = slice(None) if "x" in whole else coords["x"]
    if core is None:
        return ref.at[z_hi, y, z_lo, x, pl.ds(first, count)]
    return ref.at[z_hi, y, core, z_lo, x, pl.ds(first, count)]


def halves(rows):
    first, count = rows
    upper = (count // 2 + 15) // 16 * 16
    return (first, upper), (first + upper, count - upper)


def gather_kernel(mine_ref, out_ref, local_sem, send_sems, recv_sems):
    place = Place()
    core = place.core
    greet(torus_neighbours(place) + [place.partner()])

    own = out_ref.at[place.section, place.at["y"], core, lax.rem(place.at["z"], 2), place.at["x"]]
    seed = pltpu.make_async_copy(mine_ref, own, local_sem)
    seed.start()
    seed.wait()

    counter = [0]
    unsent = []

    def send(ref, device):
        slot = counter[0]
        counter[0] += 1
        copy = pltpu.make_async_remote_copy(
            src_ref=ref,
            dst_ref=ref,
            send_sem=send_sems.at[slot],
            recv_sem=recv_sems.at[slot],
            device_id=device,
            device_id_type=MESH,
        )
        copy.start()
        unsent.append(copy)
        return copy

    to_partner = []
    for phase in range(3):
        arriving = []
        for third, rows in enumerate(THIRDS):
            axis = AXIS_ORDERS[third][phase]
            whole = AXIS_ORDERS[third][:phase]
            block = region(out_ref, place.at, whole, rows, core)
            arriving.append(
                [send(block, place.neighbour(axis, 1)), send(block, place.neighbour(axis, -1))]
            )
            if phase == 2:
                to_partner.append(send(block, place.partner()))
        second = []
        for third, rows in enumerate(THIRDS):
            axis = AXIS_ORDERS[third][phase]
            whole = AXIS_ORDERS[third][:phase]
            for copy in arriving[third]:
                copy.wait_recv()
            upper, lower = halves(rows)
            left = dict(place.at, **{axis: place.shifted(axis, -1)})
            right = dict(place.at, **{axis: place.shifted(axis, 1)})
            second.append(
                [
                    send(region(out_ref, left, whole, upper, core), place.neighbour(axis, 1)),
                    send(region(out_ref, right, whole, lower, core), place.neighbour(axis, -1)),
                ]
            )
            if phase == 2:
                for coords in (left, right):
                    to_partner.append(
                        send(region(out_ref, coords, whole, rows, core), place.partner())
                    )
        for third, rows in enumerate(THIRDS):
            axis = AXIS_ORDERS[third][phase]
            whole = AXIS_ORDERS[third][:phase]
            for copy in second[third]:
                copy.wait_recv()
            if phase == 2:
                far = dict(place.at, **{axis: place.shifted(axis, 2)})
                to_partner.append(send(region(out_ref, far, whole, rows, core), place.partner()))
    for copy in to_partner:
        copy.wait_recv()
    for copy in unsent:
        copy.wait_send()


def gather_weights(packed):
    slots = 3 * 3 * 4 + 3 * 4
    return pl.pallas_call(
        gather_kernel,
        out_shape=jax.ShapeDtypeStruct((2, 4, 2, 2, 4, PACKED, LANES), BF16),
        in_specs=[ANY],
        out_specs=ANY,
        scratch_shapes=[
            pltpu.SemaphoreType.DMA,
            pltpu.SemaphoreType.DMA((slots,)),
            pltpu.SemaphoreType.DMA((slots,)),
        ],
        compiler_params=params(0),
        name="gather_weights",
    )(packed)


def scatter_kernel(
    first_ref,
    second_ref,
    edge_ref,
    out_ref,
    edge_out_ref,
    total,
    swapped,
    arrivals_0,
    arrivals_1,
    arrivals_2,
    local_sems,
    swap_send,
    swap_recv,
    send_sems,
    recv_sems,
    edge_send,
    edge_recv,
):
    place = Place()
    core = place.core
    across = (1 - place.section, lax.axis_index("ctx"), lax.axis_index("fsdp"))
    greet(torus_neighbours(place) + [place.partner(), across])

    swaps = []
    loads = []
    for third, (first, count) in enumerate(THIRDS):
        rows = pl.ds(first, count)
        for layer, part_ref in enumerate((first_ref, second_ref)):
            slot = third * 2 + layer
            swap = pltpu.make_async_remote_copy(
                src_ref=part_ref.at[:, 1 - core, :, :, rows],
                dst_ref=swapped.at[layer, :, :, :, rows],
                send_sem=swap_send.at[slot],
                recv_sem=swap_recv.at[slot],
                device_id=place.partner(),
                device_id_type=MESH,
            )
            swap.start()
            load = pltpu.make_async_copy(
                part_ref.at[:, core, :, :, rows],
                total.at[layer, :, :, :, rows],
                local_sems.at[slot],
            )
            load.start()
            swaps.append(swap)
            loads.append(load)
    edge = pltpu.make_async_remote_copy(
        src_ref=edge_ref,
        dst_ref=edge_out_ref,
        send_sem=edge_send,
        recv_sem=edge_recv,
        device_id=across,
        device_id_type=MESH,
    )
    edge.start()

    counter = [0]
    unsent = []

    def send(source, target, device):
        slot = counter[0]
        counter[0] += 1
        copy = pltpu.make_async_remote_copy(
            src_ref=source,
            dst_ref=target,
            send_sem=send_sems.at[slot],
            recv_sem=recv_sems.at[slot],
            device_id=device,
            device_id_type=MESH,
        )
        copy.start()
        unsent.append(copy)
        return copy

    def add(coords, whole, rows, source, first=0):
        at, count = rows
        sizes = [4 if axis in whole else 1 for axis in "zyx"]

        def body(step, carry):
            z = step // (sizes[1] * sizes[2])
            y = lax.rem(step // sizes[2], sizes[1])
            x = lax.rem(step, sizes[2])
            spot = (
                z if "z" in whole else coords["z"],
                y if "y" in whole else coords["y"],
                x if "x" in whole else coords["x"],
            )
            here = (spot[0] // 2, spot[1], lax.rem(spot[0], 2), spot[2], pl.ds(at, count))
            total[here] = (
                total[here].astype(F32) + source(z, y, x, first, count).astype(F32)
            ).astype(BF16)
            return carry

        lax.fori_loop(0, sizes[0] * sizes[1] * sizes[2], body, 0)

    def swapped_part(rows):
        def load(z, y, x, first, count):
            return swapped[z // 2, y, lax.rem(z, 2), x, pl.ds(rows[0], count)]

        return load

    arrivals = (arrivals_0, arrivals_1, arrivals_2)
    used = [0, 0, 0]

    def ring(third, phase, step):
        rows = THIRDS[third]
        order = AXIS_ORDERS[third][::-1]
        axis = order[phase]
        whole = order[phase + 1 :]
        upper, lower = halves(rows)
        right = dict(place.at, **{axis: place.shifted(axis, 1)})
        left = dict(place.at, **{axis: place.shifted(axis, -1)})
        far = dict(place.at, **{axis: place.shifted(axis, 2)})
        if step == 0:
            plan = ((far, upper, 1, right), (far, lower, -1, left))
        else:
            plan = ((right, rows, 1, place.at), (left, rows, -1, place.at))
        started = []
        for source_at, part, way, lands in plan:
            device = place.neighbour(axis, way)
            first = used[third]
            used[third] += 1
            copy = send(
                region(total, source_at, whole, part, None),
                landing(third, first, whole, part[1]),
                device,
            )
            started.append((copy, lands, part, first, whole))
        return started

    def landing(third, slot, whole, count):
        z_hi = slice(None) if "z" in whole else 0
        z_lo = slice(None) if "z" in whole else 0
        y = slice(None) if "y" in whole else 0
        x = slice(None) if "x" in whole else 0
        return arrivals[third].at[slot, z_hi, y, z_lo, x, pl.ds(0, count)]

    def arrived_part(third, slot):
        def load(z, y, x, first, count):
            return arrivals[third][slot, z // 2, y, lax.rem(z, 2), x, pl.ds(0, count)]

        return load

    def finish(third, started):
        for copy, lands, part, slot, whole in started:
            copy.wait()
            add(lands, whole, part, arrived_part(third, slot))

    flights = []
    for third, rows in enumerate(THIRDS):
        for layer in range(2):
            loads[third * 2 + layer].wait()
            swaps[third * 2 + layer].wait()
        add(place.at, ("z", "y", "x"), rows, swapped_part(rows))
        flights.append(ring(third, 0, 0))
    for phase in range(3):
        for step in range(2):
            for third in range(3):
                finish(third, flights[third])
                if step == 0:
                    flights[third] = ring(third, phase, 1)
                elif phase < 2:
                    flights[third] = ring(third, phase + 1, 0)

    z, y, x = place.at["z"], place.at["y"], place.at["x"]
    out_ref[...] = total[z // 2, y, lax.rem(z, 2), x].astype(F32)
    edge.wait()


def scatter_grads(first, second, edge):
    slots = 3 * 3 * 4
    return pl.pallas_call(
        scatter_kernel,
        out_shape=(
            jax.ShapeDtypeStruct((PACKED, LANES), F32),
            jax.ShapeDtypeStruct((ROWS, D), F32),
        ),
        in_specs=[ANY, ANY, VMEM],
        out_specs=(VMEM, VMEM),
        scratch_shapes=[
            pltpu.VMEM((2, 4, 2, 4, PACKED, LANES), BF16),
            pltpu.VMEM((2, 4, 2, 4, PACKED, LANES), BF16),
            pltpu.VMEM((12, 2, 1, 2, 4, 160, LANES), BF16),
            pltpu.VMEM((12, 1, 4, 1, 4, 144, LANES), BF16),
            pltpu.VMEM((12, 2, 4, 2, 1, 144, LANES), BF16),
            pltpu.SemaphoreType.DMA((6,)),
            pltpu.SemaphoreType.DMA((6,)),
            pltpu.SemaphoreType.DMA((6,)),
            pltpu.SemaphoreType.DMA((slots,)),
            pltpu.SemaphoreType.DMA((slots,)),
            pltpu.SemaphoreType.DMA,
            pltpu.SemaphoreType.DMA,
        ],
        compiler_params=params(1),
        name="scatter_grads",
    )(first, second, edge)


def ctx_device(index):
    return (lax.axis_index("section"), index, lax.axis_index("fsdp"))


def greet_ctx(mine):
    greet([ctx_device(lax.rem(mine + away, 8)) for away in range(1, 8)])


def keys_kernel(mine_ref, out_ref, send_sems, recv_sems):
    mine = lax.axis_index("ctx")
    greet_ctx(mine)

    def copy_to(away):
        return pltpu.make_async_remote_copy(
            src_ref=mine_ref,
            dst_ref=out_ref.at[mine],
            send_sem=send_sems.at[away],
            recv_sem=recv_sems.at[away],
            device_id=ctx_device(lax.rem(mine + away, 8)),
            device_id_type=MESH,
        )

    for away in range(1, 8):

        @pl.when(mine + away < 8)
        def _():
            copy_to(away).start()

    out_ref[mine] = mine_ref[...]
    for away in range(1, 8):

        @pl.when(mine + away < 8)
        def _():
            out_ref[mine + away] = jnp.zeros(out_ref.shape[1:], out_ref.dtype)

    for away in range(1, 8):

        @pl.when(mine - away >= 0)
        def _():
            copy_to(away).wait_recv()

    for away in range(1, 8):

        @pl.when(mine + away < 8)
        def _():
            copy_to(away).wait_send()


def gather_keys(joined, collective_id):
    return pl.pallas_call(
        keys_kernel,
        out_shape=jax.ShapeDtypeStruct((8, ROWS, 2 * KVD), BF16),
        in_specs=[VMEM],
        out_specs=VMEM,
        scratch_shapes=[pltpu.SemaphoreType.DMA((8,)), pltpu.SemaphoreType.DMA((8,))],
        compiler_params=params(collective_id),
        name="gather_keys",
    )(joined)


def key_grads_kernel(parts_ref, out_ref, arrived, send_sems, recv_sems):
    mine = lax.axis_index("ctx")
    greet_ctx(mine)

    def copy_to(away):
        return pltpu.make_async_remote_copy(
            src_ref=parts_ref.at[lax.rem(mine - away + 8, 8)],
            dst_ref=arrived.at[away],
            send_sem=send_sems.at[away],
            recv_sem=recv_sems.at[away],
            device_id=ctx_device(lax.rem(mine - away + 8, 8)),
            device_id_type=MESH,
        )

    for away in range(1, 8):

        @pl.when(mine - away >= 0)
        def _():
            copy_to(away).start()

    out_ref[...] = parts_ref[mine].astype(F32)
    for away in range(1, 8):

        @pl.when(mine + away < 8)
        def _():
            copy_to(away).wait_recv()
            out_ref[...] += arrived[away].astype(F32)

    for away in range(1, 8):

        @pl.when(mine - away >= 0)
        def _():
            copy_to(away).wait_send()


def scatter_key_grads(parts, collective_id):
    return pl.pallas_call(
        key_grads_kernel,
        out_shape=jax.ShapeDtypeStruct((2 * KVD, ROWS), F32),
        in_specs=[VMEM],
        out_specs=VMEM,
        scratch_shapes=[
            pltpu.VMEM((8, 2 * KVD, ROWS), BF16),
            pltpu.SemaphoreType.DMA((8,)),
            pltpu.SemaphoreType.DMA((8,)),
        ],
        compiler_params=params(collective_id),
        name="scatter_key_grads",
    )(parts)


def pack_kernel(
    attn_ref, query_ref, key_ref, value_ref, w_out_ref, gate_ref, up_ref, down_ref, mlp_ref, out_ref
):
    def wide(ref):
        return ref[0].astype(F32)

    joined = jnp.concatenate(
        [wide(r) for r in (query_ref, key_ref, gate_ref, up_ref, w_out_ref, value_ref)], axis=1
    )
    down = wide(down_ref)
    pieces = [down[:, i * LANES : (i + 1) * LANES] for i in range(4)]
    half = DOWN_ROWS // 2
    pieces.append(jnp.concatenate([down[:half, 4 * LANES :], down[half:, 4 * LANES :]], axis=1))
    pieces += [joined[:, i * LANES : (i + 1) * LANES] for i in range(BLOCKS)]
    for ref in (attn_ref, mlp_ref):
        gain = ref[...].astype(F32)
        pieces.append(jnp.concatenate([gain, jnp.zeros((1, LANES - 9), F32)], axis=1))
    pieces.append(jnp.zeros((14, LANES), F32))
    out_ref[...] = jnp.concatenate(pieces, axis=0).astype(BF16)


def pack_shards(shards):
    return pl.pallas_call(
        pack_kernel,
        out_shape=jax.ShapeDtypeStruct((PACKED, LANES), BF16),
        in_specs=[VMEM] * 9,
        out_specs=VMEM,
        compiler_params=params(),
        name="pack_shards",
    )(*shards)


def gain_masks(first_device, devices, rows_each):
    shape = (devices * rows_each, D)
    row = lax.broadcasted_iota(jnp.int32, shape, 0)
    owner = lax.broadcasted_iota(jnp.int32, shape, 1) // 9
    same = owner == first_device + row // rows_each
    place = lax.rem(row, rows_each)
    return same & (place == 0), same & (place == 1)


def lane_spread():
    lane = lax.broadcasted_iota(jnp.int32, (LANES, D), 0)
    feature = lax.broadcasted_iota(jnp.int32, (LANES, D), 1)
    return (lane == lax.rem(feature, 9)).astype(BF16)


def unpack_kernel(packed_ref, wide_ref, down_ref, gains_ref):
    block = pl.program_id(1)
    count = packed_ref.shape[0]
    held = [packed_ref[i].astype(F32) for i in range(count)]
    for column in range(BLOCKS):
        at = WIDE_ROW + 9 * column
        wide_ref[0, :, column * LANES : (column + 1) * LANES] = jnp.concatenate(
            [h[at : at + 9] for h in held], axis=0
        ).astype(BF16)
    for column in range(4):
        at = DOWN_ROWS * column
        down_ref[0, :, column * LANES : (column + 1) * LANES] = jnp.concatenate(
            [h[at : at + DOWN_ROWS] for h in held], axis=0
        ).astype(BF16)
    tails = []
    for h in held:
        tail = h[TAIL_ROW:WIDE_ROW]
        tails += [tail[:, :HEAD], tail[:, HEAD:]]
    down_ref[0, :, 4 * LANES :] = jnp.concatenate(tails, axis=0).astype(BF16)
    rows = packed_ref[:, GAIN_ROW:, :].reshape(count * 16, LANES)
    spread = dot(rows, lane_spread())
    first, second = gain_masks(block * count, count, 16)
    gains = [
        jnp.sum(jnp.where(mask, spread, 0.0), axis=0, keepdims=True) for mask in (first, second)
    ]

    @pl.when(block == 0)
    def _():
        gains_ref[...] = jnp.zeros_like(gains_ref)

    gains_ref[0, 0:1] += gains[0]
    gains_ref[0, 1:2] += gains[1]


def unpack_weights(gathered):
    count = 16
    return pl.pallas_call(
        unpack_kernel,
        grid=(2, 4),
        out_shape=(
            jax.ShapeDtypeStruct((2, D, WIDE), BF16),
            jax.ShapeDtypeStruct((2, FF, D), BF16),
            jax.ShapeDtypeStruct((2, 8, D), F32),
        ),
        in_specs=[pl.BlockSpec((count, PACKED, LANES), lambda s, y: (s * 4 + y, 0, 0))],
        out_specs=(
            pl.BlockSpec((1, 9 * count, WIDE), lambda s, y: (s, y, 0)),
            pl.BlockSpec((1, DOWN_ROWS * count, D), lambda s, y: (s, y, 0)),
            pl.BlockSpec((1, 8, D), lambda s, y: (s, 0, 0)),
        ),
        compiler_params=params(),
        name="unpack_weights",
    )(gathered.reshape(128, PACKED, LANES))


def finish_kernel(
    packed_ref,
    kept_ref,
    came_ref,
    edges_ref,
    attn_ref,
    query_ref,
    key_ref,
    value_ref,
    w_out_ref,
    gate_ref,
    up_ref,
    down_ref,
    mlp_ref,
):
    section = lax.axis_index("section")
    edges_ref[0, section, 0] = kept_ref[...]
    edges_ref[0, 1 - section, 0] = came_ref[...]
    packed = packed_ref[...]
    joined = jnp.concatenate(
        [packed[WIDE_ROW + 9 * i : WIDE_ROW + 9 * i + 9] for i in range(BLOCKS)], axis=1
    )
    query_ref[0] = joined[:, :D]
    key_ref[0] = joined[:, D:GATE_AT]
    gate_ref[0] = joined[:, GATE_AT:UP_AT]
    up_ref[0] = joined[:, UP_AT:OUT_AT]
    w_out_ref[0] = joined[:, OUT_AT:VALUE_AT]
    value_ref[0] = joined[:, VALUE_AT:]
    tail = packed[TAIL_ROW:WIDE_ROW]
    down_ref[0] = jnp.concatenate(
        [packed[DOWN_ROWS * i : DOWN_ROWS * (i + 1)] for i in range(4)]
        + [jnp.concatenate([tail[:, :HEAD], tail[:, HEAD:]], axis=0)],
        axis=1,
    )
    attn_ref[...] = packed[GAIN_ROW : GAIN_ROW + 1, :9]
    mlp_ref[...] = packed[GAIN_ROW + 1 : GAIN_ROW + 2, :9]


def finish(packed, kept, came):
    shapes = (
        (1, 2, 1, ROWS, D),
        (1, 9),
        (1, 9, D),
        (1, 9, KVD),
        (1, 9, KVD),
        (1, 9, D),
        (1, 9, FF),
        (1, 9, FF),
        (1, DOWN_ROWS, D),
        (1, 9),
    )
    return pl.pallas_call(
        finish_kernel,
        out_shape=tuple(jax.ShapeDtypeStruct(shape, F32) for shape in shapes),
        in_specs=[VMEM] * 3,
        out_specs=(VMEM,) * len(shapes),
        compiler_params=params(),
        name="finish",
    )(packed, kept, came)


def swap_halves(block):
    lane = lax.broadcasted_iota(jnp.int32, block.shape, 1)
    return jnp.where(
        lax.rem(lane, HEAD) < HEAD // 2,
        pltpu.roll(block, LANES - HEAD // 2, 1),
        pltpu.roll(block, HEAD // 2, 1),
    )


def rotated(block, cos, sin):
    return block * cos + swap_halves(block) * sin


def project(current, gain, weights, cos, sin, normed_ref, query_ref, joined_ref):
    scale = lax.rsqrt(jnp.mean(current * current, axis=1, keepdims=True) + norm_eps)
    normed = (current * scale * gain).astype(BF16)
    normed_ref[...] = normed
    raw = dot(normed, weights.get("qk"))
    turned = [
        rotated(raw[:, i * LANES : (i + 1) * LANES], cos, sin).astype(BF16) for i in range(6)
    ]
    for i in range(4):
        query_ref[:, i * LANES : (i + 1) * LANES] = turned[i]
    query_ref[:, 4 * LANES :] = turned[4][:, :HEAD]
    values = dot(normed, weights.get("tail"))[:, HEAD:]
    joined_ref[...] = jnp.concatenate(
        [turned[4][:, HEAD:].astype(F32), turned[5].astype(F32), values], axis=1
    ).astype(BF16)


def heads_of(rows, group):
    return jnp.concatenate(
        [rows[:, (group * GROUP + r) * HEAD : (group * GROUP + r + 1) * HEAD] for r in range(GROUP)],
        axis=0,
    )


def attend(query_ref, keys_ref, own_seg_ref, seg_ref, probs_ref):
    first = lax.axis_index("ctx") * ROWS
    rows = first + lax.broadcasted_iota(jnp.int32, (ROWS, SEQ), 0)
    columns = lax.broadcasted_iota(jnp.int32, (ROWS, SEQ), 1)
    allowed = (columns <= rows) & (seg_ref[...] == own_seg_ref[...])
    bias = jnp.where(allowed, 0.0, masked_score)
    bias = jnp.concatenate([bias] * GROUP, axis=0)
    queries = query_ref[...]
    mixed = []
    for group in range(KV_HEADS):
        keys = keys_ref[:, :, group * HEAD : (group + 1) * HEAD].reshape(SEQ, HEAD)
        values = keys_ref[:, :, KVD + group * HEAD : KVD + (group + 1) * HEAD].reshape(SEQ, HEAD)
        scores = dot_nt(heads_of(queries, group), keys) * HEAD**-0.5 + bias
        shifted = jnp.exp(scores - jnp.max(scores, axis=1, keepdims=True))
        probs = (shifted / jnp.sum(shifted, axis=1, keepdims=True)).astype(BF16)
        probs_ref[group] = probs
        mixture = dot(probs, values)
        mixed += [mixture[r * ROWS : (r + 1) * ROWS] for r in range(GROUP)]
    return jnp.concatenate(mixed, axis=1).astype(BF16)


def feed_forward(current, attended, gain, weights):
    midway = current + dot(attended, weights.out())
    scale = lax.rsqrt(jnp.mean(midway * midway, axis=1, keepdims=True) + norm_eps)
    normed = (midway * scale * gain).astype(BF16)
    gate = dot(normed, weights.get("gate"))
    up = dot(normed, weights.get("up"))
    hidden = (gate / (1.0 + jnp.exp(-gate)) * up).astype(BF16)
    result = midway + dot(hidden, weights.get("down"))
    return midway, scale, normed, gate, up, hidden, result


def norm_backward(scaled, values, scale):
    return scale * scaled - values * scale**3 * jnp.mean(scaled * values, axis=1, keepdims=True)


def feed_forward_back(
    incoming, midway, gate, up, gain, weights
):
    scale = lax.rsqrt(jnp.mean(midway * midway, axis=1, keepdims=True) + norm_eps)
    down_grad = incoming.astype(BF16)
    hidden_grad = dot_nt(down_grad, weights.get("down"))
    sigmoid = 1.0 / (1.0 + jnp.exp(-gate))
    gate_grad = (hidden_grad * up * sigmoid * (1.0 + gate * (1.0 - sigmoid))).astype(BF16)
    up_grad = (hidden_grad * gate * sigmoid).astype(BF16)
    normed_grad = dot_nt(gate_grad, weights.get("gate")) + dot_nt(
        up_grad, weights.get("up")
    )
    gain_grad = jnp.sum(normed_grad * midway * scale, axis=0, keepdims=True)
    midway_grad = incoming + norm_backward(normed_grad * gain, midway, scale)
    out_grad = midway_grad.astype(BF16)
    mixed_grad = dot_nt(out_grad, weights.out()).astype(BF16)
    return down_grad, gate_grad, up_grad, gain_grad, midway_grad, out_grad, mixed_grad


def attend_back(mixed_grad, attended, query_ref, keys_ref, probs_ref, parts_ref):
    queries = query_ref[...]
    query_grads = []
    for group in range(KV_HEADS):
        keys = keys_ref[:, :, group * HEAD : (group + 1) * HEAD].reshape(SEQ, HEAD)
        values = keys_ref[:, :, KVD + group * HEAD : KVD + (group + 1) * HEAD].reshape(SEQ, HEAD)
        grads = heads_of(mixed_grad, group)
        delta = jnp.sum(
            grads.astype(F32) * heads_of(attended, group).astype(F32), axis=1, keepdims=True
        )
        probs = probs_ref[group]
        score_grad = (probs.astype(F32) * (dot_nt(grads, values) - delta)).astype(BF16)
        query_grad = dot(score_grad, keys) * HEAD**-0.5
        query_grads += [query_grad[r * ROWS : (r + 1) * ROWS] for r in range(GROUP)]
        key_part = (dot_tn(heads_of(queries, group), score_grad) * HEAD**-0.5).astype(BF16)
        value_part = dot_tn(grads, probs).astype(BF16)
        for block in range(8):
            columns = slice(block * ROWS, (block + 1) * ROWS)
            parts_ref[block, group * HEAD : (group + 1) * HEAD] = key_part[:, columns]
            parts_ref[block, KVD + group * HEAD : KVD + (group + 1) * HEAD] = value_part[:, columns]
    return jnp.concatenate(query_grads, axis=1)


def project_back(
    query_grad, key_grads, midway_grad, current, gain, cos, sin, weights
):
    key_grads = key_grads.T
    joined = jnp.concatenate([query_grad, key_grads[:, :KVD]], axis=1)
    turned = jnp.concatenate(
        [rotated(joined[:, i * LANES : (i + 1) * LANES], cos, -sin) for i in range(6)], axis=1
    ).astype(BF16)
    values = key_grads[:, KVD:].astype(BF16)
    padded = jnp.concatenate([jnp.zeros((ROWS, HEAD), F32), key_grads[:, KVD:]], axis=1)
    normed_grad = dot_nt(turned, weights.get("qk")) + dot_nt(
        padded.astype(BF16), weights.get("tail")
    )
    scale = lax.rsqrt(jnp.mean(current * current, axis=1, keepdims=True) + norm_eps)
    gain_grad = jnp.sum(normed_grad * current * scale, axis=0, keepdims=True)
    grad_in = midway_grad + norm_backward(normed_grad * gain, current, scale)
    return turned, values, gain_grad, grad_in


GRAD_DEVICES = 16


def weight_grads(
    normed,
    turned,
    values,
    attended,
    out_grad,
    normed_two,
    gate_grad,
    up_grad,
    hidden,
    down_grad,
    attn_gain_grad,
    mlp_gain_grad,
    out_ref,
    lhs_ref,
    hidden_ref,
    stage,
):
    lhs_ref[0] = normed.astype(F32).T.astype(BF16)
    lhs_ref[1] = normed_two.astype(F32).T.astype(BF16)
    lhs_ref[2] = attended.astype(F32).T.astype(BF16)
    hidden_ref[...] = hidden.astype(F32).T.astype(BF16)
    count = GRAD_DEVICES

    def body(step, carry):
        rows = pl.ds(pl.multiple_of(step * 9 * count, 16), 9 * count)

        def place_wide(column, product):
            for i in range(product.shape[1] // LANES):
                at = WIDE_ROW + 9 * (column + i)
                part = product[:, i * LANES : (i + 1) * LANES]
                for d in range(count):
                    stage[d, at : at + 9] = part[9 * d : 9 * d + 9]

        first = lhs_ref[0, rows]
        place_wide(0, dot(first, turned))
        second = lhs_ref[1, rows]
        place_wide(GATE_AT // LANES, dot(second, gate_grad))
        place_wide(UP_AT // LANES, dot(second, up_grad))
        place_wide(
            OUT_AT // LANES,
            jnp.concatenate([dot(lhs_ref[2, rows], out_grad), dot(first, values)], axis=1),
        )
        down_rows = pl.ds(pl.multiple_of(step * DOWN_ROWS * count, 16), DOWN_ROWS * count)
        down = dot(hidden_ref[down_rows], down_grad)
        half = DOWN_ROWS // 2
        for d in range(count):
            own = down[DOWN_ROWS * d : DOWN_ROWS * (d + 1)]
            for i in range(4):
                stage[d, DOWN_ROWS * i : DOWN_ROWS * (i + 1)] = own[:, i * LANES : (i + 1) * LANES]
            stage[d, TAIL_ROW:WIDE_ROW] = jnp.concatenate(
                [own[:half, 4 * LANES :], own[half:, 4 * LANES :]], axis=1
            )
        out_ref[pl.ds(step * count, count), :GAIN_ROW] = stage[...].astype(BF16)
        return carry

    lax.fori_loop(0, 64 // count, body, 0)

    shape = (64 * 16, D)
    row = lax.broadcasted_iota(jnp.int32, shape, 0)
    first, second = gain_masks(0, 64, 16)
    chosen = jnp.where(first, attn_gain_grad, 0.0) + jnp.where(second, mlp_gain_grad, 0.0)
    gathered = dot_nt(chosen.astype(BF16), lane_spread())
    out_ref[:, GAIN_ROW:] = gathered.astype(BF16).reshape(64, 16, LANES)


GRAD_SCRATCH = [
    pltpu.VMEM((3, D, ROWS), BF16),
    pltpu.VMEM((FF, ROWS), BF16),
    pltpu.VMEM((GRAD_DEVICES, GAIN_ROW, LANES), F32),
]


COLUMNS = {
    "qk": (0, GATE_AT),
    "gate": (GATE_AT, FF),
    "up": (UP_AT, FF),
    "out": (OUT_AT, D + KVD),
    "tail": (TAIL_AT, HEAD + KVD),
}
PROJECTION = ("qk", "tail")
REST = ("out", "gate", "up", "down")


def weight_scratch(*names):
    shapes = [(FF, D) if name == "down" else (D, COLUMNS[name][1]) for name in names]
    return [pltpu.VMEM(shape, BF16) for shape in shapes] + [pltpu.SemaphoreType.DMA((len(names),))]


class Weights:
    def __init__(self, wide_ref, down_ref, layer, names, scratch):
        *buffers, sems = scratch
        self.copies = {}
        self.buffers = dict(zip(names, buffers))
        for i, name in enumerate(names):
            if name == "down":
                source = down_ref.at[layer]
            else:
                first, width = COLUMNS[name]
                source = wide_ref.at[layer, :, pl.ds(first, width)]
            self.copies[name] = pltpu.make_async_copy(source, buffers[i], sems.at[i])
            self.copies[name].start()

    def get(self, name):
        if name in self.copies:
            self.copies.pop(name).wait()
        return self.buffers[name][...]

    def out(self):
        return self.get("out")[:, :D]


def like(shape, dtype):
    return jax.ShapeDtypeStruct(shape, dtype)


def start_kernel(
    x_ref, gains_ref, wide_ref, cos_ref, sin_ref, normed_ref, query_ref, joined_ref, *scratch
):
    project(
        x_ref[...].astype(F32),
        gains_ref[0, 0:1],
        Weights(wide_ref, None, 0, PROJECTION, scratch),
        cos_ref[...],
        sin_ref[...],
        normed_ref,
        query_ref,
        joined_ref,
    )


def middle_kernel(
    x_ref,
    gains_ref,
    wide_ref,
    down_ref,
    cos_ref,
    sin_ref,
    query_ref,
    keys_ref,
    own_seg_ref,
    seg_ref,
    probs_ref,
    attended_ref,
    midway_ref,
    normed_two_ref,
    gate_ref,
    up_ref,
    hidden_ref,
    next_x_ref,
    normed_ref,
    next_query_ref,
    joined_ref,
    *scratch,
):
    own = Weights(wide_ref, down_ref, 0, REST, scratch[:5])
    later = Weights(wide_ref, None, 1, PROJECTION, scratch[5:])
    attended = attend(query_ref, keys_ref, own_seg_ref, seg_ref, probs_ref)
    attended_ref[...] = attended
    midway, scale, normed_two, gate, up, hidden, result = feed_forward(
        x_ref[...].astype(F32), attended, gains_ref[0, 1:2], own
    )
    midway_ref[...] = midway
    normed_two_ref[...] = normed_two
    gate_ref[...] = gate
    up_ref[...] = up
    hidden_ref[...] = hidden
    passed = result.astype(BF16)
    next_x_ref[...] = passed
    project(
        passed.astype(F32),
        gains_ref[1, 0:1],
        later,
        cos_ref[...],
        sin_ref[...],
        normed_ref,
        next_query_ref,
        joined_ref,
    )


def turn_kernel(
    x_ref,
    cotangent_ref,
    gains_ref,
    wide_ref,
    down_ref,
    query_ref,
    keys_ref,
    own_seg_ref,
    seg_ref,
    result_ref,
    attended_ref,
    normed_two_ref,
    hidden_ref,
    gate_grad_ref,
    up_grad_ref,
    gain_grad_ref,
    midway_grad_ref,
    out_grad_ref,
    query_grad_ref,
    parts_ref,
    probs,
    *scratch,
):
    own = Weights(wide_ref, down_ref, 1, REST, scratch)
    attended = attend(query_ref, keys_ref, own_seg_ref, seg_ref, probs)
    attended_ref[...] = attended
    gain = gains_ref[1, 1:2]
    midway, scale, normed_two, gate, up, hidden, result = feed_forward(
        x_ref[...].astype(F32), attended, gain, own
    )
    result_ref[...] = result
    normed_two_ref[...] = normed_two
    hidden_ref[...] = hidden
    down_grad, gate_grad, up_grad, gain_grad, midway_grad, out_grad, mixed_grad = feed_forward_back(
        cotangent_ref[...].astype(F32),
        midway,
        gate,
        up,
        gain,
        own,
    )
    gate_grad_ref[...] = gate_grad
    up_grad_ref[...] = up_grad
    gain_grad_ref[...] = gain_grad
    midway_grad_ref[...] = midway_grad
    out_grad_ref[...] = out_grad
    query_grad_ref[...] = attend_back(mixed_grad, attended, query_ref, keys_ref, probs, parts_ref)


def back_kernel(
    key_grads_ref,
    query_grad_ref,
    midway_grad_ref,
    x_ref,
    gains_ref,
    cos_ref,
    sin_ref,
    wide_ref,
    down_ref,
    midway_ref,
    gate_ref,
    up_ref,
    attended_ref,
    query_ref,
    keys_ref,
    probs_ref,
    turned_ref,
    values_ref,
    attn_gain_grad_ref,
    down_grad_ref,
    gate_grad_ref,
    up_grad_ref,
    mlp_gain_grad_ref,
    lower_midway_grad_ref,
    out_grad_ref,
    lower_query_grad_ref,
    parts_ref,
    *scratch,
):
    own = Weights(wide_ref, None, 1, PROJECTION, scratch[:3])
    lower = Weights(wide_ref, down_ref, 0, REST, scratch[3:])
    turned, values, gain_grad, grad_in = project_back(
        query_grad_ref[...],
        key_grads_ref[...],
        midway_grad_ref[...],
        x_ref[...].astype(F32),
        gains_ref[1, 0:1],
        cos_ref[...],
        sin_ref[...],
        own,
    )
    turned_ref[...] = turned
    values_ref[...] = values
    attn_gain_grad_ref[...] = gain_grad
    attended = attended_ref[...]
    down_grad, gate_grad, up_grad, gain_grad, midway_grad, out_grad, mixed_grad = feed_forward_back(
        grad_in.astype(BF16).astype(F32),
        midway_ref[...],
        gate_ref[...],
        up_ref[...],
        gains_ref[0, 1:2],
        lower,
    )
    down_grad_ref[...] = down_grad
    gate_grad_ref[...] = gate_grad
    up_grad_ref[...] = up_grad
    mlp_gain_grad_ref[...] = gain_grad
    lower_midway_grad_ref[...] = midway_grad
    out_grad_ref[...] = out_grad
    lower_query_grad_ref[...] = attend_back(
        mixed_grad, attended, query_ref, keys_ref, probs_ref, parts_ref
    )


def grads_kernel(
    normed_ref,
    turned_ref,
    values_ref,
    attended_ref,
    out_grad_ref,
    normed_two_ref,
    gate_grad_ref,
    up_grad_ref,
    hidden_ref,
    down_grad_ref,
    attn_gain_grad_ref,
    mlp_gain_grad_ref,
    out_ref,
    lhs,
    hidden_t,
    stage,
):
    weight_grads(
        normed_ref[...],
        turned_ref[...],
        values_ref[...],
        attended_ref[...],
        out_grad_ref[...],
        normed_two_ref[...],
        gate_grad_ref[...],
        up_grad_ref[...],
        hidden_ref[...],
        down_grad_ref[...],
        attn_gain_grad_ref[...],
        mlp_gain_grad_ref[...],
        out_ref,
        lhs,
        hidden_t,
        stage,
    )


def end_kernel(
    key_grads_ref,
    query_grad_ref,
    midway_grad_ref,
    x_ref,
    gains_ref,
    cos_ref,
    sin_ref,
    wide_ref,
    grad_in_ref,
    turned_ref,
    values_ref,
    gain_grad_ref,
    *scratch,
):
    own = Weights(wide_ref, None, 0, PROJECTION, scratch)
    turned, values, gain_grad, grad_in = project_back(
        query_grad_ref[...],
        key_grads_ref[...],
        midway_grad_ref[...],
        x_ref[...].astype(F32),
        gains_ref[0, 0:1],
        cos_ref[...],
        sin_ref[...],
        own,
    )
    grad_in_ref[...] = grad_in
    turned_ref[...] = turned
    values_ref[...] = values
    gain_grad_ref[...] = gain_grad


def call(kernel, name, out_shape, *operands, scratch=(), specs=None):
    return pl.pallas_call(
        kernel,
        out_shape=out_shape,
        in_specs=[VMEM] * len(operands) if specs is None else specs,
        out_specs=jax.tree.map(lambda _: VMEM, out_shape),
        scratch_shapes=list(scratch),
        compiler_params=params(),
        name=name,
    )(*operands)


def rope_tables(first):
    places = first + jnp.arange(ROWS, dtype=jnp.int32)
    pair_index = jnp.arange(HEAD // 2).astype(F32)
    frequency = rope_base ** (-2.0 * pair_index / HEAD)
    angles = places.astype(F32)[:, None] * frequency[None, :]
    cos, sin = jnp.cos(angles), jnp.sin(angles)
    return jnp.concatenate([cos] * 4, axis=1), jnp.concatenate([-sin, sin] * 2, axis=1)


def local(block_input, cotangent, segment_ids, *shards):
    section = lax.axis_index("section")
    ctx = lax.axis_index("ctx")
    x = lax.dynamic_index_in_dim(block_input[:, 0], section, 0, keepdims=False)
    late = lax.dynamic_index_in_dim(cotangent[:, 0], section, 0, keepdims=False)
    seg_row = lax.dynamic_index_in_dim(segment_ids[:, 0], section, 0)
    own_seg = lax.dynamic_slice_in_dim(seg_row, ctx * ROWS, ROWS, 1).reshape(ROWS, 1)
    cos, sin = rope_tables(ctx * ROWS)

    gathered = gather_weights(pack_shards(shards))
    wide, down, gains = unpack_weights(gathered)

    whole = like((ROWS, D), F32)
    half = like((ROWS, D), BF16)
    keys_shape = like((ROWS, 2 * KVD), BF16)
    hidden_shape = like((ROWS, FF), BF16)
    acts = like((ROWS, FF), F32)
    probs_shape = (KV_HEADS, GROUP * ROWS, SEQ)
    turned_shape = like((ROWS, D + KVD), BF16)
    values_shape = like((ROWS, KVD), BF16)
    row_shape = like((1, D), F32)
    parts_shape = like((8, 2 * KVD, ROWS), BF16)

    first_part = weight_scratch(*PROJECTION)
    second_part = weight_scratch(*REST)

    normed_1, query_1, joined_1 = call(
        start_kernel,
        "start",
        (half, half, keys_shape),
        x,
        gains,
        wide,
        cos,
        sin,
        specs=[VMEM, VMEM, ANY, VMEM, VMEM],
        scratch=first_part,
    )
    keys_1 = gather_keys(joined_1, 2)
    (
        probs_1,
        attended_1,
        midway_1,
        normed_two_1,
        gate_1,
        up_1,
        hidden_1,
        x_2,
        normed_2,
        query_2,
        joined_2,
    ) = call(
        middle_kernel,
        "middle",
        (
            like(probs_shape, BF16),
            half,
            whole,
            half,
            acts,
            acts,
            hidden_shape,
            half,
            half,
            half,
            keys_shape,
        ),
        x,
        gains,
        wide,
        down,
        cos,
        sin,
        query_1,
        keys_1,
        own_seg,
        seg_row,
        specs=[VMEM] * 2 + [ANY] * 2 + [VMEM] * 6,
        scratch=second_part + first_part,
    )
    keys_2 = gather_keys(joined_2, 3)
    (
        result,
        attended_2,
        normed_two_2,
        hidden_2,
        gate_grad_2,
        up_grad_2,
        mlp_gain_grad_2,
        midway_grad_2,
        out_grad_2,
        query_grad_2,
        parts_2,
    ) = call(
        turn_kernel,
        "turn",
        (
            whole,
            half,
            half,
            hidden_shape,
            hidden_shape,
            hidden_shape,
            row_shape,
            whole,
            half,
            whole,
            parts_shape,
        ),
        x_2,
        late,
        gains,
        wide,
        down,
        query_2,
        keys_2,
        own_seg,
        seg_row,
        scratch=[pltpu.VMEM(probs_shape, BF16)] + second_part,
        specs=[VMEM] * 3 + [ANY] * 2 + [VMEM] * 4,
    )
    key_grads_2 = scatter_key_grads(parts_2, 4)
    (
        turned_2,
        values_2,
        attn_gain_grad_2,
        down_grad_1,
        gate_grad_1,
        up_grad_1,
        mlp_gain_grad_1,
        midway_grad_1,
        out_grad_1,
        query_grad_1,
        parts_1,
    ) = call(
        back_kernel,
        "back",
        (
            turned_shape,
            values_shape,
            row_shape,
            half,
            hidden_shape,
            hidden_shape,
            row_shape,
            whole,
            half,
            whole,
            parts_shape,
        ),
        key_grads_2,
        query_grad_2,
        midway_grad_2,
        x_2,
        gains,
        cos,
        sin,
        wide,
        down,
        midway_1,
        gate_1,
        up_1,
        attended_1,
        query_1,
        keys_1,
        probs_1,
        specs=[VMEM] * 7 + [ANY] * 2 + [VMEM] * 7,
        scratch=first_part + second_part,
    )
    grads_shape = like((64, PACKED, LANES), BF16)
    grads_2 = call(
        grads_kernel,
        "grads",
        grads_shape,
        normed_2,
        turned_2,
        values_2,
        attended_2,
        out_grad_2,
        normed_two_2,
        gate_grad_2,
        up_grad_2,
        hidden_2,
        late,
        attn_gain_grad_2,
        mlp_gain_grad_2,
        scratch=GRAD_SCRATCH,
    )
    key_grads_1 = scatter_key_grads(parts_1, 5)
    grad_in, turned_1, values_1, attn_gain_grad_1 = call(
        end_kernel,
        "end",
        (whole, turned_shape, values_shape, row_shape),
        key_grads_1,
        query_grad_1,
        midway_grad_1,
        x,
        gains,
        cos,
        sin,
        wide,
        specs=[VMEM] * 7 + [ANY],
        scratch=first_part,
    )
    grads_1 = call(
        grads_kernel,
        "grads",
        grads_shape,
        normed_1,
        turned_1,
        values_1,
        attended_1,
        out_grad_1,
        normed_two_1,
        gate_grad_1,
        up_grad_1,
        hidden_1,
        down_grad_1,
        attn_gain_grad_1,
        mlp_gain_grad_1,
        scratch=GRAD_SCRATCH,
    )
    by_device = (4, 2, 2, 4, PACKED, LANES)
    leaving = jnp.where(section == 0, result, grad_in)
    staying = jnp.where(section == 0, grad_in, result)
    packed, came = scatter_grads(
        grads_1.reshape(by_device), grads_2.reshape(by_device), leaving
    )
    return finish(packed, staying, came)


def solution(mesh):
    shard = P("section", ("ctx", "fsdp"))
    matrix = P("section", ("ctx", "fsdp"), None)
    return jax.shard_map(
        local,
        mesh=mesh,
        in_specs=(
            P(None, "fsdp", "ctx", None),
            P(None, "fsdp", "ctx", None),
            P(None, "fsdp", None),
            shard,
            matrix,
            matrix,
            matrix,
            matrix,
            matrix,
            matrix,
            matrix,
            shard,
        ),
        out_specs=(
            P("section", None, "fsdp", "ctx", None),
            shard,
            matrix,
            matrix,
            matrix,
            matrix,
            matrix,
            matrix,
            matrix,
            shard,
        ),
        check_vma=False,
    )
```

time: 1790 us -> 275 us (0.15)
  blocking collectives: 945 us -> 0 us
  waiting for transfers between devices: 596 us -> 0 us
  Pallas kernels: 0 us -> 256 us
  matrix products: 100 us -> 0 us
  local copies, waits for them, and re-layouts: 64.9 us -> 14.8 us
  other arithmetic: 40.4 us -> 2.04 us
  between operations: 19.3 us -> 0.82 us
    all_gather x10 -> x0, blocking collectives: 660 us -> none  [the longest x1 155 us: local(): lax.all_gather(w_out, ('ctx', 'fsdp'), axis=1, tiled=True)]
    unnamed x11 -> x0, waiting for transfers between devices: 470 us -> none
    unnamed x2 -> x0, blocking collectives: 286 us -> none
    pallas_call x0 -> x16, Pallas kernels: none -> 256 us  [the longest x7 61.5 us: call(): pl.pallas_call(kernel, out_shape=out_shape, in_specs=[VMEM] * len(operand...]
    reduce_scatter x6 -> x0, waiting for transfers between devices: 108 us -> none  [the longest x3 79.2 us: backward_layer(): lax.psum_scatter(value_part.reshape(seq_len, KV_HEADS * HEAD_DIM), 'ctx',...]
    dot_general x70 -> x0, matrix products: 100 us -> none  [the longest x21 30.3 us: product_back(): lax.dot_general(left, right, (((1,), (1,)), ((), ())), preferred_element_...]
    unnamed x376 -> x6, local copies, waits for them, and re-layouts: 35 us -> 0.02 us
    broadcast_in_dim x7 -> x0, local copies, waits for them, and re-layouts: 24.7 us -> none  [the longest x1 5.86 us: grad_terms(): row_contract(hidden, down_grad)[None]]
  transfers between devices with their start and end apart: 14 -> 0, of which waited for: 10 -> 0; matrix products, arithmetic and copies ran while one was open for 7% -> 0% of each run, Pallas kernels for 0% -> 0%
where the time goes in v1:
time: 275 us; the launch traced here: 274 us
  Pallas kernels  256 us (93%)
  local copies, waits for them, and re-layouts  14.8 us (5%)
    pallas_call x7, Pallas kernels, call(): pl.pallas_call(kernel, out_shape=out_shape, in_specs=[VMEM] * len(operand...  61.5 us
    pallas_call x1, Pallas kernels, scatter_grads(): pl.pallas_call(scatter_kernel, out_shape=(jax.ShapeDtypeStruct((PACKED, L...  60 us
    pallas_call x1, Pallas kernels, gather_weights(): pl.pallas_call(gather_kernel, out_shape=jax.ShapeDtypeStruct((2, 4, 2, 2,...  55.6 us
    pallas_call x2, Pallas kernels, scatter_key_grads(): pl.pallas_call(key_grads_kernel, out_shape=jax.ShapeDtypeStruct((2 * KVD,...  30.8 us
    pallas_call x2, Pallas kernels, gather_keys(): pl.pallas_call(keys_kernel, out_shape=jax.ShapeDtypeStruct((8, ROWS, 2 *...  28.7 us
    pallas_call x1, Pallas kernels, unpack_weights(): pl.pallas_call(unpack_kernel, grid=(2, 4), out_shape=(jax.ShapeDtypeStruc...  15.5 us
    pallas_call x7, local copies, waits for them, and re-layouts, finish(): pl.pallas_call(finish_kernel, out_shape=tuple((jax.ShapeDtypeStruct(shape...  10.7 us

profile of v1, /device:TPU:0, one launch (start us, length us, event | category | flops | bytes accessed | tf_op | source)
XLA Modules:
  0.0 273.6 jit_solution(4054097242999008941)
XLA Ops:
  0.6 0.0 copy-start
  0.7 1.0 constant_dynamic-slice_fusion
  1.7 0.8 copy.33
  2.5 1.6 pack_shards.1.mine_ref
  4.1 55.6 %gather_weights.1 = bf16[2,4,2,2,4,448,128]{6,5,4,3,2,1,0:T(8,128)(2,1)} custom-call(bf16[448,128]{1,0:T(8,128)(2,1)} %pack_shards.1.mine_ref), custom_call_target="tpu_custom_call" | custom-call | tf_op jit(solution)/shard_map/gather_weights/pallas_call | solution.py:199
  59.8 15.5 %unpack_weights.1 = (bf16[2,576,4608]{2,1,0:T(8,128)(2,1)}, bf16[2,1536,576]{2,1,0:T(8,128)(2,1)}, f32[2,8,576]{2,1,0:T(8,128)}) custom-call(bf16[128,448,128]{2,1,0:T(8,128)(2,1)} %bitcast.9), custom_call_target="tpu_custom_call" | custom-call | tf_op jit(solution)/shard_map/unpack_weights/pallas_call | solution.py:607
  75.3 0.3 fusion
  75.7 0.8 pad_maximum_fusion
  76.5 3.6 %start.1 = (bf16[128,576]{1,0:T(8,128)(2,1)}, bf16[128,576]{1,0:T(8,128)(2,1)}, bf16[128,384]{1,0:T(8,128)(2,1)}) custom-call(bf16[128,576]{1,0:T(8,128)(2,1)} %bitcast.12, f32[2,8,576]{2,1,0:T(8,128)} %get-tuple-element.55.gains_ref, bf16[2,576,4608]{2,1,0:T(8,128)(2,1)} %get-tuple-element.56.wide_ref, f32[128,128]{1,0:T(8,128)} %get-tuple-element.127.cos_ref, ...), custom_call_target="tpu_custom_call" | custom-call | tf_op jit(solution)/shard_map/start/pallas_call | solution.py:1191
  80.1 14.4 %gather_keys.2.keys_ref = bf16[8,128,384]{2,1,0:T(8,128)(2,1)} custom-call(bf16[128,384]{1,0:T(8,128)(2,1)} %get-tuple-element.60.mine_ref), custom_call_target="tpu_custom_call" | custom-call | tf_op jit(solution)/shard_map/gather_keys/pallas_call | solution.py:462
  94.4 0.0 copy-done
  94.5 0.1 fusion.1
  94.5 0.7 copy.35.own_seg_ref
  95.3 0.6 dynamic-slice_bitcast_fusion.seg_ref
  95.9 9.4 %middle.1 = (bf16[3,384,1024]{2,1,0:T(8,128)(2,1)}, bf16[128,576]{1,0:T(8,128)(2,1)}, f32[128,576]{1,0:T(8,128)}, bf16[128,576]{1,0:T(8,128)(2,1)}, f32[128,1536...) custom-call(bf16[128,576]{1,0:T(8,128)(2,1)} %bitcast.13, ...), custom_call_target="tpu_custom_call" | custom-call | tf_op jit(solution)/shard_map/middle/pallas_call | solution.py:1191
  105.3 0.8 copy.36
  106.1 14.3 %gather_keys.3.keys_ref = bf16[8,128,384]{2,1,0:T(8,128)(2,1)} custom-call(bf16[128,384]{1,0:T(8,128)(2,1)} %get-tuple-element.63.mine_ref), custom_call_target="tpu_custom_call" | custom-call | tf_op jit(solution)/shard_map/gather_keys/pallas_call | solution.py:462
  120.4 12.3 %turn.1 = (f32[128,576]{1,0:T(8,128)}, bf16[128,576]{1,0:T(8,128)(2,1)}, bf16[128,576]{1,0:T(8,128)(2,1)}, bf16[128,1536]{1,0:T(8,128)(2,1)}, bf16[128,1536]{1,0...) custom-call(bf16[128,576]{1,0:T(8,128)(2,1)} %get-tuple-element.61.x, ...), custom_call_target="tpu_custom_call" | custom-call | tf_op jit(solution)/shard_map/turn/pallas_call | solution.py:1191
  132.7 15.7 %scatter_key_grads.2.key_grads_ref = f32[384,128]{1,0:T(8,128)} custom-call(bf16[8,384,128]{2,1,0:T(8,128)(2,1)} %get-tuple-element.64.parts_ref), custom_call_target="tpu_custom_call" | custom-call | tf_op jit(solution)/shard_map/scatter_key_grads/pallas_call | solution.py:509
  148.4 13.6 %back.1 = (bf16[128,768]{1,0:T(8,128)(2,1)}, bf16[128,192]{1,0:T(8,128)(2,1)}, f32[1,576]{1,0:T(1,128)}, bf16[128,576]{1,0:T(8,128)(2,1)}, bf16[128,1536]{1,0:T(...) custom-call(f32[384,128]{1,0:T(8,128)} %scatter_key_grads.2.key_grad, ...), custom_call_target="tpu_custom_call" | custom-call | tf_op jit(solution)/shard_map/back/pallas_call | solution.py:1191
  162.0 15.0 %scatter_key_grads.3.key_grads_ref = f32[384,128]{1,0:T(8,128)} custom-call(bf16[8,384,128]{2,1,0:T(8,128)(2,1)} %get-tuple-element.72.parts_ref), custom_call_target="tpu_custom_call" | custom-call | tf_op jit(solution)/shard_map/scatter_key_grads/pallas_call | solution.py:509
  177.0 3.8 %end.1 = (f32[128,576]{1,0:T(8,128)}, bf16[128,768]{1,0:T(8,128)(2,1)}, bf16[128,192]{1,0:T(8,128)(2,1)}, f32[1,576]{1,0:T(1,128)}) custom-call(f32[384,128]{1,0:T(8,128)} %scatter_key_grads.3.key_grads_ref, f32[128,576]{1,0:T(8,128)} %get-tuple-element.73.query_grad_ref, f32[128,576]{1,0:T(8,128)} %get-tuple-element.74.midway_grad_ref, ...), custom_call_target="tpu_custom_call" | custom-call | tf_op jit(solution)/shard_map/end/pallas_call | solution.py:1191
  180.9 0.0 copy-start.1
  180.9 0.0 copy-start.2
  180.9 9.4 %grads.2 = bf16[64,448,128]{2,1,0:T(8,128)(2,1)} custom-call(bf16[128,576]{1,0:T(8,128)(2,1)} %get-tuple-element.57.normed_ref, bf16[128,768]{1,0:T(8,128)(2,1)} %get-tuple-element.75.turned_ref, bf16[128,192]{1,0:T(8,128)(2,1)} %get-tuple-element.76.values_ref, bf16[128,576]{1,0:T(8,128)(2,1)} %get-tuple-element.70.attended_ref, ...), custom_call_target="tpu_custom_call" | custom-call | tf_op jit(solution)/shard_map/grads/pallas_call | solution.py:1191
  190.3 9.4 %grads.3 = bf16[64,448,128]{2,1,0:T(8,128)(2,1)} custom-call(bf16[128,576]{1,0:T(8,128)(2,1)} %get-tuple-element.85.normed_ref, bf16[128,768]{1,0:T(8,128)(2,1)} %get-tuple-element.86.turned_ref, bf16[128,192]{1,0:T(8,128)(2,1)} %get-tuple-element.87.values_ref, bf16[128,576]{1,0:T(8,128)(2,1)} %get-tuple-element.88.attended_ref, ...), custom_call_target="tpu_custom_call" | custom-call | tf_op jit(solution)/shard_map/grads/pallas_call | solution.py:1191
  199.8 0.0 copy-done.1
  199.8 0.0 copy-done.2
  199.8 0.9 broadcast_select_fusion
  200.7 60.0 %scatter_grads.1 = (f32[448,128]{1,0:T(8,128)}, f32[128,576]{1,0:T(8,128)}) custom-call(bf16[4,2,2,4,448,128]{5,4,3,2,1,0:T(8,128)(2,1)} %bitcast.10, bf16[4,2,2,4,448,128]{5,4,3,2,1,0:T(8,128)(2,1)} %bitcast.11, f32[128,576]{1,0:T(8,128)} %get-tuple-element.121.edge_ref), custom_call_target="tpu_custom_call" | custom-call | tf_op jit(solution)/shard_map/scatter_grads/pallas_call | solution.py:386
  260.7 2.2 finish.1
  262.9 2.1 copy.38
  265.0 1.4 copy.39
  266.4 1.3 copy.40
  267.7 1.3 copy.41
  269.1 1.4 copy.42
  270.5 1.6 copy.43
  272.0 1.6 copy.44
  (2 shorter events, 0.0 us)
Async XLA Ops:
  0.6 93.8 %copy-start = (s32[2,1,1024]{2,1,0:T(1,128)S(1)}, s32[2,1,1024]{2,1,0:T(1,128)}, u32[]{:S(2)}) copy-start(s32[2,1,1024]{2,1,0:T(1,128)} %param.14) | copy-start | bytes 24580
  180.9 18.9 %copy-start.1 = (f32[128,576]{1,0:T(8,128)S(1)}, f32[128,576]{1,0:T(8,128)}, u32[]{:S(2)}) copy-start(f32[128,576]{1,0:T(8,128)} %get-tuple-element.96) | copy-start | bytes 884740
  180.9 18.9 %copy-start.2 = (f32[128,576]{1,0:T(8,128)S(1)}, f32[128,576]{1,0:T(8,128)}, u32[]{:S(2)}) copy-start(f32[128,576]{1,0:T(8,128)} %get-tuple-element.97) | copy-start | bytes 884740

commit v2 on v1

--- a/solution.py
+++ b/solution.py
@@ -387,7 +387,7 @@
         scatter_kernel,
         out_shape=(
             jax.ShapeDtypeStruct((PACKED, LANES), F32),
-            jax.ShapeDtypeStruct((ROWS, D), F32),
+            jax.ShapeDtypeStruct((D, ROWS), F32),
         ),
         in_specs=[ANY, ANY, VMEM],
         out_specs=(VMEM, VMEM),
@@ -410,115 +410,131 @@
     )(first, second, edge)
 
 
-def ctx_device(index):
-    return (lax.axis_index("section"), index, lax.axis_index("fsdp"))
-
-
-def greet_ctx(mine):
-    greet([ctx_device(lax.rem(mine + away, 8)) for away in range(1, 8)])
-
-
-def keys_kernel(mine_ref, out_ref, send_sems, recv_sems):
-    mine = lax.axis_index("ctx")
-    greet_ctx(mine)
-
-    def copy_to(away):
+class Exchange:
+    def __init__(self, place, send_sems, recv_sems):
+        self.place = place
+        self.send_sems = send_sems
+        self.recv_sems = recv_sems
+
+    def copy(self, slot, source, target, device):
         return pltpu.make_async_remote_copy(
-            src_ref=mine_ref,
-            dst_ref=out_ref.at[mine],
-            send_sem=send_sems.at[away],
-            recv_sem=recv_sems.at[away],
-            device_id=ctx_device(lax.rem(mine + away, 8)),
+            src_ref=source,
+            dst_ref=target,
+            send_sem=self.send_sems.at[slot],
+            recv_sem=self.recv_sems.at[slot],
+            device_id=device,
             device_id_type=MESH,
         )
 
-    for away in range(1, 8):
-
-        @pl.when(mine + away < 8)
-        def _():
-            copy_to(away).start()
-
-    out_ref[mine] = mine_ref[...]
-    for away in range(1, 8):
-
-        @pl.when(mine + away < 8)
-        def _():
-            out_ref[mine + away] = jnp.zeros(out_ref.shape[1:], out_ref.dtype)
-
-    for away in range(1, 8):
-
-        @pl.when(mine - away >= 0)
-        def _():
-            copy_to(away).wait_recv()
-
-    for away in range(1, 8):
-
-        @pl.when(mine + away < 8)
-        def _():
-            copy_to(away).wait_send()
-
-
-def gather_keys(joined, collective_id):
-    return pl.pallas_call(
-        keys_kernel,
-        out_shape=jax.ShapeDtypeStruct((8, ROWS, 2 * KVD), BF16),
-        in_specs=[VMEM],
-        out_specs=VMEM,
-        scratch_shapes=[pltpu.SemaphoreType.DMA((8,)), pltpu.SemaphoreType.DMA((8,))],
-        compiler_params=params(collective_id),
-        name="gather_keys",
-    )(joined)
-
-
-def key_grads_kernel(parts_ref, out_ref, arrived, send_sems, recv_sems):
-    mine = lax.axis_index("ctx")
-    greet_ctx(mine)
-
-    def copy_to(away):
-        return pltpu.make_async_remote_copy(
-            src_ref=parts_ref.at[lax.rem(mine - away + 8, 8)],
-            dst_ref=arrived.at[away],
-            send_sem=send_sems.at[away],
-            recv_sem=recv_sems.at[away],
-            device_id=ctx_device(lax.rem(mine - away + 8, 8)),
-            device_id_type=MESH,
-        )
-
-    for away in range(1, 8):
-
-        @pl.when(mine - away >= 0)
-        def _():
-            copy_to(away).start()
-
-    out_ref[...] = parts_ref[mine].astype(F32)
-    for away in range(1, 8):
-
-        @pl.when(mine + away < 8)
-        def _():
-            copy_to(away).wait_recv()
-            out_ref[...] += arrived[away].astype(F32)
-
-    for away in range(1, 8):
-
-        @pl.when(mine - away >= 0)
-        def _():
-            copy_to(away).wait_send()
-
-
-def scatter_key_grads(parts, collective_id):
-    return pl.pallas_call(
-        key_grads_kernel,
-        out_shape=jax.ShapeDtypeStruct((2 * KVD, ROWS), F32),
-        in_specs=[VMEM],
-        out_specs=VMEM,
-        scratch_shapes=[
-            pltpu.VMEM((8, 2 * KVD, ROWS), BF16),
-            pltpu.SemaphoreType.DMA((8,)),
-            pltpu.SemaphoreType.DMA((8,)),
-        ],
-        compiler_params=params(collective_id),
-        name="scatter_key_grads",
-    )(parts)
+    def along_y(self, step):
+        return self.place.device(y=lax.rem(self.place.at["y"] + step + 4, 4))
+
+
+class KeyGather(Exchange):
+    def __init__(self, place, keys_ref, send_sems, recv_sems):
+        super().__init__(place, send_sems, recv_sems)
+        self.keys_ref = keys_ref
+
+    def direct(self, away):
+        own = self.keys_ref.at[self.place.at["y"] * 2 + self.place.core]
+        return self.copy(away, own, own, self.along_y(away))
+
+    def passed_on(self, away):
+        block = self.keys_ref.at[
+            lax.rem(self.place.at["y"] - away + 4, 4) * 2 + self.place.core
+        ]
+        return self.copy(4 + away, block, block, self.place.partner())
+
+    def start(self):
+        y = self.place.at["y"]
+        for away in (1, 3, 2):
+
+            @pl.when(y + away < 4)
+            def _():
+                self.direct(away).start()
+
+        self.passed_on(0).start()
+        for away in range(1, 4):
+
+            @pl.when(y + away < 4)
+            def _():
+                self.keys_ref[pl.ds((y + away) * 2, 2)] = jnp.zeros(
+                    (2,) + self.keys_ref.shape[1:], self.keys_ref.dtype
+                )
+
+    def finish(self):
+        y = self.place.at["y"]
+        for away in range(1, 4):
+
+            @pl.when(y - away >= 0)
+            def _():
+                self.direct(away).wait_recv()
+                self.passed_on(away).start()
+
+        self.passed_on(0).wait()
+        for away in range(1, 4):
+
+            @pl.when(y - away >= 0)
+            def _():
+                self.passed_on(away).wait()
+
+            @pl.when(y + away < 4)
+            def _():
+                self.direct(away).wait_send()
+
+
+class KeyGradSum(Exchange):
+    def __init__(self, place, parts_ref, pair_ref, ring_ref, send_sems, recv_sems):
+        super().__init__(place, send_sems, recv_sems)
+        self.parts_ref = parts_ref
+        self.pair_ref = pair_ref
+        self.ring_ref = ring_ref
+
+    def swap(self):
+        return self.copy(
+            0, self.parts_ref.at[1 - self.place.core], self.pair_ref, self.place.partner()
+        )
+
+    def direct(self, away):
+        y = lax.rem(self.place.at["y"] - away + 4, 4)
+        return self.copy(
+            away,
+            self.parts_ref.at[self.place.core, y],
+            self.ring_ref.at[away],
+            self.along_y(-away),
+        )
+
+    def start(self):
+        self.swap().start()
+
+    def middle(self):
+        self.swap().wait()
+        core = self.place.core
+        for y in range(4):
+            self.parts_ref[core, y] = (
+                self.parts_ref[core, y].astype(F32) + self.pair_ref[y].astype(F32)
+            ).astype(BF16)
+        for away in (1, 3, 2):
+
+            @pl.when(self.place.at["y"] - away >= 0)
+            def _():
+                self.direct(away).start()
+
+    def finish(self, out_ref):
+        y = self.place.at["y"]
+        out_ref[...] = self.parts_ref[self.place.core, y].astype(F32)
+        for away in range(1, 4):
+
+            @pl.when(y + away < 4)
+            def _():
+                self.direct(away).wait_recv()
+                out_ref[...] += self.ring_ref[away].astype(F32)
+
+        for away in range(1, 4):
+
+            @pl.when(y - away >= 0)
+            def _():
+                self.direct(away).wait_send()
 
 
 def pack_kernel(
@@ -645,12 +661,12 @@
     joined = jnp.concatenate(
         [packed[WIDE_ROW + 9 * i : WIDE_ROW + 9 * i + 9] for i in range(BLOCKS)], axis=1
     )
-    query_ref[0] = joined[:, :D]
-    key_ref[0] = joined[:, D:GATE_AT]
-    gate_ref[0] = joined[:, GATE_AT:UP_AT]
-    up_ref[0] = joined[:, UP_AT:OUT_AT]
-    w_out_ref[0] = joined[:, OUT_AT:VALUE_AT]
-    value_ref[0] = joined[:, VALUE_AT:]
+    query_ref[:, 0] = joined[:, :D]
+    key_ref[:, 0] = joined[:, D:GATE_AT]
+    gate_ref[:, 0] = joined[:, GATE_AT:UP_AT]
+    up_ref[:, 0] = joined[:, UP_AT:OUT_AT]
+    w_out_ref[:, 0] = joined[:, OUT_AT:VALUE_AT]
+    value_ref[:, 0] = joined[:, VALUE_AT:]
     tail = packed[TAIL_ROW:WIDE_ROW]
     down_ref[0] = jnp.concatenate(
         [packed[DOWN_ROWS * i : DOWN_ROWS * (i + 1)] for i in range(4)]
@@ -663,18 +679,18 @@
 
 def finish(packed, kept, came):
     shapes = (
-        (1, 2, 1, ROWS, D),
+        (1, 2, 1, D, ROWS),
         (1, 9),
-        (1, 9, D),
-        (1, 9, KVD),
-        (1, 9, KVD),
-        (1, 9, D),
-        (1, 9, FF),
-        (1, 9, FF),
+        (9, 1, D),
+        (9, 1, KVD),
+        (9, 1, KVD),
+        (9, 1, D),
+        (9, 1, FF),
+        (9, 1, FF),
         (1, DOWN_ROWS, D),
         (1, 9),
     )
-    return pl.pallas_call(
+    edges, attn, *wide, down, mlp = pl.pallas_call(
         finish_kernel,
         out_shape=tuple(jax.ShapeDtypeStruct(shape, F32) for shape in shapes),
         in_specs=[VMEM] * 3,
@@ -682,6 +698,8 @@
         compiler_params=params(),
         name="finish",
     )(packed, kept, came)
+    wide = [grad.transpose(1, 0, 2) for grad in wide]
+    return (edges.transpose(0, 1, 2, 4, 3), attn, *wide, down, mlp)
 
 
 def swap_halves(block):
@@ -697,7 +715,7 @@
     return block * cos + swap_halves(block) * sin
 
 
-def project(current, gain, weights, cos, sin, normed_ref, query_ref, joined_ref):
+def project(current, gain, weights, cos, sin, normed_ref, query_ref):
     scale = lax.rsqrt(jnp.mean(current * current, axis=1, keepdims=True) + norm_eps)
     normed = (current * scale * gain).astype(BF16)
     normed_ref[...] = normed
@@ -709,7 +727,7 @@
         query_ref[:, i * LANES : (i + 1) * LANES] = turned[i]
     query_ref[:, 4 * LANES :] = turned[4][:, :HEAD]
     values = dot(normed, weights.get("tail"))[:, HEAD:]
-    joined_ref[...] = jnp.concatenate(
+    return jnp.concatenate(
         [turned[4][:, HEAD:].astype(F32), turned[5].astype(F32), values], axis=1
     ).astype(BF16)
 
@@ -794,8 +812,9 @@
         value_part = dot_tn(grads, probs).astype(BF16)
         for block in range(8):
             columns = slice(block * ROWS, (block + 1) * ROWS)
-            parts_ref[block, group * HEAD : (group + 1) * HEAD] = key_part[:, columns]
-            parts_ref[block, KVD + group * HEAD : KVD + (group + 1) * HEAD] = value_part[:, columns]
+            at = (block % 2, block // 2)
+            parts_ref[*at, group * HEAD : (group + 1) * HEAD] = key_part[:, columns]
+            parts_ref[*at, KVD + group * HEAD : KVD + (group + 1) * HEAD] = value_part[:, columns]
     return jnp.concatenate(query_grads, axis=1)
 
 
@@ -821,77 +840,80 @@
 GRAD_DEVICES = 16
 
 
-def weight_grads(
-    normed,
-    turned,
-    values,
-    attended,
-    out_grad,
-    normed_two,
-    gate_grad,
-    up_grad,
-    hidden,
-    down_grad,
-    attn_gain_grad,
-    mlp_gain_grad,
-    out_ref,
-    lhs_ref,
-    hidden_ref,
-    stage,
-):
-    lhs_ref[0] = normed.astype(F32).T.astype(BF16)
-    lhs_ref[1] = normed_two.astype(F32).T.astype(BF16)
-    lhs_ref[2] = attended.astype(F32).T.astype(BF16)
-    hidden_ref[...] = hidden.astype(F32).T.astype(BF16)
-    count = GRAD_DEVICES
-
-    def body(step, carry):
-        rows = pl.ds(pl.multiple_of(step * 9 * count, 16), 9 * count)
-
-        def place_wide(column, product):
-            for i in range(product.shape[1] // LANES):
-                at = WIDE_ROW + 9 * (column + i)
-                part = product[:, i * LANES : (i + 1) * LANES]
-                for d in range(count):
-                    stage[d, at : at + 9] = part[9 * d : 9 * d + 9]
-
-        first = lhs_ref[0, rows]
-        place_wide(0, dot(first, turned))
-        second = lhs_ref[1, rows]
-        place_wide(GATE_AT // LANES, dot(second, gate_grad))
-        place_wide(UP_AT // LANES, dot(second, up_grad))
-        place_wide(
-            OUT_AT // LANES,
-            jnp.concatenate([dot(lhs_ref[2, rows], out_grad), dot(first, values)], axis=1),
-        )
-        down_rows = pl.ds(pl.multiple_of(step * DOWN_ROWS * count, 16), DOWN_ROWS * count)
-        down = dot(hidden_ref[down_rows], down_grad)
+def transposed(rows):
+    return rows.astype(F32).T.astype(BF16)
+
+
+class WeightGrads:
+    def __init__(self, stage, lhs, hidden_lhs):
+        self.stage = stage
+        self.lhs = lhs
+        self.hidden_lhs = hidden_lhs
+
+    def place(self, step, column, product):
+        for i in range(product.shape[1] // LANES):
+            at = WIDE_ROW + 9 * (column + i)
+            part = product[:, i * LANES : (i + 1) * LANES]
+            for d in range(GRAD_DEVICES):
+                self.stage[step * GRAD_DEVICES + d, at : at + 9] = part[9 * d : 9 * d + 9]
+
+    def prepare(self, normed, normed_two, attended, hidden):
+        self.lhs[0] = transposed(normed)
+        self.lhs[1] = transposed(normed_two)
+        self.lhs[2] = transposed(attended)
+        self.hidden_lhs[...] = transposed(hidden)
+
+    def rows(self, step, each):
+        return pl.ds(pl.multiple_of(step * each * GRAD_DEVICES, 16), each * GRAD_DEVICES)
+
+    def rest(self, gate_grad_ref, up_grad_ref, down_grad_ref):
         half = DOWN_ROWS // 2
-        for d in range(count):
-            own = down[DOWN_ROWS * d : DOWN_ROWS * (d + 1)]
-            for i in range(4):
-                stage[d, DOWN_ROWS * i : DOWN_ROWS * (i + 1)] = own[:, i * LANES : (i + 1) * LANES]
-            stage[d, TAIL_ROW:WIDE_ROW] = jnp.concatenate(
-                [own[:half, 4 * LANES :], own[half:, 4 * LANES :]], axis=1
+
+        def body(step, carry):
+            second = self.lhs[1, self.rows(step, 9)]
+            self.place(step, GATE_AT // LANES, dot(second, gate_grad_ref[...]))
+            self.place(step, UP_AT // LANES, dot(second, up_grad_ref[...]))
+            down = dot(self.hidden_lhs[self.rows(step, DOWN_ROWS)], down_grad_ref[...])
+            for d in range(GRAD_DEVICES):
+                own = down[DOWN_ROWS * d : DOWN_ROWS * (d + 1)]
+                at = step * GRAD_DEVICES + d
+                for i in range(4):
+                    self.stage[at, DOWN_ROWS * i : DOWN_ROWS * (i + 1)] = own[
+                        :, i * LANES : (i + 1) * LANES
+                    ]
+                self.stage[at, TAIL_ROW:WIDE_ROW] = jnp.concatenate(
+                    [own[:half, 4 * LANES :], own[half:, 4 * LANES :]], axis=1
+                )
+            return carry
+
+        lax.fori_loop(0, 64 // GRAD_DEVICES, body, 0)
+
+    def projections(self, turned_ref, values_ref, out_grad_ref):
+        def body(step, carry):
+            first = self.lhs[0, self.rows(step, 9)]
+            self.place(step, 0, dot(first, turned_ref[...]))
+            third = self.lhs[2, self.rows(step, 9)]
+            self.place(
+                step,
+                OUT_AT // LANES,
+                jnp.concatenate(
+                    [dot(third, out_grad_ref[...]), dot(first, values_ref[...])], axis=1
+                ),
             )
-        out_ref[pl.ds(step * count, count), :GAIN_ROW] = stage[...].astype(BF16)
-        return carry
-
-    lax.fori_loop(0, 64 // count, body, 0)
-
-    shape = (64 * 16, D)
-    row = lax.broadcasted_iota(jnp.int32, shape, 0)
-    first, second = gain_masks(0, 64, 16)
-    chosen = jnp.where(first, attn_gain_grad, 0.0) + jnp.where(second, mlp_gain_grad, 0.0)
-    gathered = dot_nt(chosen.astype(BF16), lane_spread())
-    out_ref[:, GAIN_ROW:] = gathered.astype(BF16).reshape(64, 16, LANES)
-
-
-GRAD_SCRATCH = [
-    pltpu.VMEM((3, D, ROWS), BF16),
-    pltpu.VMEM((FF, ROWS), BF16),
-    pltpu.VMEM((GRAD_DEVICES, GAIN_ROW, LANES), F32),
-]
+            return carry
+
+        lax.fori_loop(0, 64 // GRAD_DEVICES, body, 0)
+
+    def round(self, packed, attn_gain_grad, mlp_gain_grad):
+        def body(step, carry):
+            packed[step, :GAIN_ROW] = self.stage[step].astype(BF16)
+            return carry
+
+        lax.fori_loop(0, 64, body, 0)
+        first, second = gain_masks(0, 64, 16)
+        chosen = jnp.where(first, attn_gain_grad, 0.0) + jnp.where(second, mlp_gain_grad, 0.0)
+        gathered = dot_nt(chosen.astype(BF16), lane_spread())
+        packed[:, GAIN_ROW:] = gathered.astype(BF16).reshape(64, 16, LANES)
 
 
 COLUMNS = {
@@ -933,270 +955,231 @@
         return self.get("out")[:, :D]
 
 
-def like(shape, dtype):
-    return jax.ShapeDtypeStruct(shape, dtype)
-
-
-def start_kernel(
-    x_ref, gains_ref, wide_ref, cos_ref, sin_ref, normed_ref, query_ref, joined_ref, *scratch
-):
-    project(
-        x_ref[...].astype(F32),
-        gains_ref[0, 0:1],
-        Weights(wide_ref, None, 0, PROJECTION, scratch),
-        cos_ref[...],
-        sin_ref[...],
-        normed_ref,
-        query_ref,
-        joined_ref,
-    )
-
-
-def middle_kernel(
+ROW = (ROWS, D)
+KEPT = {
+    "joined": ((2, 8, ROWS, 2 * KVD), BF16),
+    "probs": ((2, KV_HEADS, GROUP * ROWS, SEQ), BF16),
+    "parts": ((2, 2, 4, 2 * KVD, ROWS), BF16),
+    "pair": ((2, 4, 2 * KVD, ROWS), BF16),
+    "ring": ((2, 4, 2 * KVD, ROWS), BF16),
+    "key_grads": ((2 * KVD, ROWS), F32),
+    "normed": ((2, *ROW), BF16),
+    "query": ((2, *ROW), BF16),
+    "attended": ((2, *ROW), BF16),
+    "normed_two": ((2, *ROW), BF16),
+    "hidden": ((2, ROWS, FF), BF16),
+    "midway": (ROW, F32),
+    "gate": ((ROWS, FF), F32),
+    "up": ((ROWS, FF), F32),
+    "x_2": (ROW, BF16),
+    "gate_grad": ((2, ROWS, FF), BF16),
+    "up_grad": ((2, ROWS, FF), BF16),
+    "down_grad": ((2, *ROW), BF16),
+    "out_grad": ((2, *ROW), BF16),
+    "midway_grad": (ROW, F32),
+    "query_grad": (ROW, F32),
+    "turned": ((2, ROWS, D + KVD), BF16),
+    "values": ((2, ROWS, KVD), BF16),
+    "lhs": ((2, 3, D, ROWS), BF16),
+    "hidden_lhs": ((2, FF, ROWS), BF16),
+    "stage": ((64, GAIN_ROW, LANES), F32),
+    "packed": ((64, PACKED, LANES), BF16),
+}
+
+
+def layers_kernel(
     x_ref,
+    late_ref,
     gains_ref,
     wide_ref,
     down_ref,
     cos_ref,
     sin_ref,
-    query_ref,
-    keys_ref,
-    own_seg_ref,
-    seg_ref,
-    probs_ref,
-    attended_ref,
-    midway_ref,
-    normed_two_ref,
-    gate_ref,
-    up_ref,
-    hidden_ref,
-    next_x_ref,
-    normed_ref,
-    next_query_ref,
-    joined_ref,
-    *scratch,
-):
-    own = Weights(wide_ref, down_ref, 0, REST, scratch[:5])
-    later = Weights(wide_ref, None, 1, PROJECTION, scratch[5:])
-    attended = attend(query_ref, keys_ref, own_seg_ref, seg_ref, probs_ref)
-    attended_ref[...] = attended
-    midway, scale, normed_two, gate, up, hidden, result = feed_forward(
-        x_ref[...].astype(F32), attended, gains_ref[0, 1:2], own
-    )
-    midway_ref[...] = midway
-    normed_two_ref[...] = normed_two
-    gate_ref[...] = gate
-    up_ref[...] = up
-    hidden_ref[...] = hidden
-    passed = result.astype(BF16)
-    next_x_ref[...] = passed
-    project(
-        passed.astype(F32),
-        gains_ref[1, 0:1],
-        later,
-        cos_ref[...],
-        sin_ref[...],
-        normed_ref,
-        next_query_ref,
-        joined_ref,
-    )
-
-
-def turn_kernel(
-    x_ref,
-    cotangent_ref,
-    gains_ref,
-    wide_ref,
-    down_ref,
-    query_ref,
-    keys_ref,
     own_seg_ref,
     seg_ref,
     result_ref,
-    attended_ref,
-    normed_two_ref,
-    hidden_ref,
-    gate_grad_ref,
-    up_grad_ref,
-    gain_grad_ref,
-    midway_grad_ref,
-    out_grad_ref,
-    query_grad_ref,
-    parts_ref,
-    probs,
+    grad_in_ref,
+    grads_1_ref,
+    grads_2_ref,
+    send_sems,
+    recv_sems,
+    out_sems,
     *scratch,
 ):
-    own = Weights(wide_ref, down_ref, 1, REST, scratch)
-    attended = attend(query_ref, keys_ref, own_seg_ref, seg_ref, probs)
-    attended_ref[...] = attended
-    gain = gains_ref[1, 1:2]
-    midway, scale, normed_two, gate, up, hidden, result = feed_forward(
-        x_ref[...].astype(F32), attended, gain, own
-    )
-    result_ref[...] = result
-    normed_two_ref[...] = normed_two
-    hidden_ref[...] = hidden
-    down_grad, gate_grad, up_grad, gain_grad, midway_grad, out_grad, mixed_grad = feed_forward_back(
-        cotangent_ref[...].astype(F32),
-        midway,
-        gate,
-        up,
-        gain,
-        own,
-    )
-    gate_grad_ref[...] = gate_grad
-    up_grad_ref[...] = up_grad
-    gain_grad_ref[...] = gain_grad
-    midway_grad_ref[...] = midway_grad
-    out_grad_ref[...] = out_grad
-    query_grad_ref[...] = attend_back(mixed_grad, attended, query_ref, keys_ref, probs, parts_ref)
-
-
-def back_kernel(
-    key_grads_ref,
-    query_grad_ref,
-    midway_grad_ref,
-    x_ref,
-    gains_ref,
-    cos_ref,
-    sin_ref,
-    wide_ref,
-    down_ref,
-    midway_ref,
-    gate_ref,
-    up_ref,
-    attended_ref,
-    query_ref,
-    keys_ref,
-    probs_ref,
-    turned_ref,
-    values_ref,
-    attn_gain_grad_ref,
-    down_grad_ref,
-    gate_grad_ref,
-    up_grad_ref,
-    mlp_gain_grad_ref,
-    lower_midway_grad_ref,
-    out_grad_ref,
-    lower_query_grad_ref,
-    parts_ref,
-    *scratch,
-):
-    own = Weights(wide_ref, None, 1, PROJECTION, scratch[:3])
-    lower = Weights(wide_ref, down_ref, 0, REST, scratch[3:])
-    turned, values, gain_grad, grad_in = project_back(
-        query_grad_ref[...],
-        key_grads_ref[...],
-        midway_grad_ref[...],
-        x_ref[...].astype(F32),
-        gains_ref[1, 0:1],
-        cos_ref[...],
-        sin_ref[...],
-        own,
-    )
-    turned_ref[...] = turned
-    values_ref[...] = values
-    attn_gain_grad_ref[...] = gain_grad
-    attended = attended_ref[...]
-    down_grad, gate_grad, up_grad, gain_grad, midway_grad, out_grad, mixed_grad = feed_forward_back(
+    place = Place()
+    kept = dict(zip(KEPT, scratch))
+    scratch = scratch[len(KEPT) :]
+    first_1 = Weights(wide_ref, None, 0, PROJECTION, scratch[:3])
+    rest_1 = Weights(wide_ref, down_ref, 0, REST, scratch[3:8])
+    first_2 = Weights(wide_ref, None, 1, PROJECTION, scratch[8:11])
+    rest_2 = Weights(wide_ref, down_ref, 1, REST, scratch[11:])
+    greet([place.partner()] + [place.device(y=place.shifted("y", step)) for step in (1, 2, 3)])
+
+    cos, sin = cos_ref[...], sin_ref[...]
+    mine = lax.axis_index("ctx")
+    gathers = [
+        KeyGather(place, kept["joined"].at[i], send_sems.at[i], recv_sems.at[i]) for i in range(2)
+    ]
+    sums = [
+        KeyGradSum(
+            place,
+            kept["parts"].at[i],
+            kept["pair"].at[i],
+            kept["ring"].at[i],
+            send_sems.at[2 + i],
+            recv_sems.at[2 + i],
+        )
+        for i in range(2)
+    ]
+    grads = [
+        WeightGrads(kept["stage"], kept["lhs"].at[i], kept["hidden_lhs"].at[i]) for i in range(2)
+    ]
+
+    def start_layer(layer, current, weights):
+        kept["joined"][layer, mine] = project(
+            current,
+            gains_ref[layer, 0:1],
+            weights,
+            cos,
+            sin,
+            kept["normed"].at[layer],
+            kept["query"].at[layer],
+        )
+        gathers[layer].start()
+
+    def rest_of_layer(layer, current, weights):
+        gathers[layer].finish()
+        attended = attend(
+            kept["query"].at[layer],
+            kept["joined"].at[layer],
+            own_seg_ref,
+            seg_ref,
+            kept["probs"].at[layer],
+        )
+        kept["attended"][layer] = attended
+        midway, scale, normed_two, gate, up, hidden, result = feed_forward(
+            current, attended, gains_ref[layer, 1:2], weights
+        )
+        kept["normed_two"][layer] = normed_two
+        kept["hidden"][layer] = hidden
+        return midway, gate, up, result
+
+    def back_of_layer(layer, incoming, midway, gate, up, weights):
+        down_grad, gate_grad, up_grad, gain_grad, midway_grad, out_grad, mixed_grad = (
+            feed_forward_back(incoming, midway, gate, up, gains_ref[layer, 1:2], weights)
+        )
+        kept["down_grad"][layer] = down_grad
+        kept["gate_grad"][layer] = gate_grad
+        kept["up_grad"][layer] = up_grad
+        kept["out_grad"][layer] = out_grad
+        kept["midway_grad"][...] = midway_grad
+        kept["query_grad"][...] = attend_back(
+            mixed_grad,
+            kept["attended"][layer],
+            kept["query"].at[layer],
+            kept["joined"].at[layer],
+            kept["probs"].at[layer],
+            kept["parts"].at[layer],
+        )
+        sums[layer].start()
+        return gain_grad
+
+    def end_of_layer(layer, current, weights):
+        sums[layer].finish(kept["key_grads"])
+        turned, values, gain_grad, grad_in = project_back(
+            kept["query_grad"][...],
+            kept["key_grads"][...],
+            kept["midway_grad"][...],
+            current,
+            gains_ref[layer, 0:1],
+            cos,
+            sin,
+            weights,
+        )
+        kept["turned"][layer] = turned
+        kept["values"][layer] = values
+        return gain_grad, grad_in
+
+    def prepare_grads(layer):
+        grads[layer].prepare(
+            kept["normed"][layer],
+            kept["normed_two"][layer],
+            kept["attended"][layer],
+            kept["hidden"][layer],
+        )
+
+    def rest_grads(layer):
+        grads[layer].rest(
+            kept["gate_grad"].at[layer], kept["up_grad"].at[layer], kept["down_grad"].at[layer]
+        )
+
+    def projection_grads(layer):
+        grads[layer].projections(
+            kept["turned"].at[layer], kept["values"].at[layer], kept["out_grad"].at[layer]
+        )
+
+    x = x_ref[...].astype(F32)
+    start_layer(0, x, first_1)
+    midway, gate, up, result = rest_of_layer(0, x, rest_1)
+    kept["midway"][...] = midway
+    kept["gate"][...] = gate
+    kept["up"][...] = up
+    passed = result.astype(BF16)
+    kept["x_2"][...] = passed
+    start_layer(1, passed.astype(F32), first_2)
+    midway, gate, up, result = rest_of_layer(1, kept["x_2"][...].astype(F32), rest_2)
+    result_ref[...] = result.T
+
+    mlp_gain_grad_2 = back_of_layer(1, late_ref[...].astype(F32), midway, gate, up, rest_2)
+    prepare_grads(1)
+    sums[1].middle()
+    rest_grads(1)
+    attn_gain_grad_2, grad_in = end_of_layer(1, kept["x_2"][...].astype(F32), first_2)
+    mlp_gain_grad_1 = back_of_layer(
+        0,
         grad_in.astype(BF16).astype(F32),
-        midway_ref[...],
-        gate_ref[...],
-        up_ref[...],
-        gains_ref[0, 1:2],
-        lower,
-    )
-    down_grad_ref[...] = down_grad
-    gate_grad_ref[...] = gate_grad
-    up_grad_ref[...] = up_grad
-    mlp_gain_grad_ref[...] = gain_grad
-    lower_midway_grad_ref[...] = midway_grad
-    out_grad_ref[...] = out_grad
-    lower_query_grad_ref[...] = attend_back(
-        mixed_grad, attended, query_ref, keys_ref, probs_ref, parts_ref
-    )
-
-
-def grads_kernel(
-    normed_ref,
-    turned_ref,
-    values_ref,
-    attended_ref,
-    out_grad_ref,
-    normed_two_ref,
-    gate_grad_ref,
-    up_grad_ref,
-    hidden_ref,
-    down_grad_ref,
-    attn_gain_grad_ref,
-    mlp_gain_grad_ref,
-    out_ref,
-    lhs,
-    hidden_t,
-    stage,
-):
-    weight_grads(
-        normed_ref[...],
-        turned_ref[...],
-        values_ref[...],
-        attended_ref[...],
-        out_grad_ref[...],
-        normed_two_ref[...],
-        gate_grad_ref[...],
-        up_grad_ref[...],
-        hidden_ref[...],
-        down_grad_ref[...],
-        attn_gain_grad_ref[...],
-        mlp_gain_grad_ref[...],
-        out_ref,
-        lhs,
-        hidden_t,
-        stage,
-    )
-
-
-def end_kernel(
-    key_grads_ref,
-    query_grad_ref,
-    midway_grad_ref,
-    x_ref,
-    gains_ref,
-    cos_ref,
-    sin_ref,
-    wide_ref,
-    grad_in_ref,
-    turned_ref,
-    values_ref,
-    gain_grad_ref,
-    *scratch,
-):
-    own = Weights(wide_ref, None, 0, PROJECTION, scratch)
-    turned, values, gain_grad, grad_in = project_back(
-        query_grad_ref[...],
-        key_grads_ref[...],
-        midway_grad_ref[...],
-        x_ref[...].astype(F32),
-        gains_ref[0, 0:1],
-        cos_ref[...],
-        sin_ref[...],
-        own,
-    )
-    grad_in_ref[...] = grad_in
-    turned_ref[...] = turned
-    values_ref[...] = values
-    gain_grad_ref[...] = gain_grad
-
-
-def call(kernel, name, out_shape, *operands, scratch=(), specs=None):
+        kept["midway"][...],
+        kept["gate"][...],
+        kept["up"][...],
+        rest_1,
+    )
+    prepare_grads(0)
+    sums[0].middle()
+    projection_grads(1)
+    grads[1].round(kept["packed"], attn_gain_grad_2, mlp_gain_grad_2)
+    leave_2 = pltpu.make_async_copy(kept["packed"], grads_2_ref, out_sems.at[0])
+    leave_2.start()
+    rest_grads(0)
+    attn_gain_grad_1, grad_in = end_of_layer(0, x_ref[...].astype(F32), first_1)
+    grad_in_ref[...] = grad_in.T
+    projection_grads(0)
+    leave_2.wait()
+    grads[0].round(kept["packed"], attn_gain_grad_1, mlp_gain_grad_1)
+    leave_1 = pltpu.make_async_copy(kept["packed"], grads_1_ref, out_sems.at[1])
+    leave_1.start()
+    leave_1.wait()
+
+
+def run_layers(x, late, gains, wide, down, cos, sin, own_seg, seg_row):
+    edge = jax.ShapeDtypeStruct((D, ROWS), F32)
+    part = jax.ShapeDtypeStruct((64, PACKED, LANES), BF16)
+    weights = weight_scratch(*PROJECTION) + weight_scratch(*REST)
     return pl.pallas_call(
-        kernel,
-        out_shape=out_shape,
-        in_specs=[VMEM] * len(operands) if specs is None else specs,
-        out_specs=jax.tree.map(lambda _: VMEM, out_shape),
-        scratch_shapes=list(scratch),
-        compiler_params=params(),
-        name=name,
-    )(*operands)
+        layers_kernel,
+        out_shape=(edge, edge, part, part),
+        in_specs=[VMEM] * 3 + [ANY] * 2 + [VMEM] * 4,
+        out_specs=(VMEM, VMEM, ANY, ANY),
+        scratch_shapes=[
+            pltpu.SemaphoreType.DMA((4, 8)),
+            pltpu.SemaphoreType.DMA((4, 8)),
+            pltpu.SemaphoreType.DMA((2,)),
+            *[pltpu.VMEM(shape, kind) for shape, kind in KEPT.values()],
+            *weights,
+            *weights,
+        ],
+        compiler_params=params(2),
+        name="layers",
+    )(x, late, gains, wide, down, cos, sin, own_seg, seg_row)
 
 
 def rope_tables(first):
@@ -1220,215 +1203,8 @@
     gathered = gather_weights(pack_shards(shards))
     wide, down, gains = unpack_weights(gathered)
 
-    whole = like((ROWS, D), F32)
-    half = like((ROWS, D), BF16)
-    keys_shape = like((ROWS, 2 * KVD), BF16)
-    hidden_shape = like((ROWS, FF), BF16)
-    acts = like((ROWS, FF), F32)
-    probs_shape = (KV_HEADS, GROUP * ROWS, SEQ)
-    turned_shape = like((ROWS, D + KVD), BF16)
-    values_shape = like((ROWS, KVD), BF16)
-    row_shape = like((1, D), F32)
-    parts_shape = like((8, 2 * KVD, ROWS), BF16)
-
-    first_part = weight_scratch(*PROJECTION)
-    second_part = weight_scratch(*REST)
-
-    normed_1, query_1, joined_1 = call(
-        start_kernel,
-        "start",
-        (half, half, keys_shape),
-        x,
-        gains,
-        wide,
-        cos,
-        sin,
-        specs=[VMEM, VMEM, ANY, VMEM, VMEM],
-        scratch=first_part,
-    )
-    keys_1 = gather_keys(joined_1, 2)
-    (
-        probs_1,
-        attended_1,
-        midway_1,
-        normed_two_1,
-        gate_1,
-        up_1,
-        hidden_1,
-        x_2,
-        normed_2,
-        query_2,
-        joined_2,
-    ) = call(
-        middle_kernel,
-        "middle",
-        (
-            like(probs_shape, BF16),
-            half,
-            whole,
-            half,
-            acts,
-            acts,
-            hidden_shape,
-            half,
-            half,
-            half,
-            keys_shape,
-        ),
-        x,
-        gains,
-        wide,
-        down,
-        cos,
-        sin,
-        query_1,
-        keys_1,
-        own_seg,
-        seg_row,
-        specs=[VMEM] * 2 + [ANY] * 2 + [VMEM] * 6,
-        scratch=second_part + first_part,
-    )
-    keys_2 = gather_keys(joined_2, 3)
-    (
-        result,
-        attended_2,
-        normed_two_2,
-        hidden_2,
-        gate_grad_2,
-        up_grad_2,
-        mlp_gain_grad_2,
-        midway_grad_2,
-        out_grad_2,
-        query_grad_2,
-        parts_2,
-    ) = call(
-        turn_kernel,
-        "turn",
-        (
-            whole,
-            half,
-            half,
-            hidden_shape,
-            hidden_shape,
-            hidden_shape,
-            row_shape,
-            whole,
-            half,
-            whole,
-            parts_shape,
-        ),
-        x_2,
-        late,
-        gains,
-        wide,
-        down,
-        query_2,
-        keys_2,
-        own_seg,
-        seg_row,
-        scratch=[pltpu.VMEM(probs_shape, BF16)] + second_part,
-        specs=[VMEM] * 3 + [ANY] * 2 + [VMEM] * 4,
-    )
-    key_grads_2 = scatter_key_grads(parts_2, 4)
-    (
-        turned_2,
-        values_2,
-        attn_gain_grad_2,
-        down_grad_1,
-        gate_grad_1,
-        up_grad_1,
-        mlp_gain_grad_1,
-        midway_grad_1,
-        out_grad_1,
-        query_grad_1,
-        parts_1,
-    ) = call(
-        back_kernel,
-        "back",
-        (
-            turned_shape,
-            values_shape,
-            row_shape,
-            half,
-            hidden_shape,
-            hidden_shape,
-            row_shape,
-            whole,
-            half,
-            whole,
-            parts_shape,
-        ),
-        key_grads_2,
-        query_grad_2,
-        midway_grad_2,
-        x_2,
-        gains,
-        cos,
-        sin,
-        wide,
-        down,
-        midway_1,
-        gate_1,
-        up_1,
-        attended_1,
-        query_1,
-        keys_1,
-        probs_1,
-        specs=[VMEM] * 7 + [ANY] * 2 + [VMEM] * 7,
-        scratch=first_part + second_part,
-    )
-    grads_shape = like((64, PACKED, LANES), BF16)
-    grads_2 = call(
-        grads_kernel,
-        "grads",
-        grads_shape,
-        normed_2,
-        turned_2,
-        values_2,
-        attended_2,
-        out_grad_2,
-        normed_two_2,
-        gate_grad_2,
-        up_grad_2,
-        hidden_2,
-        late,
-        attn_gain_grad_2,
-        mlp_gain_grad_2,
-        scratch=GRAD_SCRATCH,
-    )
-    key_grads_1 = scatter_key_grads(parts_1, 5)
-    grad_in, turned_1, values_1, attn_gain_grad_1 = call(
-        end_kernel,
-        "end",
-        (whole, turned_shape, values_shape, row_shape),
-        key_grads_1,
-        query_grad_1,
-        midway_grad_1,
-        x,
-        gains,
-        cos,
-        sin,
-        wide,
-        specs=[VMEM] * 7 + [ANY],
-        scratch=first_part,
-    )
-    grads_1 = call(
-        grads_kernel,
-        "grads",
-        grads_shape,
-        normed_1,
-        turned_1,
-        values_1,
-        attended_1,
-        out_grad_1,
-        normed_two_1,
-        gate_grad_1,
-        up_grad_1,
-        hidden_1,
-        down_grad_1,
-        attn_gain_grad_1,
-        mlp_gain_grad_1,
-        scratch=GRAD_SCRATCH,
+    result, grad_in, grads_1, grads_2 = run_layers(
+        x, late, gains, wide, down, cos, sin, own_seg, seg_row
     )
     by_device = (4, 2, 2, 4, PACKED, LANES)
     leaving = jnp.where(section == 0, result, grad_in)

time: 275 us -> 210 us (0.76)
  Pallas kernels: 256 us -> 201 us
  local copies, waits for them, and re-layouts: 14.8 us -> 4.72 us
    pallas_call x11 -> x1, Pallas kernels: 121 us -> 63.8 us  [run_layers(): pl.pallas_call(layers_kernel, out_shape=(edge, edge, part, part), in_spec...]
    pallas_call x7 -> x0, local copies, waits for them, and re-layouts: 10.7 us -> none  [finish(): pl.pallas_call(finish_kernel, out_shape=tuple((jax.ShapeDtypeStruct(shape...]
where the time goes in v2:
time: 210 us; the launch traced here: 209 us
  Pallas kernels  201 us (96%)
  local copies, waits for them, and re-layouts  4.72 us (2%)
  other arithmetic  3.06 us (1%)
    pallas_call x1, Pallas kernels, run_layers(): pl.pallas_call(layers_kernel, out_shape=(edge, edge, part, part), in_spec...  63.8 us
    pallas_call x1, Pallas kernels, scatter_grads(): pl.pallas_call(scatter_kernel, out_shape=(jax.ShapeDtypeStruct((PACKED, L...  62.1 us
    pallas_call x1, Pallas kernels, gather_weights(): pl.pallas_call(gather_kernel, out_shape=jax.ShapeDtypeStruct((2, 4, 2, 2,...  55.6 us
    pallas_call x1, Pallas kernels, unpack_weights(): pl.pallas_call(unpack_kernel, grid=(2, 4), out_shape=(jax.ShapeDtypeStruc...  15.6 us

profile of v2, /device:TPU:0, one launch (start us, length us, event | category | flops | bytes accessed | tf_op | source)
XLA Modules:
  0.0 209.5 jit_solution(11286806401395224015)
XLA Ops:
  0.6 0.0 copy-start
  0.7 0.7 copy-done
  1.3 0.1 fusion.1
  1.4 0.6 dynamic-slice_bitcast_fusion.seg_ref
  2.0 0.7 copy.28.own_seg_ref
  2.8 1.6 pack_shards.1.mine_ref
  4.4 0.3 fusion
  4.7 0.8 pad_maximum_fusion
  5.6 1.0 constant_dynamic-slice_fusion.1
  6.6 0.8 copy.26
  7.4 0.8 copy.25
  8.2 55.6 %gather_weights.1 = bf16[2,4,2,2,4,448,128]{6,5,4,3,2,1,0:T(8,128)(2,1)} custom-call(bf16[448,128]{1,0:T(8,128)(2,1)} %pack_shards.1.mine_ref), custom_call_target="tpu_custom_call" | custom-call | tf_op jit(solution)/shard_map/gather_weights/pallas_call | solution.py:199
  63.8 15.6 %unpack_weights.1 = (bf16[2,576,4608]{2,1,0:T(8,128)(2,1)}, bf16[2,1536,576]{2,1,0:T(8,128)(2,1)}, f32[2,8,576]{2,1,0:T(8,128)}) custom-call(bf16[128,448,128]{2,1,0:T(8,128)(2,1)} %bitcast.16), custom_call_target="tpu_custom_call" | custom-call | tf_op jit(solution)/shard_map/unpack_weights/pallas_call | solution.py:623
  79.4 63.8 %layers.1 = (f32[576,128]{1,0:T(8,128)}, f32[576,128]{1,0:T(8,128)}, bf16[64,448,128]{2,1,0:T(8,128)(2,1)}, bf16[64,448,128]{2,1,0:T(8,128)(2,1)}) custom-call(bf16[128,576]{1,0:T(8,128)(2,1)} %bitcast.20, bf16[128,576]{1,0:T(8,128)(2,1)} %bitcast.19, f32[2,8,576]{2,1,0:T(8,128)} %get-tuple-element.29.gains_ref, ...), custom_call_target="tpu_custom_call" | custom-call | tf_op jit(solution)/shard_map/layers/pallas_call | solution.py:1167
  143.2 1.9 broadcast_select_fusion
  145.1 62.1 %scatter_grads.1 = (f32[448,128]{1,0:T(8,128)}, f32[576,128]{1,0:T(8,128)}) custom-call(bf16[4,2,2,4,448,128]{5,4,3,2,1,0:T(8,128)(2,1)} %bitcast.17, bf16[4,2,2,4,448,128]{5,4,3,2,1,0:T(8,128)(2,1)} %bitcast.18, f32[576,128]{1,0:T(8,128)} %get-tuple-element.49.edge_ref), custom_call_target="tpu_custom_call" | custom-call | tf_op jit(solution)/shard_map/scatter_grads/pallas_call | solution.py:386
  207.2 2.1 %finish.1 = (f32[1,2,1,576,128]{4,3,2,1,0:T(8,128)}, f32[1,9]{1,0:T(1,128)}, f32[9,1,576]{2,1,0:T(1,128)}, f32[9,1,192]{2,1,0:T(1,128)}, f32[9,1,192]{2,1,0:T(1,...) custom-call(f32[448,128]{1,0:T(8,128)} %get-tuple-element.36.packed_, ...), custom_call_target="tpu_custom_call" | custom-call | tf_op jit(solution)/shard_map/finish/pallas_call | solution.py:693
  (2 shorter events, 0.0 us)
Async XLA Ops:
  0.6 0.7 copy-start

commit v3 on v2

v3 whole, which is shorter than its diff:
```python
import functools

import jax
import jax.numpy as jnp
from jax import lax
from jax.experimental import pallas as pl
from jax.experimental.pallas import tpu as pltpu
from jax.sharding import PartitionSpec as P

MESH = pl.DeviceIdType.MESH
F32 = jnp.float32
BF16 = jnp.bfloat16
ANY = pl.BlockSpec(memory_space=pl.ANY)
VMEM = pl.BlockSpec(memory_space=pltpu.VMEM)

D = 576
FF = 1536
KVD = 192
HEAD = 64
GROUP = 3
KV_HEADS = 3
ROWS = 128
SEQ = 1024
LANES = 128

norm_eps = 1e-05
rope_base = 100000.0
masked_score = -1e30

WIDE = 4608
GATE_AT = 768
UP_AT = GATE_AT + FF
OUT_AT = UP_AT + FF
VALUE_AT = OUT_AT + D
TAIL_AT = VALUE_AT - HEAD
BLOCKS = WIDE // LANES

DOWN_ROWS = 24
TAIL_ROW = 4 * DOWN_ROWS
UPPER_ROW = TAIL_ROW + DOWN_ROWS // 2
LOWER_ROW = 336
GAIN_ROW = LOWER_ROW + 9 * 12
PACKED = 448
GAIN_TILE = 432
UPPER_COLUMNS = tuple(range(GATE_AT // LANES, OUT_AT // LANES))
LOWER_COLUMNS = tuple(range(GATE_AT // LANES)) + tuple(range(OUT_AT // LANES, BLOCKS))


def packed_row(column):
    if column in UPPER_COLUMNS:
        return UPPER_ROW + 9 * UPPER_COLUMNS.index(column)
    return LOWER_ROW + 9 * LOWER_COLUMNS.index(column)


GATHER_PARTS = (
    ((0, 336), (((0, 176), "xy"), ((176, 160), "yx"))),
    ((336, 112), (((336, 64), "xy"), ((400, 48), "yx"))),
)
VMEM_BYTES = 63 * 1024 * 1024


def params(collective_id=None):
    if collective_id is None:
        return pltpu.CompilerParams(vmem_limit_bytes=VMEM_BYTES)
    return pltpu.CompilerParams(
        vmem_limit_bytes=VMEM_BYTES, collective_id=collective_id, has_side_effects=True
    )


def dot(left, right):
    return jnp.dot(left, right, preferred_element_type=F32)


def dot_nt(left, right):
    return lax.dot_general(left, right, (((1,), (1,)), ((), ())), preferred_element_type=F32)


def dot_tn(left, right):
    return lax.dot_general(left, right, (((0,), (0,)), ((), ())), preferred_element_type=F32)


class Place:
    def __init__(self):
        self.section = lax.axis_index("section")
        ctx = lax.axis_index("ctx")
        fsdp = lax.axis_index("fsdp")
        self.core = lax.rem(ctx, 2)
        self.at = {
            "x": lax.rem(fsdp, 4),
            "y": ctx // 2,
            "z": self.section * 2 + fsdp // 4,
        }

    def device(self, core=None, **moved):
        at = dict(self.at, **moved)
        core = self.core if core is None else core
        return (at["z"] // 2, at["y"] * 2 + core, lax.rem(at["z"], 2) * 4 + at["x"])

    def shifted(self, axis, step):
        return lax.rem(self.at[axis] + step + 4, 4)

    def neighbour(self, axis, step):
        return self.device(**{axis: self.shifted(axis, step)})

    def partner(self):
        return self.device(core=1 - self.core)


def greet(devices):
    barrier = pltpu.get_barrier_semaphore()
    for device in devices:
        pl.semaphore_signal(barrier, inc=1, device_id=device, device_id_type=MESH)
    pl.semaphore_wait(barrier, len(devices))


def halves(rows):
    first, count = rows
    upper = (count // 2 + 15) // 16 * 16
    return (first, upper), (first + upper, count - upper)


def layer_region(ref, layer, coords, whole, rows, core):
    y = slice(None) if "y" in whole else coords["y"]
    x = slice(None) if "x" in whole else coords["x"]
    return ref.at[layer, y, core, :, x, pl.ds(*rows)]


GATHER_SLOTS = 3 + 2 * 2 * 4 + 2 * 4


def gather_steps(place, layer, part, held, send_sems, recv_sems):
    core = place.core
    all_rows, chunks = part
    plane = lax.rem(place.at["z"] + 4 - 2 * layer, 4)

    def copy(slot, ref, device):
        return pltpu.make_async_remote_copy(
            src_ref=ref,
            dst_ref=ref,
            send_sem=send_sems.at[slot],
            recv_sem=recv_sems.at[slot],
            device_id=device,
            device_id_type=MESH,
        )

    def shard(z_lo):
        return held.at[layer, place.at["y"], core, z_lo, place.at["x"], pl.ds(*all_rows)]

    def up(z_lo, slot):
        return copy(slot, shard(z_lo), place.neighbour("z", 1))

    def down(z_lo, slot):
        return copy(slot, shard(z_lo), place.neighbour("z", -1))

    for source in range(2):

        @pl.when(plane == source)
        def _():
            up(source, 0).start()
            down(source, 1).start()

    yield

    @pl.when((plane == 1) | (plane == 2))
    def _():
        up(0, 0).wait_recv()

    @pl.when((plane == 0) | (plane == 3))
    def _():
        down(0, 1).wait_recv()

    @pl.when(plane == 2)
    def _():
        up(1, 2).start()

    @pl.when(plane == 3)
    def _():
        down(0, 2).start()

    yield

    @pl.when(plane >= 2)
    def _():
        up(0, 2).wait_recv()

    counter = [3]
    sent = []

    def send(ref, device):
        made = copy(counter[0], ref, device)
        counter[0] += 1
        made.start()
        sent.append(made)
        return made

    to_partner = []
    for phase in range(2):
        first, second = [], []
        for rows, order in chunks:
            axis, whole = order[phase], order[:phase]
            block = layer_region(held, layer, place.at, whole, rows, core)
            first.append([send(block, place.neighbour(axis, way)) for way in (1, -1)])
            if phase == 1:
                to_partner.append(send(block, place.partner()))
        yield
        for copies, (rows, order) in zip(first, chunks):
            axis, whole = order[phase], order[:phase]
            for made in copies:
                made.wait_recv()
            left = dict(place.at, **{axis: place.shifted(axis, -1)})
            right = dict(place.at, **{axis: place.shifted(axis, 1)})
            upper, lower = halves(rows)
            second += [
                send(
                    layer_region(held, layer, left, whole, upper, core), place.neighbour(axis, 1)
                ),
                send(
                    layer_region(held, layer, right, whole, lower, core), place.neighbour(axis, -1)
                ),
            ]
            if phase == 1:
                for coords in (left, right):
                    to_partner.append(
                        send(layer_region(held, layer, coords, whole, rows, core), place.partner())
                    )
        yield
        for made in second:
            made.wait_recv()
    for rows, order in chunks:
        axis, whole = order[1], order[:1]
        far = dict(place.at, **{axis: place.shifted(axis, 2)})
        to_partner.append(send(layer_region(held, layer, far, whole, rows, core), place.partner()))
    yield
    for made in to_partner:
        made.wait_recv()
    for made in sent:
        made.wait_send()

    @pl.when(plane <= 1)
    def _():
        up(0, 0).wait_send()
        down(0, 1).wait_send()

    @pl.when(plane >= 2)
    def _():
        up(0, 2).wait_send()

    yield


SCATTER_PARTS = (
    ((0, 336), (((0, 176), "yx"), ((176, 160), "xy"))),
    ((336, 112), (((336, 64), "yx"), ((400, 48), "xy"))),
)
SCATTER_SLOTS = 1 + 2 * 2 * 4 + 2


def scatter_inboxes(part):
    (first, count), chunks = part
    boxes = []
    for (_, rows), order in chunks:
        others = (2, 4) if order == "yx" else (4, 2)
        boxes.append(pltpu.VMEM((3, *others, rows, LANES), BF16))
        boxes.append(pltpu.VMEM((3, 2, rows, LANES), BF16))
    boxes.append(pltpu.VMEM((2, count, LANES), BF16))
    return boxes


def scatter_steps(place, layer, part, held, boxes, send_sems, recv_sems, out_ref):
    core = place.core
    here_y, here_x = place.at["y"], place.at["x"]
    (first, count), chunks = part
    counter = [0]
    sent = []

    def copy(source, target, device):
        slot = counter[0]
        counter[0] += 1
        return pltpu.make_async_remote_copy(
            src_ref=source,
            dst_ref=target,
            send_sem=send_sems.at[slot],
            recv_sem=recv_sems.at[slot],
            device_id=device,
            device_id_type=MESH,
        )

    def send(source, target, device):
        made = copy(source, target, device)
        made.start()
        sent.append(made)
        return made

    def add(spot, source, rows):
        held[spot] = (held[spot].astype(F32) + source().astype(F32)).astype(BF16)

    all_rows = pl.ds(first, count)
    swap = copy(
        held.at[layer, :, 1 - core, :, :, all_rows],
        held.at[1 - layer, :, core, :, :, all_rows],
        place.partner(),
    )
    swap.start()
    yield
    swap.wait()

    def add_swapped(step, carry):
        y, z_lo, x = step // 8, lax.rem(step // 4, 2), lax.rem(step, 4)
        add(
            (layer, y, core, z_lo, x, all_rows),
            lambda: held[1 - layer, y, 1 - core, z_lo, x, all_rows],
            count,
        )
        return carry

    lax.fori_loop(0, 32, add_swapped, 0)

    def add_block(phase, axis, coords, rows, box, slot):
        at, size = rows

        def in_box(begin):
            return pl.ds(begin, size)

        begin = 0 if slot else at[1]
        here = pl.ds(at[0], size)
        if phase == 0:

            def body(step, carry):
                if axis == "y":
                    z_lo, x = step // 4, lax.rem(step, 4)
                    spot = (layer, coords["y"], core, z_lo, x, here)
                    add(spot, lambda: box[slot, z_lo, x, in_box(begin)], size)
                else:
                    y, z_lo = step // 2, lax.rem(step, 2)
                    spot = (layer, y, core, z_lo, coords["x"], here)
                    add(spot, lambda: box[slot, y, z_lo, in_box(begin)], size)
                return carry

            lax.fori_loop(0, 8, body, 0)
        else:
            for z_lo in range(2):
                spot = (layer, coords["y"], core, z_lo, coords["x"], here)
                add(spot, lambda: box[slot, z_lo, in_box(begin)], size)

    flights = [None, None]
    for phase in range(2):
        for step in range(2):
            for i, (rows, order) in enumerate(chunks):
                box = boxes[2 * i + phase]
                if flights[i] is not None:
                    for made, before_phase, before_axis, lands, spot_rows, before_box, slot in flights[i]:
                        made.wait_recv()
                        add_block(before_phase, before_axis, lands, spot_rows, before_box, slot)
                axis, whole = order[phase], order[phase + 1 :]
                right = dict(place.at, **{axis: place.shifted(axis, 1)})
                left = dict(place.at, **{axis: place.shifted(axis, -1)})
                far = dict(place.at, **{axis: place.shifted(axis, 2)})
                upper, lower = halves(rows)
                if step == 0:
                    plan = ((far, upper, 1, right, 0), (far, lower, -1, left, 0))
                else:
                    plan = ((right, rows, 1, place.at, 1), (left, rows, -1, place.at, 2))
                flights[i] = []
                for source_at, part_rows, way, lands, slot in plan:
                    begin = part_rows[0] - rows[0]
                    lead = (slice(None),) * (2 if phase == 0 else 1)
                    made = send(
                        layer_region(held, layer, source_at, whole, part_rows, core),
                        box.at[(slot, *lead, pl.ds(begin, part_rows[1]))],
                        place.neighbour(axis, way),
                    )
                    flights[i].append(
                        (made, phase, axis, lands, ((part_rows[0], begin), part_rows[1]), box, slot)
                    )
            yield
    for flight in flights:
        for made, phase, axis, lands, spot_rows, box, slot in flight:
            made.wait_recv()
            add_block(phase, axis, lands, spot_rows, box, slot)

    plane = lax.rem(place.at["z"] + 4 - 2 * layer, 4)
    odd = lax.rem(plane, 2)
    stays = lax.rem((plane + 1) // 2, 2)
    box = boxes[4]

    def shard(z_lo):
        return held.at[layer, here_y, core, z_lo, here_x, all_rows]

    def along_z(step):
        return place.device(z=lax.rem(place.at["z"] + step + 4, 4))

    pair = send(shard(1 - stays), box.at[0], along_z(1 - 2 * odd))
    last = copy(shard(stays), box.at[1], along_z(2 * odd - 1))
    yield
    pair.wait_recv()
    add((layer, here_y, core, stays, here_x, all_rows), lambda: box[0], count)

    @pl.when(plane >= 2)
    def _():
        last.start()

    yield

    @pl.when(plane < 2)
    def _():
        last.wait_recv()
        out_ref[all_rows] = held[layer, here_y, core, stays, here_x, all_rows].astype(
            F32
        ) + box[1].astype(F32)

    for made in sent:
        made.wait_send()

    @pl.when(plane >= 2)
    def _():
        last.wait_send()

    yield


class Exchange:
    def __init__(self, place, send_sems, recv_sems):
        self.place = place
        self.send_sems = send_sems
        self.recv_sems = recv_sems

    def copy(self, slot, source, target, device):
        return pltpu.make_async_remote_copy(
            src_ref=source,
            dst_ref=target,
            send_sem=self.send_sems.at[slot],
            recv_sem=self.recv_sems.at[slot],
            device_id=device,
            device_id_type=MESH,
        )

    def along_y(self, step):
        return self.place.device(y=lax.rem(self.place.at["y"] + step + 4, 4))


class KeyGather(Exchange):
    def __init__(self, place, keys_ref, send_sems, recv_sems):
        super().__init__(place, send_sems, recv_sems)
        self.keys_ref = keys_ref

    def direct(self, away):
        own = self.keys_ref.at[self.place.at["y"] * 2 + self.place.core]
        return self.copy(away, own, own, self.along_y(away))

    def passed_on(self, away):
        block = self.keys_ref.at[
            lax.rem(self.place.at["y"] - away + 4, 4) * 2 + self.place.core
        ]
        return self.copy(4 + away, block, block, self.place.partner())

    def start(self):
        y = self.place.at["y"]
        for away in (1, 3, 2):

            @pl.when(y + away < 4)
            def _():
                self.direct(away).start()

        self.passed_on(0).start()
        for away in range(1, 4):

            @pl.when(y + away < 4)
            def _():
                self.keys_ref[pl.ds((y + away) * 2, 2)] = jnp.zeros(
                    (2,) + self.keys_ref.shape[1:], self.keys_ref.dtype
                )

    def finish(self):
        y = self.place.at["y"]
        for away in range(1, 4):

            @pl.when(y - away >= 0)
            def _():
                self.direct(away).wait_recv()
                self.passed_on(away).start()

        self.passed_on(0).wait()
        for away in range(1, 4):

            @pl.when(y - away >= 0)
            def _():
                self.passed_on(away).wait()

            @pl.when(y + away < 4)
            def _():
                self.direct(away).wait_send()


class KeyGradSum(Exchange):
    def __init__(self, place, parts_ref, pair_ref, ring_ref, send_sems, recv_sems):
        super().__init__(place, send_sems, recv_sems)
        self.parts_ref = parts_ref
        self.pair_ref = pair_ref
        self.ring_ref = ring_ref

    def swap(self):
        return self.copy(
            0, self.parts_ref.at[1 - self.place.core], self.pair_ref, self.place.partner()
        )

    def direct(self, away):
        y = lax.rem(self.place.at["y"] - away + 4, 4)
        return self.copy(
            away,
            self.parts_ref.at[self.place.core, y],
            self.ring_ref.at[away],
            self.along_y(-away),
        )

    def start(self):
        self.swap().start()

    def middle(self):
        self.swap().wait()
        core = self.place.core
        for y in range(4):
            self.parts_ref[core, y] = (
                self.parts_ref[core, y].astype(F32) + self.pair_ref[y].astype(F32)
            ).astype(BF16)
        for away in (1, 3, 2):

            @pl.when(self.place.at["y"] - away >= 0)
            def _():
                self.direct(away).start()

    def finish(self, out_ref):
        y = self.place.at["y"]
        out_ref[...] = self.parts_ref[self.place.core, y].astype(F32)
        for away in range(1, 4):

            @pl.when(y + away < 4)
            def _():
                self.direct(away).wait_recv()
                out_ref[...] += self.ring_ref[away].astype(F32)

        for away in range(1, 4):

            @pl.when(y - away >= 0)
            def _():
                self.direct(away).wait_send()


def packed_shard(attn_ref, query_ref, key_ref, value_ref, w_out_ref, gate_ref, up_ref, down_ref, mlp_ref):
    def wide(ref):
        return ref[0].astype(F32)

    joined = jnp.concatenate(
        [wide(r) for r in (query_ref, key_ref, gate_ref, up_ref, w_out_ref, value_ref)], axis=1
    )
    down = wide(down_ref)
    pieces = [down[:, i * LANES : (i + 1) * LANES] for i in range(4)]
    half = DOWN_ROWS // 2
    pieces.append(jnp.concatenate([down[:half, 4 * LANES :], down[half:, 4 * LANES :]], axis=1))
    pieces += [joined[:, i * LANES : (i + 1) * LANES] for i in UPPER_COLUMNS]
    pieces.append(jnp.zeros((12, LANES), F32))
    pieces += [joined[:, i * LANES : (i + 1) * LANES] for i in LOWER_COLUMNS]
    for ref in (attn_ref, mlp_ref):
        gain = ref[...].astype(F32)
        pieces.append(jnp.concatenate([gain, jnp.zeros((1, LANES - 9), F32)], axis=1))
    pieces.append(jnp.zeros((2, LANES), F32))
    return jnp.concatenate(pieces, axis=0).astype(BF16)


def gain_masks(first_device, devices, rows_each, rows):
    shape = (devices * rows_each, D)
    row = lax.broadcasted_iota(jnp.int32, shape, 0)
    owner = lax.broadcasted_iota(jnp.int32, shape, 1) // 9
    same = owner == first_device + row // rows_each
    place = lax.rem(row, rows_each)
    return [same & (place == at) for at in rows]


def lane_spread():
    lane = lax.broadcasted_iota(jnp.int32, (LANES, D), 0)
    feature = lax.broadcasted_iota(jnp.int32, (LANES, D), 1)
    return (lane == lax.rem(feature, 9)).astype(BF16)


def packed_rows(held, layer, y, first, count):
    start = first // 16 * 16
    size = (first + count + 15) // 16 * 16 - start
    return [
        held[layer, y, core, z_lo, x, start : start + size].astype(F32)[
            first - start : first - start + count
        ]
        for core in range(2)
        for z_lo in range(2)
        for x in range(4)
    ]


def unpack_wide(held, layer, columns, wide):
    def body(y, carry):
        rows = pl.ds(pl.multiple_of(y * 144, 16), 144)
        for column in columns:
            wide[layer, rows, column * LANES : (column + 1) * LANES] = jnp.concatenate(
                packed_rows(held, layer, y, packed_row(column), 9), axis=0
            ).astype(BF16)
        return carry

    lax.fori_loop(0, 4, body, 0)


def unpack_down(held, layer, down):
    def body(y, carry):
        rows = pl.ds(pl.multiple_of(y * 384, 16), 384)
        for column in range(4):
            down[layer, rows, column * LANES : (column + 1) * LANES] = jnp.concatenate(
                packed_rows(held, layer, y, DOWN_ROWS * column, DOWN_ROWS), axis=0
            ).astype(BF16)
        tails = []
        for tail in packed_rows(held, layer, y, TAIL_ROW, DOWN_ROWS // 2):
            tails += [tail[:, :HEAD], tail[:, HEAD:]]
        down[layer, rows, 4 * LANES :] = jnp.concatenate(tails, axis=0).astype(BF16)
        return carry

    lax.fori_loop(0, 4, body, 0)


def unpack_gains(held, layer, gains):
    totals = [jnp.zeros((1, D), F32)] * 2
    spread_to = lane_spread()
    for y in range(4):
        rows = held[layer, y, :, :, :, GAIN_TILE:, :].reshape(16 * 16, LANES)
        spread = dot(rows, spread_to)
        masks = gain_masks(y * 16, 16, 16, (GAIN_ROW - GAIN_TILE, GAIN_ROW - GAIN_TILE + 1))
        totals = [
            total + jnp.sum(jnp.where(mask, spread, 0.0), axis=0, keepdims=True)
            for total, mask in zip(totals, masks)
        ]
    gains[layer, 0:1] = totals[0]
    gains[layer, 1:2] = totals[1]


def finish_kernel(
    packed_ref,
    kept_ref,
    came_ref,
    edges_ref,
    attn_ref,
    query_ref,
    key_ref,
    value_ref,
    w_out_ref,
    gate_ref,
    up_ref,
    down_ref,
    mlp_ref,
):
    section = lax.axis_index("section")
    edges_ref[0, section, 0] = kept_ref[...]
    edges_ref[0, 1 - section, 0] = came_ref[...]
    packed = packed_ref[...]
    joined = jnp.concatenate(
        [packed[packed_row(i) : packed_row(i) + 9] for i in range(BLOCKS)], axis=1
    )
    query_ref[:, 0] = joined[:, :D]
    key_ref[:, 0] = joined[:, D:GATE_AT]
    gate_ref[:, 0] = joined[:, GATE_AT:UP_AT]
    up_ref[:, 0] = joined[:, UP_AT:OUT_AT]
    w_out_ref[:, 0] = joined[:, OUT_AT:VALUE_AT]
    value_ref[:, 0] = joined[:, VALUE_AT:]
    tail = packed[TAIL_ROW:UPPER_ROW]
    down_ref[0] = jnp.concatenate(
        [packed[DOWN_ROWS * i : DOWN_ROWS * (i + 1)] for i in range(4)]
        + [jnp.concatenate([tail[:, :HEAD], tail[:, HEAD:]], axis=0)],
        axis=1,
    )
    attn_ref[...] = packed[GAIN_ROW : GAIN_ROW + 1, :9]
    mlp_ref[...] = packed[GAIN_ROW + 1 : GAIN_ROW + 2, :9]


def finish(packed, kept, came):
    shapes = (
        (1, 2, 1, D, ROWS),
        (1, 9),
        (9, 1, D),
        (9, 1, KVD),
        (9, 1, KVD),
        (9, 1, D),
        (9, 1, FF),
        (9, 1, FF),
        (1, DOWN_ROWS, D),
        (1, 9),
    )
    edges, attn, *wide, down, mlp = pl.pallas_call(
        finish_kernel,
        out_shape=tuple(jax.ShapeDtypeStruct(shape, F32) for shape in shapes),
        in_specs=[VMEM] * 3,
        out_specs=(VMEM,) * len(shapes),
        compiler_params=params(),
        name="finish",
    )(packed, kept, came)
    wide = [grad.transpose(1, 0, 2) for grad in wide]
    return (edges.transpose(0, 1, 2, 4, 3), attn, *wide, down, mlp)


def swap_halves(block):
    lane = lax.broadcasted_iota(jnp.int32, block.shape, 1)
    return jnp.where(
        lax.rem(lane, HEAD) < HEAD // 2,
        pltpu.roll(block, LANES - HEAD // 2, 1),
        pltpu.roll(block, HEAD // 2, 1),
    )


def rotated(block, cos, sin):
    return block * cos + swap_halves(block) * sin


def project(current, gain, weights, cos, sin, normed_ref, query_ref):
    scale = lax.rsqrt(jnp.mean(current * current, axis=1, keepdims=True) + norm_eps)
    normed = (current * scale * gain).astype(BF16)
    normed_ref[...] = normed
    raw = dot(normed, weights.get("qk"))
    turned = [
        rotated(raw[:, i * LANES : (i + 1) * LANES], cos, sin).astype(BF16) for i in range(6)
    ]
    for i in range(4):
        query_ref[:, i * LANES : (i + 1) * LANES] = turned[i]
    query_ref[:, 4 * LANES :] = turned[4][:, :HEAD]
    values = dot(normed, weights.get("tail"))[:, HEAD:]
    return jnp.concatenate(
        [turned[4][:, HEAD:].astype(F32), turned[5].astype(F32), values], axis=1
    ).astype(BF16)


def heads_of(rows, group):
    return jnp.concatenate(
        [rows[:, (group * GROUP + r) * HEAD : (group * GROUP + r + 1) * HEAD] for r in range(GROUP)],
        axis=0,
    )


def attend(query_ref, keys_ref, seg_row, probs_ref):
    first = lax.axis_index("ctx") * ROWS
    rows = first + lax.broadcasted_iota(jnp.int32, (ROWS, SEQ), 0)
    columns = lax.broadcasted_iota(jnp.int32, (ROWS, SEQ), 1)
    own_seg = jnp.sum(jnp.where(columns == rows, seg_row, 0), axis=1, keepdims=True)
    allowed = (columns <= rows) & (seg_row == own_seg)
    bias = jnp.where(allowed, 0.0, masked_score)
    bias = jnp.concatenate([bias] * GROUP, axis=0)
    queries = query_ref[...]
    mixed = []
    for group in range(KV_HEADS):
        keys = keys_ref[:, :, group * HEAD : (group + 1) * HEAD].reshape(SEQ, HEAD)
        values = keys_ref[:, :, KVD + group * HEAD : KVD + (group + 1) * HEAD].reshape(SEQ, HEAD)
        scores = dot_nt(heads_of(queries, group), keys) * HEAD**-0.5 + bias
        shifted = jnp.exp(scores - jnp.max(scores, axis=1, keepdims=True))
        probs = (shifted / jnp.sum(shifted, axis=1, keepdims=True)).astype(BF16)
        probs_ref[group] = probs
        mixture = dot(probs, values)
        mixed += [mixture[r * ROWS : (r + 1) * ROWS] for r in range(GROUP)]
    return jnp.concatenate(mixed, axis=1).astype(BF16)


def feed_forward(current, attended, gain, weights):
    midway = current + dot(attended, weights.get("out"))
    scale = lax.rsqrt(jnp.mean(midway * midway, axis=1, keepdims=True) + norm_eps)
    normed = (midway * scale * gain).astype(BF16)
    gate = dot(normed, weights.get("gate"))
    up = dot(normed, weights.get("up"))
    hidden = (gate / (1.0 + jnp.exp(-gate)) * up).astype(BF16)
    result = midway + dot(hidden, weights.get("down"))
    return midway, scale, normed, gate, up, hidden, result


def norm_backward(scaled, values, scale):
    return scale * scaled - values * scale**3 * jnp.mean(scaled * values, axis=1, keepdims=True)


def feed_forward_back(
    incoming, midway, gate, up, gain, weights
):
    scale = lax.rsqrt(jnp.mean(midway * midway, axis=1, keepdims=True) + norm_eps)
    down_grad = incoming.astype(BF16)
    hidden_grad = dot_nt(down_grad, weights.get("down"))
    sigmoid = 1.0 / (1.0 + jnp.exp(-gate))
    gate_grad = (hidden_grad * up * sigmoid * (1.0 + gate * (1.0 - sigmoid))).astype(BF16)
    up_grad = (hidden_grad * gate * sigmoid).astype(BF16)
    normed_grad = dot_nt(gate_grad, weights.get("gate")) + dot_nt(
        up_grad, weights.get("up")
    )
    gain_grad = jnp.sum(normed_grad * midway * scale, axis=0, keepdims=True)
    midway_grad = incoming + norm_backward(normed_grad * gain, midway, scale)
    out_grad = midway_grad.astype(BF16)
    mixed_grad = dot_nt(out_grad, weights.get("out")).astype(BF16)
    return down_grad, gate_grad, up_grad, gain_grad, midway_grad, out_grad, mixed_grad


def attend_back(mixed_grad, attended, query_ref, keys_ref, probs_ref, parts_ref, between):
    queries = query_ref[...]
    query_grads = []
    for group in range(KV_HEADS):
        keys = keys_ref[:, :, group * HEAD : (group + 1) * HEAD].reshape(SEQ, HEAD)
        values = keys_ref[:, :, KVD + group * HEAD : KVD + (group + 1) * HEAD].reshape(SEQ, HEAD)
        grads = heads_of(mixed_grad, group)
        delta = jnp.sum(
            grads.astype(F32) * heads_of(attended, group).astype(F32), axis=1, keepdims=True
        )
        probs = probs_ref[group]
        score_grad = (probs.astype(F32) * (dot_nt(grads, values) - delta)).astype(BF16)
        query_grad = dot(score_grad, keys) * HEAD**-0.5
        query_grads += [query_grad[r * ROWS : (r + 1) * ROWS] for r in range(GROUP)]
        key_part = (dot_tn(heads_of(queries, group), score_grad) * HEAD**-0.5).astype(BF16)
        value_part = dot_tn(grads, probs).astype(BF16)
        for block in range(8):
            columns = slice(block * ROWS, (block + 1) * ROWS)
            at = (block % 2, block // 2)
            parts_ref[*at, group * HEAD : (group + 1) * HEAD] = key_part[:, columns]
            parts_ref[*at, KVD + group * HEAD : KVD + (group + 1) * HEAD] = value_part[:, columns]
        between[group]()
    return jnp.concatenate(query_grads, axis=1)


def project_back(
    query_grad, key_grads, midway_grad, current, gain, cos, sin, weights
):
    key_grads = key_grads.T
    joined = jnp.concatenate([query_grad, key_grads[:, :KVD]], axis=1)
    turned = jnp.concatenate(
        [rotated(joined[:, i * LANES : (i + 1) * LANES], cos, -sin) for i in range(6)], axis=1
    ).astype(BF16)
    values = key_grads[:, KVD:].astype(BF16)
    padded = jnp.concatenate([jnp.zeros((ROWS, HEAD), F32), key_grads[:, KVD:]], axis=1)
    normed_grad = dot_nt(turned, weights.get("qk")) + dot_nt(
        padded.astype(BF16), weights.get("tail")
    )
    scale = lax.rsqrt(jnp.mean(current * current, axis=1, keepdims=True) + norm_eps)
    gain_grad = jnp.sum(normed_grad * current * scale, axis=0, keepdims=True)
    grad_in = midway_grad + norm_backward(normed_grad * gain, current, scale)
    return turned, values, gain_grad, grad_in


GRAD_DEVICES = 16


def transposed(rows):
    return rows.astype(F32).T.astype(BF16)


class WeightGrads:
    def __init__(self, packed, upper, lower, gain_rows, lhs, hidden_lhs):
        self.packed = packed
        self.upper = upper
        self.lower = lower
        self.gain_rows = gain_rows
        self.lhs = lhs
        self.hidden_lhs = hidden_lhs

    def place(self, stage, first_row, column, product):
        for i in range(product.shape[1] // LANES):
            at = packed_row(column + i) - first_row
            part = product[:, i * LANES : (i + 1) * LANES]
            for d in range(GRAD_DEVICES):
                stage[d, at : at + 9] = part[9 * d : 9 * d + 9]

    def prepare(self, normed, normed_two, attended, hidden):
        self.lhs[0] = transposed(normed)
        self.lhs[1] = transposed(normed_two)
        self.lhs[2] = transposed(attended)
        self.hidden_lhs[...] = transposed(hidden)

    def rows(self, step, each):
        return pl.ds(pl.multiple_of(step * each * GRAD_DEVICES, 16), each * GRAD_DEVICES)

    def round(self, stage, y, first_row):
        rounded = stage[...].astype(BF16)
        self.packed[y, :, :, :, first_row : first_row + stage.shape[1]] = rounded.reshape(
            (2, 2, 4) + rounded.shape[1:]
        )

    def rest(self, gate_grad_ref, up_grad_ref, down_grad_ref):
        half = DOWN_ROWS // 2
        self.upper[:, LOWER_ROW - 12 :] = jnp.zeros((GRAD_DEVICES, 12, LANES), F32)

        def body(y, carry):
            second = self.lhs[1, self.rows(y, 9)]
            self.place(self.upper, 0, GATE_AT // LANES, dot(second, gate_grad_ref[...]))
            self.place(self.upper, 0, UP_AT // LANES, dot(second, up_grad_ref[...]))
            down = dot(self.hidden_lhs[self.rows(y, DOWN_ROWS)], down_grad_ref[...])
            for d in range(GRAD_DEVICES):
                own = down[DOWN_ROWS * d : DOWN_ROWS * (d + 1)]
                for i in range(4):
                    self.upper[d, DOWN_ROWS * i : DOWN_ROWS * (i + 1)] = own[
                        :, i * LANES : (i + 1) * LANES
                    ]
                self.upper[d, TAIL_ROW:UPPER_ROW] = jnp.concatenate(
                    [own[:half, 4 * LANES :], own[half:, 4 * LANES :]], axis=1
                )
            self.round(self.upper, y, 0)
            return carry

        lax.fori_loop(0, 64 // GRAD_DEVICES, body, 0)

    def projections(
        self, turned_ref, values_ref, out_grad_ref, attn_gain_grad, mlp_gain_grad
    ):
        spread_to = lane_spread()
        (mask,) = gain_masks(0, 64, 1, (0,))
        for i, gain_grad in enumerate((attn_gain_grad, mlp_gain_grad)):
            chosen = jnp.where(mask, gain_grad, 0.0).astype(BF16)
            self.gain_rows[i] = dot_nt(chosen, spread_to)
        self.lower[:, GAIN_ROW + 2 - LOWER_ROW :] = jnp.zeros((GRAD_DEVICES, 2, LANES), F32)

        def body(y, carry):
            first = self.lhs[0, self.rows(y, 9)]
            self.place(self.lower, LOWER_ROW, 0, dot(first, turned_ref[...]))
            third = self.lhs[2, self.rows(y, 9)]
            self.place(
                self.lower,
                LOWER_ROW,
                OUT_AT // LANES,
                jnp.concatenate(
                    [dot(third, out_grad_ref[...]), dot(first, values_ref[...])], axis=1
                ),
            )
            for i in range(2):
                gains = self.gain_rows[i, self.rows(y, 1)]
                for d in range(GRAD_DEVICES):
                    at = GAIN_ROW + i - LOWER_ROW
                    self.lower[d, at : at + 1] = gains[d : d + 1]
            self.round(self.lower, y, LOWER_ROW)
            return carry

        lax.fori_loop(0, 64 // GRAD_DEVICES, body, 0)


COLUMNS = {
    "qk": (0, GATE_AT),
    "gate": (GATE_AT, UP_AT),
    "up": (UP_AT, OUT_AT),
    "out": (OUT_AT, VALUE_AT),
    "tail": (TAIL_AT, WIDE),
}


class Weights:
    def __init__(self, layer, wide, down):
        self.layer = layer
        self.wide = wide
        self.down = down

    def get(self, name):
        if name == "down":
            return self.down[self.layer]
        first, end = COLUMNS[name]
        return self.wide[self.layer, :, first:end]


ROW = (ROWS, D)
KEPT = {
    "joined": ((2, 8, ROWS, 2 * KVD), BF16),
    "probs": ((2, KV_HEADS, GROUP * ROWS, SEQ), BF16),
    "parts": ((2, 2, 4, 2 * KVD, ROWS), BF16),
    "pair": ((4, 2 * KVD, ROWS), BF16),
    "ring": ((2, 4, 2 * KVD, ROWS), BF16),
    "key_grads": ((2 * KVD, ROWS), F32),
    "normed": ((2, *ROW), BF16),
    "query": ((2, *ROW), BF16),
    "attended": ((2, *ROW), BF16),
    "normed_two": ((2, *ROW), BF16),
    "hidden": ((2, ROWS, FF), BF16),
    "midway": (ROW, F32),
    "gate": ((ROWS, FF), F32),
    "up": ((ROWS, FF), F32),
    "x_2": (ROW, BF16),
    "gate_grad": ((ROWS, FF), BF16),
    "up_grad": ((ROWS, FF), BF16),
    "down_grad": (ROW, BF16),
    "out_grad": (ROW, BF16),
    "midway_grad": (ROW, F32),
    "query_grad": (ROW, F32),
    "turned": ((ROWS, D + KVD), BF16),
    "values": ((ROWS, KVD), BF16),
    "lhs": ((3, D, ROWS), BF16),
    "hidden_lhs": ((FF, ROWS), BF16),
    "upper": ((GRAD_DEVICES, LOWER_ROW, LANES), F32),
    "lower": ((GRAD_DEVICES, PACKED - LOWER_ROW, LANES), F32),
    "gain_rows": ((2, 64, LANES), F32),
    "held": ((2, 4, 2, 2, 4, PACKED, LANES), BF16),
    "wide": ((2, D, WIDE), BF16),
    "down": ((2, FF, D), BF16),
    "gains": ((2, 8, D), F32),
    "edge": ((D, ROWS), F32),
}


def layers_kernel(
    x_ref,
    late_ref,
    cos_ref,
    sin_ref,
    seg_ref,
    *rest,
):
    shards = rest[:9]
    summed_ref, stays_ref, came_ref = rest[9:12]
    send_sems, recv_sems, gather_send, gather_recv, scatter_send, scatter_recv, edge_sems, credit_sem, *scratch = (
        rest[12:]
    )
    place = Place()
    kept = dict(zip(KEPT, scratch))
    boxes = scratch[len(KEPT) :]
    held, gains_ref = kept["held"], kept["gains"]
    weights = [Weights(i, kept["wide"], kept["down"]) for i in range(2)]
    held[
        place.section, place.at["y"], place.core, lax.rem(place.at["z"], 2), place.at["x"]
    ] = packed_shard(*shards)
    greet(
        [place.partner()]
        + [place.neighbour(axis, way) for axis in "xz" for way in (1, -1)]
        + [place.device(y=place.shifted("y", step)) for step in (1, 2, 3)]
        + [place.device(z=place.shifted("z", 2))]
    )
    leaving = [
        [
            scatter_steps(
                place,
                layer,
                part,
                held,
                boxes[(2 * layer + i) * 5 : (2 * layer + i) * 5 + 5],
                scatter_send.at[layer, i],
                scatter_recv.at[layer, i],
                summed_ref,
            )
            for i, part in enumerate(SCATTER_PARTS)
        ]
        for layer in range(2)
    ]
    edge = pltpu.make_async_remote_copy(
        src_ref=kept["edge"],
        dst_ref=came_ref,
        send_sem=edge_sems.at[0],
        recv_sem=edge_sems.at[1],
        device_id=place.device(z=place.shifted("z", 2)),
        device_id_type=MESH,
    )

    def finish_edge(section, mine):
        @pl.when(place.section == section)
        def _():
            stays_ref[...] = mine

        @pl.when(place.section != section)
        def _():
            kept["edge"][...] = mine
            edge.start()

    def go(layer, part):
        next(leaving[layer][part])

    arriving = [
        [
            gather_steps(
                place, layer, part, held, gather_send.at[layer, i], gather_recv.at[layer, i]
            )
            for i, part in enumerate(GATHER_PARTS)
        ]
        for layer in range(2)
    ]

    def come(layer, part, steps=1):
        for _ in range(steps):
            next(arriving[layer][part])

    cos, sin = cos_ref[...], sin_ref[...]
    mine = lax.axis_index("ctx")
    gathers = [
        KeyGather(place, kept["joined"].at[i], send_sems.at[i], recv_sems.at[i]) for i in range(2)
    ]
    sums = [
        KeyGradSum(
            place,
            kept["parts"].at[i],
            kept["pair"],
            kept["ring"].at[i],
            send_sems.at[2 + i],
            recv_sems.at[2 + i],
        )
        for i in range(2)
    ]
    grads = [
        WeightGrads(
            held.at[i],
            kept["upper"],
            kept["lower"],
            kept["gain_rows"],
            kept["lhs"],
            kept["hidden_lhs"],
        )
        for i in range(2)
    ]

    def start_layer(layer, current):
        unpack_gains(held, layer, gains_ref)
        unpack_wide(held, layer, LOWER_COLUMNS, kept["wide"])
        kept["joined"][layer, mine] = project(
            current,
            gains_ref[layer, 0:1],
            weights[layer],
            cos,
            sin,
            kept["normed"].at[layer],
            kept["query"].at[layer],
        )
        gathers[layer].start()

    def attention_of_layer(layer):
        gathers[layer].finish()
        attended = attend(
            kept["query"].at[layer],
            kept["joined"].at[layer],
            seg_ref[place.section],
            kept["probs"].at[layer],
        )
        kept["attended"][layer] = attended

    def rest_of_layer(layer, current):
        unpack_wide(held, layer, UPPER_COLUMNS, kept["wide"])
        unpack_down(held, layer, kept["down"])
        attended = kept["attended"][layer]
        midway, scale, normed_two, gate, up, hidden, result = feed_forward(
            current, attended, gains_ref[layer, 1:2], weights[layer]
        )
        kept["normed_two"][layer] = normed_two
        kept["hidden"][layer] = hidden
        return midway, gate, up, result

    def back_of_layer(layer, incoming, midway, gate, up, after, between):
        down_grad, gate_grad, up_grad, gain_grad, midway_grad, out_grad, mixed_grad = (
            feed_forward_back(incoming, midway, gate, up, gains_ref[layer, 1:2], weights[layer])
        )
        kept["down_grad"][...] = down_grad
        kept["gate_grad"][...] = gate_grad
        kept["up_grad"][...] = up_grad
        kept["out_grad"][...] = out_grad
        kept["midway_grad"][...] = midway_grad
        after()
        kept["query_grad"][...] = attend_back(
            mixed_grad,
            kept["attended"][layer],
            kept["query"].at[layer],
            kept["joined"].at[layer],
            kept["probs"].at[layer],
            kept["parts"].at[layer],
            between,
        )
        sums[layer].start()
        return gain_grad

    def end_of_layer(layer, current):
        sums[layer].finish(kept["key_grads"])
        turned, values, gain_grad, grad_in = project_back(
            kept["query_grad"][...],
            kept["key_grads"][...],
            kept["midway_grad"][...],
            current,
            gains_ref[layer, 0:1],
            cos,
            sin,
            weights[layer],
        )
        kept["turned"][...] = turned
        kept["values"][...] = values
        return gain_grad, grad_in

    def prepare_grads(layer):
        grads[layer].prepare(
            kept["normed"][layer],
            kept["normed_two"][layer],
            kept["attended"][layer],
            kept["hidden"][layer],
        )

    def rest_grads(layer):
        grads[layer].rest(
            kept["gate_grad"], kept["up_grad"], kept["down_grad"]
        )

    def projection_grads(layer, attn_gain_grad, mlp_gain_grad):
        grads[layer].projections(
            kept["turned"],
            kept["values"],
            kept["out_grad"],
            attn_gain_grad,
            mlp_gain_grad,
        )

    upper, lower = 0, 1
    come(0, lower, 2)
    come(0, upper)
    come(0, lower)
    come(0, upper)
    come(0, lower)
    come(0, upper)
    come(0, lower)
    come(0, upper)
    come(1, lower)
    come(1, upper)
    come(0, lower)
    come(0, upper)
    come(1, lower)
    come(1, upper)
    come(0, lower, 2)
    come(1, lower)
    come(1, upper)

    x = x_ref[place.section].astype(F32).T
    start_layer(0, x)
    come(1, lower)
    come(1, upper)
    come(0, upper)
    come(1, lower)
    attention_of_layer(0)
    come(0, upper)
    come(1, lower)
    come(1, upper)
    come(0, upper)
    midway, gate, up, result = rest_of_layer(0, x)
    kept["midway"][...] = midway
    kept["gate"][...] = gate
    kept["up"][...] = up
    passed = result.astype(BF16)
    kept["x_2"][...] = passed
    come(1, lower)
    come(1, lower)
    start_layer(1, passed.astype(F32))
    come(1, upper)
    attention_of_layer(1)
    come(1, upper)
    come(1, upper)
    midway, gate, up, result = rest_of_layer(1, kept["x_2"][...].astype(F32))
    finish_edge(1, result.T)

    def nothing():
        pass

    mlp_gain_grad_2 = back_of_layer(
        1, late_ref[place.section].astype(F32).T, midway, gate, up, nothing, [nothing] * 3
    )
    prepare_grads(1)
    sums[1].middle()
    rest_grads(1)
    go(1, upper)
    go(1, upper)
    attn_gain_grad_2, grad_in = end_of_layer(1, kept["x_2"][...].astype(F32))
    projection_grads(1, attn_gain_grad_2, mlp_gain_grad_2)
    go(1, lower)

    def after_feed_forward():
        go(1, lower)
        pl.semaphore_signal(
            credit_sem, inc=1, device_id=place.partner(), device_id_type=MESH
        )
        go(1, upper)
        prepare_grads(0)
        rest_grads(0)
        pl.semaphore_wait(credit_sem, 1)
        go(0, upper)

    mlp_gain_grad_1 = back_of_layer(
        0,
        grad_in.astype(BF16).astype(F32),
        kept["midway"][...],
        kept["gate"][...],
        kept["up"][...],
        after_feed_forward,
        [nothing] * 3,
    )
    go(1, lower)
    sums[0].middle()
    go(0, upper)
    go(1, upper)
    go(1, lower)
    attn_gain_grad_1, grad_in = end_of_layer(0, x_ref[place.section].astype(F32).T)
    projection_grads(0, attn_gain_grad_1, mlp_gain_grad_1)
    go(0, lower)
    go(1, upper)
    go(1, lower)
    go(0, upper)
    finish_edge(0, grad_in.T)
    go(0, lower)
    go(1, upper)
    go(1, lower)
    go(0, lower)
    go(1, upper)
    go(1, lower)
    go(0, upper)
    go(0, lower)
    go(0, upper)
    go(0, lower)
    go(0, upper)
    go(0, lower)
    go(0, upper)
    go(0, lower)
    go(1, upper)
    go(1, lower)
    go(0, upper)
    go(0, lower)
    edge.wait()


def run_layers(x, late, cos, sin, segments, shards):
    edge = jax.ShapeDtypeStruct((D, ROWS), F32)
    summed = jax.ShapeDtypeStruct((PACKED, LANES), F32)
    return pl.pallas_call(
        layers_kernel,
        out_shape=(summed, edge, edge),
        in_specs=[VMEM] * 14,
        out_specs=(VMEM, VMEM, VMEM),
        scratch_shapes=[
            pltpu.SemaphoreType.DMA((4, 8)),
            pltpu.SemaphoreType.DMA((4, 8)),
            pltpu.SemaphoreType.DMA((2, 2, GATHER_SLOTS)),
            pltpu.SemaphoreType.DMA((2, 2, GATHER_SLOTS)),
            pltpu.SemaphoreType.DMA((2, 2, SCATTER_SLOTS)),
            pltpu.SemaphoreType.DMA((2, 2, SCATTER_SLOTS)),
            pltpu.SemaphoreType.DMA((2,)),
            pltpu.SemaphoreType.REGULAR,
            *[pltpu.VMEM(shape, kind) for shape, kind in KEPT.values()],
            *[box for layer in range(2) for part in SCATTER_PARTS for box in scatter_inboxes(part)],
        ],
        compiler_params=params(2),
        name="layers",
    )(x, late, cos, sin, segments, *shards)


def rope_tables(first):
    places = first + jnp.arange(ROWS, dtype=jnp.int32)
    pair_index = jnp.arange(HEAD // 2).astype(F32)
    frequency = rope_base ** (-2.0 * pair_index / HEAD)
    angles = places.astype(F32)[:, None] * frequency[None, :]
    cos, sin = jnp.cos(angles), jnp.sin(angles)
    return jnp.concatenate([cos] * 4, axis=1), jnp.concatenate([-sin, sin] * 2, axis=1)


def local(block_input, cotangent, segment_ids, *shards):
    cos, sin = rope_tables(lax.axis_index("ctx") * ROWS)
    x = block_input[:, 0].transpose(0, 2, 1)
    late = cotangent[:, 0].transpose(0, 2, 1)
    return finish(*run_layers(x, late, cos, sin, segment_ids, shards))


def solution(mesh):
    shard = P("section", ("ctx", "fsdp"))
    matrix = P("section", ("ctx", "fsdp"), None)
    return jax.shard_map(
        local,
        mesh=mesh,
        in_specs=(
            P(None, "fsdp", "ctx", None),
            P(None, "fsdp", "ctx", None),
            P(None, "fsdp", None),
            shard,
            matrix,
            matrix,
            matrix,
            matrix,
            matrix,
            matrix,
            matrix,
            shard,
        ),
        out_specs=(
            P("section", None, "fsdp", "ctx", None),
            shard,
            matrix,
            matrix,
            matrix,
            matrix,
            matrix,
            matrix,
            matrix,
            shard,
        ),
        check_vma=False,
    )
```

time: 210 us -> 160 us (0.76)
  Pallas kernels: 201 us -> 158 us
  local copies, waits for them, and re-layouts: 4.72 us -> 0 us
    pallas_call x5 -> x1, Pallas kernels: 199 us -> 156 us  [run_layers(): pl.pallas_call(layers_kernel, out_shape=(summed, edge, edge), in_specs=[V...]
    dynamic_slice x4 -> x0, local copies, waits for them, and re-layouts: 3.23 us -> none  [the longest x2 1.82 us: local(): late = lax.dynamic_index_in_dim(cotangent[:, 0], section, 0, keepdims=False)]
where the time goes in v3:
time: 160 us
  Pallas kernels  158 us (99%)
    pallas_call x1, Pallas kernels, run_layers(): pl.pallas_call(layers_kernel, out_shape=(summed, edge, edge), in_specs=[V...  156 us

profile of v3, /device:TPU:0, one launch (start us, length us, event | category | flops | bytes accessed | tf_op | source)
XLA Modules:
  0.0 160.2 jit_solution(18152826274300740698)
XLA Ops:
  0.7 0.3 fusion
  1.0 0.8 pad_maximum_fusion
  1.8 156.1 %layers.1 = (f32[448,128]{1,0:T(8,128)}, f32[576,128]{1,0:T(8,128)}, f32[576,128]{1,0:T(8,128)}) custom-call(bf16[2,576,128]{2,1,0:T(8,128)(2,1)} %bitcast.13, bf16[2,576,128]{2,1,0:T(8,128)(2,1)} %bitcast.14, f32[128,128]{1,0:T(8,128)} %get-tuple-element.39.cos_ref, f32[128,128]{1,0:T(8,128)} %get-tuple-element.40.sin_ref, s32[2,1,1024]{2,1,0:T(1,128)} %seg_ref.1, ...), custom_call_target="tpu_custom_call" | custom-call | tf_op jit(solution)/shard_map/layers/pallas_call | solution.py:1313
  157.9 2.1 %finish.1 = (f32[1,2,1,576,128]{4,3,2,1,0:T(8,128)}, f32[1,9]{1,0:T(1,128)}, f32[9,1,576]{2,1,0:T(1,128)}, f32[9,1,192]{2,1,0:T(1,128)}, f32[9,1,192]{2,1,0:T(1,...) custom-call(f32[448,128]{1,0:T(8,128)} %get-tuple-element.23.packed_, ...), custom_call_target="tpu_custom_call" | custom-call | tf_op jit(solution)/shard_map/finish/pallas_call | solution.py:691
  (2 shorter events, 0.0 us)

commit v4 on v3

--- a/solution.py
+++ b/solution.py
@@ -37,25 +37,32 @@
 
 DOWN_ROWS = 24
 TAIL_ROW = 4 * DOWN_ROWS
-UPPER_ROW = TAIL_ROW + DOWN_ROWS // 2
-LOWER_ROW = 336
-GAIN_ROW = LOWER_ROW + 9 * 12
+UPPER_ROW = 112
+LOWER_ROW = 368
 PACKED = 448
+UPPER = tuple(range(6, 34))
+LOWER = tuple(range(6)) + (34, 35)
+GAIN_ROW = LOWER_ROW + 9 * len(LOWER)
 GAIN_TILE = 432
-UPPER_COLUMNS = tuple(range(GATE_AT // LANES, OUT_AT // LANES))
-LOWER_COLUMNS = tuple(range(GATE_AT // LANES)) + tuple(range(OUT_AT // LANES, BLOCKS))
+EARLY = 4 * LANES
 
 
 def packed_row(column):
-    if column in UPPER_COLUMNS:
-        return UPPER_ROW + 9 * UPPER_COLUMNS.index(column)
-    return LOWER_ROW + 9 * LOWER_COLUMNS.index(column)
+    if column in UPPER:
+        return UPPER_ROW + 9 * UPPER.index(column)
+    return LOWER_ROW + 9 * LOWER.index(column)
 
 
 GATHER_PARTS = (
-    ((0, 336), (((0, 176), "xy"), ((176, 160), "yx"))),
-    ((336, 112), (((336, 64), "xy"), ((400, 48), "yx"))),
+    ((0, 368), (((0, 160), "xy"), ((160, 208), "yx"))),
+    ((368, 80), (((368, 48), "xy"), ((416, 32), "yx"))),
 )
+SCATTER_PARTS = (
+    ((0, 112), (((0, 48), "yx"), ((48, 64), "xy"))),
+    ((112, 256), (((112, 112), "yx"), ((224, 144), "xy"))),
+    ((368, 80), (((368, 48), "yx"), ((416, 32), "xy"))),
+)
+SCATTER_DIRECT = (((), (1,), (0, 1)), ((), (), (0, 1)))
 VMEM_BYTES = 63 * 1024 * 1024
 
 
@@ -126,9 +133,10 @@
 
 
 GATHER_SLOTS = 3 + 2 * 2 * 4 + 2 * 4
-
-
-def gather_steps(place, layer, part, held, send_sems, recv_sems):
+WAYS = (1, -1, 2)
+
+
+def gather_steps(place, layer, part, direct, held, send_sems, recv_sems):
     core = place.core
     all_rows, chunks = part
     plane = lax.rem(place.at["z"] + 4 - 2 * layer, 4)
@@ -143,48 +151,34 @@
             device_id_type=MESH,
         )
 
-    def shard(z_lo):
-        return held.at[layer, place.at["y"], core, z_lo, place.at["x"], pl.ds(*all_rows)]
-
-    def up(z_lo, slot):
-        return copy(slot, shard(z_lo), place.neighbour("z", 1))
-
-    def down(z_lo, slot):
-        return copy(slot, shard(z_lo), place.neighbour("z", -1))
+    def across(z_lo, slot):
+        shard = held.at[layer, place.at["y"], core, z_lo, place.at["x"], pl.ds(*all_rows)]
+        return copy(slot, shard, place.neighbour("z", WAYS[slot]))
 
     for source in range(2):
 
         @pl.when(plane == source)
         def _():
-            up(source, 0).start()
-            down(source, 1).start()
+            for slot in range(3):
+                across(source, slot).start()
 
     yield
 
     @pl.when((plane == 1) | (plane == 2))
     def _():
-        up(0, 0).wait_recv()
+        across(0, 0).wait_recv()
 
     @pl.when((plane == 0) | (plane == 3))
     def _():
-        down(0, 1).wait_recv()
-
-    @pl.when(plane == 2)
-    def _():
-        up(1, 2).start()
-
-    @pl.when(plane == 3)
-    def _():
-        down(0, 2).start()
-
-    yield
+        across(0, 1).wait_recv()
 
     @pl.when(plane >= 2)
     def _():
-        up(0, 2).wait_recv()
+        across(0, 2).wait_recv()
 
     counter = [3]
     sent = []
+    to_partner = []
 
     def send(ref, device):
         made = copy(counter[0], ref, device)
@@ -193,13 +187,14 @@
         sent.append(made)
         return made
 
-    to_partner = []
     for phase in range(2):
+        one_step = phase in direct
         first, second = [], []
         for rows, order in chunks:
             axis, whole = order[phase], order[:phase]
             block = layer_region(held, layer, place.at, whole, rows, core)
-            first.append([send(block, place.neighbour(axis, way)) for way in (1, -1)])
+            ways = WAYS if one_step else WAYS[:2]
+            first.append([send(block, place.neighbour(axis, way)) for way in ways])
             if phase == 1:
                 to_partner.append(send(block, place.partner()))
         yield
@@ -209,27 +204,35 @@
                 made.wait_recv()
             left = dict(place.at, **{axis: place.shifted(axis, -1)})
             right = dict(place.at, **{axis: place.shifted(axis, 1)})
-            upper, lower = halves(rows)
-            second += [
-                send(
-                    layer_region(held, layer, left, whole, upper, core), place.neighbour(axis, 1)
-                ),
-                send(
-                    layer_region(held, layer, right, whole, lower, core), place.neighbour(axis, -1)
-                ),
-            ]
+            far = dict(place.at, **{axis: place.shifted(axis, 2)})
+            if not one_step:
+                upper, lower = halves(rows)
+                second += [
+                    send(
+                        layer_region(held, layer, left, whole, upper, core),
+                        place.neighbour(axis, 1),
+                    ),
+                    send(
+                        layer_region(held, layer, right, whole, lower, core),
+                        place.neighbour(axis, -1),
+                    ),
+                ]
             if phase == 1:
-                for coords in (left, right):
+                for coords in (left, right, far) if one_step else (left, right):
                     to_partner.append(
                         send(layer_region(held, layer, coords, whole, rows, core), place.partner())
                     )
-        yield
-        for made in second:
-            made.wait_recv()
-    for rows, order in chunks:
-        axis, whole = order[1], order[:1]
-        far = dict(place.at, **{axis: place.shifted(axis, 2)})
-        to_partner.append(send(layer_region(held, layer, far, whole, rows, core), place.partner()))
+        if not one_step:
+            yield
+            for made in second:
+                made.wait_recv()
+    if 1 not in direct:
+        for rows, order in chunks:
+            axis, whole = order[1], order[:1]
+            far = dict(place.at, **{axis: place.shifted(axis, 2)})
+            to_partner.append(
+                send(layer_region(held, layer, far, whole, rows, core), place.partner())
+            )
     yield
     for made in to_partner:
         made.wait_recv()
@@ -238,21 +241,13 @@
 
     @pl.when(plane <= 1)
     def _():
-        up(0, 0).wait_send()
-        down(0, 1).wait_send()
-
-    @pl.when(plane >= 2)
-    def _():
-        up(0, 2).wait_send()
+        for slot in range(3):
+            across(0, slot).wait_send()
 
     yield
 
 
-SCATTER_PARTS = (
-    ((0, 336), (((0, 176), "yx"), ((176, 160), "xy"))),
-    ((336, 112), (((336, 64), "yx"), ((400, 48), "xy"))),
-)
-SCATTER_SLOTS = 1 + 2 * 2 * 4 + 2
+SCATTER_SLOTS = 1 + 2 * 2 * 4 + 3
 
 
 def scatter_inboxes(part):
@@ -262,11 +257,11 @@
         others = (2, 4) if order == "yx" else (4, 2)
         boxes.append(pltpu.VMEM((3, *others, rows, LANES), BF16))
         boxes.append(pltpu.VMEM((3, 2, rows, LANES), BF16))
-    boxes.append(pltpu.VMEM((2, count, LANES), BF16))
+    boxes.append(pltpu.VMEM((3, count, LANES), BF16))
     return boxes
 
 
-def scatter_steps(place, layer, part, held, boxes, send_sems, recv_sems, out_ref):
+def scatter_steps(place, layer, part, direct, held, boxes, send_sems, recv_sems, out_ref):
     core = place.core
     here_y, here_x = place.at["y"], place.at["x"]
     (first, count), chunks = part
@@ -342,21 +337,31 @@
                 spot = (layer, coords["y"], core, z_lo, coords["x"], here)
                 add(spot, lambda: box[slot, z_lo, in_box(begin)], size)
 
-    flights = [None, None]
+    flights = [[], []]
+
+    def land(flight):
+        for made, phase, axis, lands, spot_rows, box, slot in flight:
+            made.wait_recv()
+            add_block(phase, axis, lands, spot_rows, box, slot)
+
     for phase in range(2):
-        for step in range(2):
+        one_step = phase in direct
+        for step in range(1 if one_step else 2):
             for i, (rows, order) in enumerate(chunks):
                 box = boxes[2 * i + phase]
-                if flights[i] is not None:
-                    for made, before_phase, before_axis, lands, spot_rows, before_box, slot in flights[i]:
-                        made.wait_recv()
-                        add_block(before_phase, before_axis, lands, spot_rows, before_box, slot)
+                land(flights[i])
                 axis, whole = order[phase], order[phase + 1 :]
                 right = dict(place.at, **{axis: place.shifted(axis, 1)})
                 left = dict(place.at, **{axis: place.shifted(axis, -1)})
                 far = dict(place.at, **{axis: place.shifted(axis, 2)})
                 upper, lower = halves(rows)
-                if step == 0:
+                if one_step:
+                    plan = (
+                        (right, rows, 1, place.at, 0),
+                        (left, rows, -1, place.at, 1),
+                        (far, rows, 2, place.at, 2),
+                    )
+                elif step == 0:
                     plan = ((far, upper, 1, right, 0), (far, lower, -1, left, 0))
                 else:
                     plan = ((right, rows, 1, place.at, 1), (left, rows, -1, place.at, 2))
@@ -374,47 +379,38 @@
                     )
             yield
     for flight in flights:
-        for made, phase, axis, lands, spot_rows, box, slot in flight:
-            made.wait_recv()
-            add_block(phase, axis, lands, spot_rows, box, slot)
+        land(flight)
 
     plane = lax.rem(place.at["z"] + 4 - 2 * layer, 4)
-    odd = lax.rem(plane, 2)
-    stays = lax.rem((plane + 1) // 2, 2)
+    stays = lax.rem(plane, 2)
     box = boxes[4]
-
-    def shard(z_lo):
-        return held.at[layer, here_y, core, z_lo, here_x, all_rows]
-
-    def along_z(step):
-        return place.device(z=lax.rem(place.at["z"] + step + 4, 4))
-
-    pair = send(shard(1 - stays), box.at[0], along_z(1 - 2 * odd))
-    last = copy(shard(stays), box.at[1], along_z(2 * odd - 1))
-    yield
-    pair.wait_recv()
-    add((layer, here_y, core, stays, here_x, all_rows), lambda: box[0], count)
-
-    @pl.when(plane >= 2)
-    def _():
-        last.start()
-
+    shards = ((3 - plane) // 3, plane // 2, lax.rem(plane, 2))
+    senders = ((plane == 0) | (plane == 3), (plane == 1) | (plane == 2), plane >= 2)
+    last = [
+        copy(
+            held.at[layer, here_y, core, z_lo, here_x, all_rows],
+            box.at[i],
+            place.neighbour("z", WAYS[i]),
+        )
+        for i, z_lo in enumerate(shards)
+    ]
+    for made, sender in zip(last, senders):
+        pl.when(sender)(made.start)
     yield
 
     @pl.when(plane < 2)
     def _():
-        last.wait_recv()
-        out_ref[all_rows] = held[layer, here_y, core, stays, here_x, all_rows].astype(
-            F32
-        ) + box[1].astype(F32)
+        for made in last:
+            made.wait_recv()
+        total = held[layer, here_y, core, stays, here_x, all_rows].astype(F32)
+        for i in range(3):
+            total += box[i].astype(F32)
+        out_ref[all_rows] = total
 
     for made in sent:
         made.wait_send()
-
-    @pl.when(plane >= 2)
-    def _():
-        last.wait_send()
-
+    for made, sender in zip(last, senders):
+        pl.when(sender)(made.wait_send)
     yield
 
 
@@ -470,15 +466,17 @@
                     (2,) + self.keys_ref.shape[1:], self.keys_ref.dtype
                 )
 
-    def finish(self):
+    def pass_on(self):
         y = self.place.at["y"]
-        for away in range(1, 4):
+        for away in (1, 3, 2):
 
             @pl.when(y - away >= 0)
             def _():
                 self.direct(away).wait_recv()
                 self.passed_on(away).start()
 
+    def finish(self):
+        y = self.place.at["y"]
         self.passed_on(0).wait()
         for away in range(1, 4):
 
@@ -508,7 +506,7 @@
         return self.copy(
             away,
             self.parts_ref.at[self.place.core, y],
-            self.ring_ref.at[away],
+            self.ring_ref.at[away - 1],
             self.along_y(-away),
         )
 
@@ -536,7 +534,7 @@
             @pl.when(y + away < 4)
             def _():
                 self.direct(away).wait_recv()
-                out_ref[...] += self.ring_ref[away].astype(F32)
+                out_ref[...] += self.ring_ref[away - 1].astype(F32)
 
         for away in range(1, 4):
 
@@ -556,13 +554,14 @@
     pieces = [down[:, i * LANES : (i + 1) * LANES] for i in range(4)]
     half = DOWN_ROWS // 2
     pieces.append(jnp.concatenate([down[:half, 4 * LANES :], down[half:, 4 * LANES :]], axis=1))
-    pieces += [joined[:, i * LANES : (i + 1) * LANES] for i in UPPER_COLUMNS]
-    pieces.append(jnp.zeros((12, LANES), F32))
-    pieces += [joined[:, i * LANES : (i + 1) * LANES] for i in LOWER_COLUMNS]
+    pieces.append(jnp.zeros((4, LANES), F32))
+    pieces += [joined[:, i * LANES : (i + 1) * LANES] for i in UPPER]
+    pieces.append(jnp.zeros((4, LANES), F32))
+    pieces += [joined[:, i * LANES : (i + 1) * LANES] for i in LOWER]
     for ref in (attn_ref, mlp_ref):
         gain = ref[...].astype(F32)
         pieces.append(jnp.concatenate([gain, jnp.zeros((1, LANES - 9), F32)], axis=1))
-    pieces.append(jnp.zeros((2, LANES), F32))
+    pieces.append(jnp.zeros((PACKED - GAIN_ROW - 2, LANES), F32))
     return jnp.concatenate(pieces, axis=0).astype(BF16)
 
 
@@ -628,7 +627,8 @@
     for y in range(4):
         rows = held[layer, y, :, :, :, GAIN_TILE:, :].reshape(16 * 16, LANES)
         spread = dot(rows, spread_to)
-        masks = gain_masks(y * 16, 16, 16, (GAIN_ROW - GAIN_TILE, GAIN_ROW - GAIN_TILE + 1))
+        at = GAIN_ROW - GAIN_TILE
+        masks = gain_masks(y * 16, 16, 16, (at, at + 1))
         totals = [
             total + jnp.sum(jnp.where(mask, spread, 0.0), axis=0, keepdims=True)
             for total, mask in zip(totals, masks)
@@ -638,9 +638,7 @@
 
 
 def finish_kernel(
-    packed_ref,
-    kept_ref,
-    came_ref,
+    all_ref,
     edges_ref,
     attn_ref,
     query_ref,
@@ -653,9 +651,9 @@
     mlp_ref,
 ):
     section = lax.axis_index("section")
-    edges_ref[0, section, 0] = kept_ref[...]
-    edges_ref[0, 1 - section, 0] = came_ref[...]
-    packed = packed_ref[...]
+    edges_ref[0, section, 0] = all_ref[PACKED : PACKED + D]
+    edges_ref[0, 1 - section, 0] = all_ref[PACKED + D :]
+    packed = all_ref[:PACKED]
     joined = jnp.concatenate(
         [packed[packed_row(i) : packed_row(i) + 9] for i in range(BLOCKS)], axis=1
     )
@@ -665,17 +663,18 @@
     up_ref[:, 0] = joined[:, UP_AT:OUT_AT]
     w_out_ref[:, 0] = joined[:, OUT_AT:VALUE_AT]
     value_ref[:, 0] = joined[:, VALUE_AT:]
-    tail = packed[TAIL_ROW:UPPER_ROW]
+    tail = packed[TAIL_ROW : TAIL_ROW + DOWN_ROWS // 2]
     down_ref[0] = jnp.concatenate(
         [packed[DOWN_ROWS * i : DOWN_ROWS * (i + 1)] for i in range(4)]
         + [jnp.concatenate([tail[:, :HEAD], tail[:, HEAD:]], axis=0)],
         axis=1,
     )
-    attn_ref[...] = packed[GAIN_ROW : GAIN_ROW + 1, :9]
-    mlp_ref[...] = packed[GAIN_ROW + 1 : GAIN_ROW + 2, :9]
-
-
-def finish(packed, kept, came):
+    at = GAIN_ROW
+    attn_ref[...] = packed[at : at + 1, :9]
+    mlp_ref[...] = packed[at + 1 : at + 2, :9]
+
+
+def finish(rows):
     shapes = (
         (1, 2, 1, D, ROWS),
         (1, 9),
@@ -691,11 +690,11 @@
     edges, attn, *wide, down, mlp = pl.pallas_call(
         finish_kernel,
         out_shape=tuple(jax.ShapeDtypeStruct(shape, F32) for shape in shapes),
-        in_specs=[VMEM] * 3,
+        in_specs=[VMEM],
         out_specs=(VMEM,) * len(shapes),
         compiler_params=params(),
         name="finish",
-    )(packed, kept, came)
+    )(rows)
     wide = [grad.transpose(1, 0, 2) for grad in wide]
     return (edges.transpose(0, 1, 2, 4, 3), attn, *wide, down, mlp)
 
@@ -845,10 +844,9 @@
 
 
 class WeightGrads:
-    def __init__(self, packed, upper, lower, gain_rows, lhs, hidden_lhs):
+    def __init__(self, packed, stages, gain_rows, lhs, hidden_lhs):
         self.packed = packed
-        self.upper = upper
-        self.lower = lower
+        self.first, self.second, self.third = stages
         self.gain_rows = gain_rows
         self.lhs = lhs
         self.hidden_lhs = hidden_lhs
@@ -860,12 +858,6 @@
             for d in range(GRAD_DEVICES):
                 stage[d, at : at + 9] = part[9 * d : 9 * d + 9]
 
-    def prepare(self, normed, normed_two, attended, hidden):
-        self.lhs[0] = transposed(normed)
-        self.lhs[1] = transposed(normed_two)
-        self.lhs[2] = transposed(attended)
-        self.hidden_lhs[...] = transposed(hidden)
-
     def rows(self, step, each):
         return pl.ds(pl.multiple_of(step * each * GRAD_DEVICES, 16), each * GRAD_DEVICES)
 
@@ -875,57 +867,74 @@
             (2, 2, 4) + rounded.shape[1:]
         )
 
-    def rest(self, gate_grad_ref, up_grad_ref, down_grad_ref):
+    def down(self, hidden, down_grad):
         half = DOWN_ROWS // 2
-        self.upper[:, LOWER_ROW - 12 :] = jnp.zeros((GRAD_DEVICES, 12, LANES), F32)
+        self.hidden_lhs[...] = transposed(hidden)
+        self.first[:, TAIL_ROW + half :] = jnp.zeros((GRAD_DEVICES, 4, LANES), F32)
+
+        def body(y, carry):
+            product = dot(self.hidden_lhs[self.rows(y, DOWN_ROWS)], down_grad)
+            for d in range(GRAD_DEVICES):
+                own = product[DOWN_ROWS * d : DOWN_ROWS * (d + 1)]
+                for i in range(4):
+                    self.first[d, DOWN_ROWS * i : DOWN_ROWS * (i + 1)] = own[
+                        :, i * LANES : (i + 1) * LANES
+                    ]
+                self.first[d, TAIL_ROW : TAIL_ROW + half] = jnp.concatenate(
+                    [own[:half, 4 * LANES :], own[half:, 4 * LANES :]], axis=1
+                )
+            self.round(self.first, y, 0)
+            return carry
+
+        lax.fori_loop(0, 64 // GRAD_DEVICES, body, 0)
+
+    def middle(self, normed_two, attended, gate_grad_ref, up_grad_ref, out_grad_ref):
+        self.lhs[1] = transposed(normed_two)
+        self.lhs[2] = transposed(attended)
+        self.second[:, 9 * len(UPPER) :] = jnp.zeros((GRAD_DEVICES, 4, LANES), F32)
 
         def body(y, carry):
             second = self.lhs[1, self.rows(y, 9)]
-            self.place(self.upper, 0, GATE_AT // LANES, dot(second, gate_grad_ref[...]))
-            self.place(self.upper, 0, UP_AT // LANES, dot(second, up_grad_ref[...]))
-            down = dot(self.hidden_lhs[self.rows(y, DOWN_ROWS)], down_grad_ref[...])
-            for d in range(GRAD_DEVICES):
-                own = down[DOWN_ROWS * d : DOWN_ROWS * (d + 1)]
-                for i in range(4):
-                    self.upper[d, DOWN_ROWS * i : DOWN_ROWS * (i + 1)] = own[
-                        :, i * LANES : (i + 1) * LANES
-                    ]
-                self.upper[d, TAIL_ROW:UPPER_ROW] = jnp.concatenate(
-                    [own[:half, 4 * LANES :], own[half:, 4 * LANES :]], axis=1
-                )
-            self.round(self.upper, y, 0)
+            self.place(self.second, UPPER_ROW, GATE_AT // LANES, dot(second, gate_grad_ref[...]))
+            self.place(self.second, UPPER_ROW, UP_AT // LANES, dot(second, up_grad_ref[...]))
+            third = self.lhs[2, self.rows(y, 9)]
+            self.place(
+                self.second, UPPER_ROW, OUT_AT // LANES, dot(third, out_grad_ref[:, :EARLY])
+            )
+            self.round(self.second, y, UPPER_ROW)
             return carry
 
         lax.fori_loop(0, 64 // GRAD_DEVICES, body, 0)
 
-    def projections(
-        self, turned_ref, values_ref, out_grad_ref, attn_gain_grad, mlp_gain_grad
-    ):
+    def late(self, normed, turned_ref, values_ref, out_grad_ref, attn_gain_grad, mlp_gain_grad):
+        self.lhs[0] = transposed(normed)
         spread_to = lane_spread()
         (mask,) = gain_masks(0, 64, 1, (0,))
         for i, gain_grad in enumerate((attn_gain_grad, mlp_gain_grad)):
             chosen = jnp.where(mask, gain_grad, 0.0).astype(BF16)
             self.gain_rows[i] = dot_nt(chosen, spread_to)
-        self.lower[:, GAIN_ROW + 2 - LOWER_ROW :] = jnp.zeros((GRAD_DEVICES, 2, LANES), F32)
+        self.third[:, GAIN_ROW + 2 - LOWER_ROW :] = jnp.zeros(
+            (GRAD_DEVICES, PACKED - GAIN_ROW - 2, LANES), F32
+        )
 
         def body(y, carry):
             first = self.lhs[0, self.rows(y, 9)]
-            self.place(self.lower, LOWER_ROW, 0, dot(first, turned_ref[...]))
+            self.place(self.third, LOWER_ROW, 0, dot(first, turned_ref[...]))
             third = self.lhs[2, self.rows(y, 9)]
             self.place(
-                self.lower,
+                self.third,
                 LOWER_ROW,
-                OUT_AT // LANES,
+                (OUT_AT + EARLY) // LANES,
                 jnp.concatenate(
-                    [dot(third, out_grad_ref[...]), dot(first, values_ref[...])], axis=1
+                    [dot(third, out_grad_ref[:, EARLY:]), dot(first, values_ref[...])], axis=1
                 ),
             )
             for i in range(2):
                 gains = self.gain_rows[i, self.rows(y, 1)]
                 for d in range(GRAD_DEVICES):
                     at = GAIN_ROW + i - LOWER_ROW
-                    self.lower[d, at : at + 1] = gains[d : d + 1]
-            self.round(self.lower, y, LOWER_ROW)
+                    self.third[d, at : at + 1] = gains[d : d + 1]
+            self.round(self.third, y, LOWER_ROW)
             return carry
 
         lax.fori_loop(0, 64 // GRAD_DEVICES, body, 0)
@@ -959,7 +968,7 @@
     "probs": ((2, KV_HEADS, GROUP * ROWS, SEQ), BF16),
     "parts": ((2, 2, 4, 2 * KVD, ROWS), BF16),
     "pair": ((4, 2 * KVD, ROWS), BF16),
-    "ring": ((2, 4, 2 * KVD, ROWS), BF16),
+    "ring": ((2, 3, 2 * KVD, ROWS), BF16),
     "key_grads": ((2 * KVD, ROWS), F32),
     "normed": ((2, *ROW), BF16),
     "query": ((2, *ROW), BF16),
@@ -980,8 +989,9 @@
     "values": ((ROWS, KVD), BF16),
     "lhs": ((3, D, ROWS), BF16),
     "hidden_lhs": ((FF, ROWS), BF16),
-    "upper": ((GRAD_DEVICES, LOWER_ROW, LANES), F32),
-    "lower": ((GRAD_DEVICES, PACKED - LOWER_ROW, LANES), F32),
+    "first": ((GRAD_DEVICES, UPPER_ROW, LANES), F32),
+    "second": ((GRAD_DEVICES, LOWER_ROW - UPPER_ROW, LANES), F32),
+    "third": ((GRAD_DEVICES, PACKED - LOWER_ROW, LANES), F32),
     "gain_rows": ((2, 64, LANES), F32),
     "held": ((2, 4, 2, 2, 4, PACKED, LANES), BF16),
     "wide": ((2, D, WIDE), BF16),
@@ -1000,9 +1010,12 @@
     *rest,
 ):
     shards = rest[:9]
-    summed_ref, stays_ref, came_ref = rest[9:12]
-    send_sems, recv_sems, gather_send, gather_recv, scatter_send, scatter_recv, edge_sems, credit_sem, *scratch = (
-        rest[12:]
+    out_ref = rest[9]
+    summed_ref = out_ref.at[:PACKED]
+    stays_ref = out_ref.at[PACKED : PACKED + D]
+    came_ref = out_ref.at[PACKED + D :]
+    send_sems, recv_sems, gather_send, gather_recv, scatter_send, scatter_recv, edge_sems, credits, *scratch = (
+        rest[10:]
     )
     place = Place()
     kept = dict(zip(KEPT, scratch))
@@ -1016,7 +1029,7 @@
         [place.partner()]
         + [place.neighbour(axis, way) for axis in "xz" for way in (1, -1)]
         + [place.device(y=place.shifted("y", step)) for step in (1, 2, 3)]
-        + [place.device(z=place.shifted("z", 2))]
+        + [place.neighbour(axis, 2) for axis in "xz"]
     )
     leaving = [
         [
@@ -1024,8 +1037,9 @@
                 place,
                 layer,
                 part,
+                SCATTER_DIRECT[layer][i],
                 held,
-                boxes[(2 * layer + i) * 5 : (2 * layer + i) * 5 + 5],
+                boxes[(3 * layer + i) * 5 : (3 * layer + i) * 5 + 5],
                 scatter_send.at[layer, i],
                 scatter_recv.at[layer, i],
                 summed_ref,
@@ -1059,7 +1073,13 @@
     arriving = [
         [
             gather_steps(
-                place, layer, part, held, gather_send.at[layer, i], gather_recv.at[layer, i]
+                place,
+                layer,
+                part,
+                (((), (0, 1)), ((), (1,)))[layer][i],
+                held,
+                gather_send.at[layer, i],
+                gather_recv.at[layer, i],
             )
             for i, part in enumerate(GATHER_PARTS)
         ]
@@ -1089,8 +1109,7 @@
     grads = [
         WeightGrads(
             held.at[i],
-            kept["upper"],
-            kept["lower"],
+            [kept[name] for name in ("first", "second", "third")],
             kept["gain_rows"],
             kept["lhs"],
             kept["hidden_lhs"],
@@ -1100,7 +1119,7 @@
 
     def start_layer(layer, current):
         unpack_gains(held, layer, gains_ref)
-        unpack_wide(held, layer, LOWER_COLUMNS, kept["wide"])
+        unpack_wide(held, layer, LOWER, kept["wide"])
         kept["joined"][layer, mine] = project(
             current,
             gains_ref[layer, 0:1],
@@ -1123,7 +1142,7 @@
         kept["attended"][layer] = attended
 
     def rest_of_layer(layer, current):
-        unpack_wide(held, layer, UPPER_COLUMNS, kept["wide"])
+        unpack_wide(held, layer, UPPER, kept["wide"])
         unpack_down(held, layer, kept["down"])
         attended = kept["attended"][layer]
         midway, scale, normed_two, gate, up, hidden, result = feed_forward(
@@ -1171,21 +1190,21 @@
         kept["values"][...] = values
         return gain_grad, grad_in
 
-    def prepare_grads(layer):
-        grads[layer].prepare(
-            kept["normed"][layer],
+    def down_grads(layer, down_grad):
+        grads[layer].down(kept["hidden"][layer], down_grad.astype(BF16))
+
+    def middle_grads(layer):
+        grads[layer].middle(
             kept["normed_two"][layer],
             kept["attended"][layer],
-            kept["hidden"][layer],
-        )
-
-    def rest_grads(layer):
-        grads[layer].rest(
-            kept["gate_grad"], kept["up_grad"], kept["down_grad"]
-        )
-
-    def projection_grads(layer, attn_gain_grad, mlp_gain_grad):
-        grads[layer].projections(
+            kept["gate_grad"],
+            kept["up_grad"],
+            kept["out_grad"],
+        )
+
+    def late_grads(layer, attn_gain_grad, mlp_gain_grad):
+        grads[layer].late(
+            kept["normed"][layer],
             kept["turned"],
             kept["values"],
             kept["out_grad"],
@@ -1193,34 +1212,39 @@
             mlp_gain_grad,
         )
 
+    def give(part):
+        pl.semaphore_signal(
+            credits.at[part], inc=1, device_id=place.partner(), device_id_type=MESH
+        )
+
+    def begin(part):
+        pl.semaphore_wait(credits.at[part], 1)
+        go(0, part)
+
     upper, lower = 0, 1
-    come(0, lower, 2)
-    come(0, upper)
     come(0, lower)
     come(0, upper)
     come(0, lower)
     come(0, upper)
     come(0, lower)
-    come(0, upper)
     come(1, lower)
     come(1, upper)
+    come(0, upper)
     come(0, lower)
     come(0, upper)
-    come(1, lower)
-    come(1, upper)
-    come(0, lower, 2)
-    come(1, lower)
-    come(1, upper)
+    come(0, lower)
 
     x = x_ref[place.section].astype(F32).T
     start_layer(0, x)
     come(1, lower)
     come(1, upper)
     come(0, upper)
+    gathers[0].pass_on()
     come(1, lower)
+    come(1, upper)
     attention_of_layer(0)
+    come(1, lower)
     come(0, upper)
-    come(1, lower)
     come(1, upper)
     come(0, upper)
     midway, gate, up, result = rest_of_layer(0, x)
@@ -1233,97 +1257,106 @@
     come(1, lower)
     start_layer(1, passed.astype(F32))
     come(1, upper)
+    gathers[1].pass_on()
     attention_of_layer(1)
     come(1, upper)
     come(1, upper)
     midway, gate, up, result = rest_of_layer(1, kept["x_2"][...].astype(F32))
     finish_edge(1, result.T)
 
+    first, second, third = 0, 1, 2
+    incoming = late_ref[place.section].astype(F32).T
+    down_grads(1, incoming)
+    go(1, first)
+
     def nothing():
         pass
 
+    def after_last_feed_forward():
+        go(1, first)
+        give(first)
+        middle_grads(1)
+        go(1, second)
+
     mlp_gain_grad_2 = back_of_layer(
-        1, late_ref[place.section].astype(F32).T, midway, gate, up, nothing, [nothing] * 3
-    )
-    prepare_grads(1)
+        1, incoming, midway, gate, up, after_last_feed_forward, [nothing] * 3
+    )
     sums[1].middle()
-    rest_grads(1)
-    go(1, upper)
-    go(1, upper)
+    go(1, first)
+    go(1, second)
+    give(second)
     attn_gain_grad_2, grad_in = end_of_layer(1, kept["x_2"][...].astype(F32))
-    projection_grads(1, attn_gain_grad_2, mlp_gain_grad_2)
-    go(1, lower)
+    go(1, first)
+    late_grads(1, attn_gain_grad_2, mlp_gain_grad_2)
+    go(1, third)
+    incoming = grad_in.astype(BF16).astype(F32)
+    down_grads(0, incoming)
+    begin(first)
+    go(1, second)
 
     def after_feed_forward():
-        go(1, lower)
-        pl.semaphore_signal(
-            credit_sem, inc=1, device_id=place.partner(), device_id_type=MESH
-        )
-        go(1, upper)
-        prepare_grads(0)
-        rest_grads(0)
-        pl.semaphore_wait(credit_sem, 1)
-        go(0, upper)
+        go(1, third)
+        give(third)
+        go(1, first)
+        go(0, first)
+        middle_grads(0)
+        begin(second)
 
     mlp_gain_grad_1 = back_of_layer(
         0,
-        grad_in.astype(BF16).astype(F32),
+        incoming,
         kept["midway"][...],
         kept["gate"][...],
         kept["up"][...],
         after_feed_forward,
         [nothing] * 3,
     )
-    go(1, lower)
+    go(1, second)
+    go(1, third)
+    go(1, first)
     sums[0].middle()
-    go(0, upper)
-    go(1, upper)
-    go(1, lower)
+    go(0, second)
+    go(0, first)
+    go(1, second)
+    go(1, third)
+    go(0, second)
     attn_gain_grad_1, grad_in = end_of_layer(0, x_ref[place.section].astype(F32).T)
-    projection_grads(0, attn_gain_grad_1, mlp_gain_grad_1)
-    go(0, lower)
-    go(1, upper)
-    go(1, lower)
-    go(0, upper)
+    late_grads(0, attn_gain_grad_1, mlp_gain_grad_1)
+    begin(third)
+    go(1, second)
     finish_edge(0, grad_in.T)
-    go(0, lower)
-    go(1, upper)
-    go(1, lower)
-    go(0, lower)
-    go(1, upper)
-    go(1, lower)
-    go(0, upper)
-    go(0, lower)
-    go(0, upper)
-    go(0, lower)
-    go(0, upper)
-    go(0, lower)
-    go(0, upper)
-    go(0, lower)
-    go(1, upper)
-    go(1, lower)
-    go(0, upper)
-    go(0, lower)
+    go(0, first)
+    go(0, third)
+    go(0, first)
+    go(0, second)
+    go(0, third)
+    go(0, first)
+    go(0, second)
+    go(0, third)
+    go(1, first)
+    go(1, second)
+    go(1, third)
+    go(0, first)
+    go(0, third)
+    go(0, second)
     edge.wait()
 
 
 def run_layers(x, late, cos, sin, segments, shards):
-    edge = jax.ShapeDtypeStruct((D, ROWS), F32)
-    summed = jax.ShapeDtypeStruct((PACKED, LANES), F32)
     return pl.pallas_call(
         layers_kernel,
-        out_shape=(summed, edge, edge),
+        out_shape=jax.ShapeDtypeStruct((PACKED + 2 * D, LANES), F32),
         in_specs=[VMEM] * 14,
-        out_specs=(VMEM, VMEM, VMEM),
+        out_specs=VMEM,
         scratch_shapes=[
             pltpu.SemaphoreType.DMA((4, 8)),
             pltpu.SemaphoreType.DMA((4, 8)),
             pltpu.SemaphoreType.DMA((2, 2, GATHER_SLOTS)),
             pltpu.SemaphoreType.DMA((2, 2, GATHER_SLOTS)),
-            pltpu.SemaphoreType.DMA((2, 2, SCATTER_SLOTS)),
-            pltpu.SemaphoreType.DMA((2, 2, SCATTER_SLOTS)),
+            pltpu.SemaphoreType.DMA((2, 3, SCATTER_SLOTS)),
+            pltpu.SemaphoreType.DMA((2, 3, SCATTER_SLOTS)),
             pltpu.SemaphoreType.DMA((2,)),
-            pltpu.SemaphoreType.REGULAR,
+            pltpu.SemaphoreType.REGULAR((3,)),
             *[pltpu.VMEM(shape, kind) for shape, kind in KEPT.values()],
             *[box for layer in range(2) for part in SCATTER_PARTS for box in scatter_inboxes(part)],
         ],
@@ -1345,7 +1378,7 @@
     cos, sin = rope_tables(lax.axis_index("ctx") * ROWS)
     x = block_input[:, 0].transpose(0, 2, 1)
     late = cotangent[:, 0].transpose(0, 2, 1)
-    return finish(*run_layers(x, late, cos, sin, segment_ids, shards))
+    return finish(run_layers(x, late, cos, sin, segment_ids, shards))
 
 
 def solution(mesh):

time: 160 us -> 153 us (0.956)
  Pallas kernels: 158 us -> 150 us
    pallas_call x1, Pallas kernels: 156 us -> 148 us  [run_layers(): pl.pallas_call(layers_kernel, out_shape=jax.ShapeDtypeStruct((PACKED + 2...]
where the time goes in v4:
time: 153 us; the launch traced here: 152 us
  Pallas kernels  150 us (98%)
    pallas_call x1, Pallas kernels, run_layers(): pl.pallas_call(layers_kernel, out_shape=jax.ShapeDtypeStruct((PACKED + 2...  148 us

profile of v4, /device:TPU:0, one launch (start us, length us, event | category | flops | bytes accessed | tf_op | source)
XLA Modules:
  0.0 151.9 jit_solution(16134804657861429372)
XLA Ops:
  0.7 0.3 fusion
  1.0 0.8 pad_maximum_fusion
  1.8 147.8 %layers.1.all_ref = f32[1600,128]{1,0:T(8,128)} custom-call(bf16[2,576,128]{2,1,0:T(8,128)(2,1)} %bitcast.13, bf16[2,576,128]{2,1,0:T(8,128)(2,1)} %bitcast.14, f32[128,128]{1,0:T(8,128)} %get-tuple-element.33.cos_ref, f32[128,128]{1,0:T(8,128)} %get-tuple-element.34.sin_ref, s32[2,1,1024]{2,1,0:T(1,128)} %seg_ref.1, bf16[1,9]{1,0:T(2,128)(2,1)} %rest_0_.1, ...), custom_call_target="tpu_custom_call" | custom-call | tf_op jit(solution)/shard_map/layers/pallas_call | solution.py:1346
  149.6 2.1 %finish.1 = (f32[1,2,1,576,128]{4,3,2,1,0:T(8,128)}, f32[1,9]{1,0:T(1,128)}, f32[9,1,576]{2,1,0:T(1,128)}, f32[9,1,192]{2,1,0:T(1,128)}, f32[9,1,192]{2,1,0:T(1,...) custom-call(f32[1600,128]{1,0:T(8,128)} %layers.1.all_ref), custom_call_target="tpu_custom_call" | custom-call | tf_op jit(solution)/shard_map/finish/pallas_call | solution.py:690
  (2 shorter events, 0.0 us)

commit v5 on v4

--- a/solution.py
+++ b/solution.py
@@ -62,7 +62,7 @@
     ((112, 256), (((112, 112), "yx"), ((224, 144), "xy"))),
     ((368, 80), (((368, 48), "yx"), ((416, 32), "xy"))),
 )
-SCATTER_DIRECT = (((), (1,), (0, 1)), ((), (), (0, 1)))
+SCATTER_DIRECT = (((1,), (1,), (0, 1)), ((), (), (0, 1)))
 VMEM_BYTES = 63 * 1024 * 1024
 
 
@@ -132,7 +132,14 @@
     return ref.at[layer, y, core, :, x, pl.ds(*rows)]
 
 
-GATHER_SLOTS = 3 + 2 * 2 * 4 + 2 * 4
+GATHER_DIRECT = (((), (0, 1)), ((), (1,)))
+
+
+def gather_slots(direct):
+    phases = sum(3 if phase in direct else 4 for phase in range(2))
+    return 3 + 2 * phases + 2 * (1 if 1 in direct else 4)
+
+
 WAYS = (1, -1, 2)
 
 
@@ -195,7 +202,7 @@
             block = layer_region(held, layer, place.at, whole, rows, core)
             ways = WAYS if one_step else WAYS[:2]
             first.append([send(block, place.neighbour(axis, way)) for way in ways])
-            if phase == 1:
+            if phase == 1 and not one_step:
                 to_partner.append(send(block, place.partner()))
         yield
         for copies, (rows, order) in zip(first, chunks):
@@ -204,7 +211,6 @@
                 made.wait_recv()
             left = dict(place.at, **{axis: place.shifted(axis, -1)})
             right = dict(place.at, **{axis: place.shifted(axis, 1)})
-            far = dict(place.at, **{axis: place.shifted(axis, 2)})
             if not one_step:
                 upper, lower = halves(rows)
                 second += [
@@ -217,8 +223,12 @@
                         place.neighbour(axis, -1),
                     ),
                 ]
-            if phase == 1:
-                for coords in (left, right, far) if one_step else (left, right):
+            if phase == 1 and one_step:
+                to_partner.append(
+                    send(layer_region(held, layer, left, order, rows, core), place.partner())
+                )
+            elif phase == 1:
+                for coords in (left, right):
                     to_partner.append(
                         send(layer_region(held, layer, coords, whole, rows, core), place.partner())
                     )
@@ -247,7 +257,8 @@
     yield
 
 
-SCATTER_SLOTS = 1 + 2 * 2 * 4 + 3
+def scatter_slots(direct):
+    return 1 + 2 * sum(3 if phase in direct else 4 for phase in range(2)) + 3
 
 
 def scatter_inboxes(part):
@@ -997,7 +1008,7 @@
     "wide": ((2, D, WIDE), BF16),
     "down": ((2, FF, D), BF16),
     "gains": ((2, 8, D), F32),
-    "edge": ((D, ROWS), F32),
+    "edge": ((2, D, ROWS), BF16),
 }
 
 
@@ -1014,9 +1025,9 @@
     summed_ref = out_ref.at[:PACKED]
     stays_ref = out_ref.at[PACKED : PACKED + D]
     came_ref = out_ref.at[PACKED + D :]
-    send_sems, recv_sems, gather_send, gather_recv, scatter_send, scatter_recv, edge_sems, credits, *scratch = (
-        rest[10:]
-    )
+    edge_sems, credits, *scratch = rest[10:]
+    key_sems, gather_sems, scatter_sems = scratch[:8], scratch[8:16], scratch[16:28]
+    scratch = scratch[28:]
     place = Place()
     kept = dict(zip(KEPT, scratch))
     boxes = scratch[len(KEPT) :]
@@ -1040,8 +1051,8 @@
                 SCATTER_DIRECT[layer][i],
                 held,
                 boxes[(3 * layer + i) * 5 : (3 * layer + i) * 5 + 5],
-                scatter_send.at[layer, i],
-                scatter_recv.at[layer, i],
+                scatter_sems[3 * layer + i],
+                scatter_sems[6 + 3 * layer + i],
                 summed_ref,
             )
             for i, part in enumerate(SCATTER_PARTS)
@@ -1049,8 +1060,8 @@
         for layer in range(2)
     ]
     edge = pltpu.make_async_remote_copy(
-        src_ref=kept["edge"],
-        dst_ref=came_ref,
+        src_ref=kept["edge"].at[0],
+        dst_ref=kept["edge"].at[1],
         send_sem=edge_sems.at[0],
         recv_sem=edge_sems.at[1],
         device_id=place.device(z=place.shifted("z", 2)),
@@ -1064,7 +1075,7 @@
 
         @pl.when(place.section != section)
         def _():
-            kept["edge"][...] = mine
+            kept["edge"][0] = mine.astype(BF16)
             edge.start()
 
     def go(layer, part):
@@ -1076,10 +1087,10 @@
                 place,
                 layer,
                 part,
-                (((), (0, 1)), ((), (1,)))[layer][i],
+                GATHER_DIRECT[layer][i],
                 held,
-                gather_send.at[layer, i],
-                gather_recv.at[layer, i],
+                gather_sems[2 * layer + i],
+                gather_sems[4 + 2 * layer + i],
             )
             for i, part in enumerate(GATHER_PARTS)
         ]
@@ -1093,7 +1104,7 @@
     cos, sin = cos_ref[...], sin_ref[...]
     mine = lax.axis_index("ctx")
     gathers = [
-        KeyGather(place, kept["joined"].at[i], send_sems.at[i], recv_sems.at[i]) for i in range(2)
+        KeyGather(place, kept["joined"].at[i], key_sems[i], key_sems[4 + i]) for i in range(2)
     ]
     sums = [
         KeyGradSum(
@@ -1101,8 +1112,8 @@
             kept["parts"].at[i],
             kept["pair"],
             kept["ring"].at[i],
-            send_sems.at[2 + i],
-            recv_sems.at[2 + i],
+            key_sems[2 + i],
+            key_sems[6 + i],
         )
         for i in range(2)
     ]
@@ -1243,8 +1254,8 @@
     come(1, lower)
     come(1, upper)
     attention_of_layer(0)
+    come(0, upper)
     come(1, lower)
-    come(0, upper)
     come(1, upper)
     come(0, upper)
     midway, gate, up, result = rest_of_layer(0, x)
@@ -1311,28 +1322,27 @@
         after_feed_forward,
         [nothing] * 3,
     )
+    go(0, second)
+    sums[0].middle()
     go(1, second)
     go(1, third)
     go(1, first)
-    sums[0].middle()
+    go(0, first)
     go(0, second)
-    go(0, first)
     go(1, second)
     go(1, third)
-    go(0, second)
     attn_gain_grad_1, grad_in = end_of_layer(0, x_ref[place.section].astype(F32).T)
     late_grads(0, attn_gain_grad_1, mlp_gain_grad_1)
     begin(third)
-    go(1, second)
     finish_edge(0, grad_in.T)
     go(0, first)
     go(0, third)
+    go(0, second)
     go(0, first)
+    go(0, third)
     go(0, second)
     go(0, third)
-    go(0, first)
-    go(0, second)
-    go(0, third)
+    go(1, second)
     go(1, first)
     go(1, second)
     go(1, third)
@@ -1340,6 +1350,7 @@
     go(0, third)
     go(0, second)
     edge.wait()
+    came_ref[...] = kept["edge"][1].astype(F32)
 
 
 def run_layers(x, late, cos, sin, segments, shards):
@@ -1349,14 +1360,11 @@
         in_specs=[VMEM] * 14,
         out_specs=VMEM,
         scratch_shapes=[
-            pltpu.SemaphoreType.DMA((4, 8)),
-            pltpu.SemaphoreType.DMA((4, 8)),
-            pltpu.SemaphoreType.DMA((2, 2, GATHER_SLOTS)),
-            pltpu.SemaphoreType.DMA((2, 2, GATHER_SLOTS)),
-            pltpu.SemaphoreType.DMA((2, 3, SCATTER_SLOTS)),
-            pltpu.SemaphoreType.DMA((2, 3, SCATTER_SLOTS)),
             pltpu.SemaphoreType.DMA((2,)),
             pltpu.SemaphoreType.REGULAR((3,)),
+            *[pltpu.SemaphoreType.DMA((n,)) for n in (8, 8, 4, 4) * 2],
+            *[pltpu.SemaphoreType.DMA((gather_slots(d),)) for row in GATHER_DIRECT for d in row] * 2,
+            *[pltpu.SemaphoreType.DMA((scatter_slots(d),)) for row in SCATTER_DIRECT for d in row] * 2,
             *[pltpu.VMEM(shape, kind) for shape, kind in KEPT.values()],
             *[box for layer in range(2) for part in SCATTER_PARTS for box in scatter_inboxes(part)],
         ],

time: 153 us -> 152 us (level)
  no operation moved by 1% of the time
where the time goes in v5:
time: 152 us; the launch traced here: 151 us
  Pallas kernels  149 us (98%)
    pallas_call x1, Pallas kernels, run_layers(): pl.pallas_call(layers_kernel, out_shape=jax.ShapeDtypeStruct((PACKED + 2...  147 us

profile of v5, /device:TPU:0, one launch (start us, length us, event | category | flops | bytes accessed | tf_op | source)
XLA Modules:
  0.0 151.3 jit_solution(7576406269242267370)
XLA Ops:
  0.7 0.3 fusion
  1.0 0.8 pad_maximum_fusion
  1.8 147.2 %layers.1.all_ref = f32[1600,128]{1,0:T(8,128)} custom-call(bf16[2,576,128]{2,1,0:T(8,128)(2,1)} %bitcast.13, bf16[2,576,128]{2,1,0:T(8,128)(2,1)} %bitcast.14, f32[128,128]{1,0:T(8,128)} %get-tuple-element.33.cos_ref, f32[128,128]{1,0:T(8,128)} %get-tuple-element.34.sin_ref, s32[2,1,1024]{2,1,0:T(1,128)} %seg_ref.1, bf16[1,9]{1,0:T(2,128)(2,1)} %rest_0_.1, ...), custom_call_target="tpu_custom_call" | custom-call | tf_op jit(solution)/shard_map/layers/pallas_call | solution.py:1357
  149.1 2.1 %finish.1 = (f32[1,2,1,576,128]{4,3,2,1,0:T(8,128)}, f32[1,9]{1,0:T(1,128)}, f32[9,1,576]{2,1,0:T(1,128)}, f32[9,1,192]{2,1,0:T(1,128)}, f32[9,1,192]{2,1,0:T(1,...) custom-call(f32[1600,128]{1,0:T(8,128)} %layers.1.all_ref), custom_call_target="tpu_custom_call" | custom-call | tf_op jit(solution)/shard_map/finish/pallas_call | solution.py:701
  (2 shorter events, 0.0 us)
